TPU v7x, 32 devices: a whole 2x2x4 slice. The times are simulated.
32 devices in a mesh: groups: 2 (over x), patch: 16 (over z, y, core).
Axes of the slice: x: 2, y: 2, z: 4, core: 2. Of those that a mesh axis runs over, the one named last changes fastest.
Arguments:
- nodes: bfloat16 [8192, 512], P(('groups', 'patch')), parts along dimension 0, may hold values from -6 to 6
- edges: bfloat16 [65536, 512], P(('groups', 'patch')), parts along dimension 0, may hold values from -6 to 6
- cot_nodes: bfloat16 [8192, 512], P(('groups', 'patch')), parts along dimension 0, may hold values from -6 to 6
- w_edge_in: bfloat16 [1536, 512], replicated, may hold values from -0.15625 to 0.15625
- w_edge_out: bfloat16 [512, 512], replicated, may hold values from -0.25 to 0.25
- w_node_in: bfloat16 [1024, 512], replicated, may hold values from -0.1875 to 0.1875
- w_node_out: bfloat16 [512, 512], replicated, may hold values from -0.25 to 0.25
- send_rows: int32 [32, 16, 4], P(('groups', 'patch')), parts along dimension 0, may hold values from 0 to 255
- edge_sender: int32 [65536], P(('groups', 'patch')), parts along dimension 0, may hold values from 0 to 319
- edge_receiver: int32 [65536], P(('groups', 'patch')), parts along dimension 0, may hold values from -1 to 255, as said below
Outputs:
- grad_nodes: bfloat16 [8192, 512], P(('groups', 'patch')), parts along dimension 0
- grad_edges: bfloat16 [65536, 512], P(('groups', 'patch')), parts along dimension 0
- grad_edge_in: float32 [3072, 512], P(('groups', 'patch')), parts along dimension 0
- grad_edge_out: float32 [1024, 512], P(('groups', 'patch')), parts along dimension 0
- grad_node_in: float32 [2048, 512], P(('groups', 'patch')), parts along dimension 0
- grad_node_out: float32 [1024, 512], P(('groups', 'patch')), parts along dimension 0
There are 2 independent parts, one for each index of `groups`. A program takes and returns all parts, laid end to end along the dimension named above; an argument that names none is the same for every part. Nothing has to cross between parts.
Inputs may be any that keep to these rules, and one draw needn't show every extreme that they name: `edge_receiver`: on each device the empty slots (-1) come last and are at most half of its 2048 slots; some device has none and some device has exactly half empty.
All inputs are finite; a program needn't handle non-finite values.
Results may differ from a plain program's by a relative error of at most 0.013.
Values may be sent and summed in bfloat16 or wider, within the bound.
No kernel may reach another device: no remote copies, remote signals or barrier semaphores. Data moves between devices by JAX's collectives and lax.ppermute only.
A program may use at most 128 MiB of HBM per device.

v0:
```python
import jax
import jax.numpy as jnp
from jax import lax
from jax.sharding import PartitionSpec as P


def normalize(values):
    center = values - jnp.mean(values, axis=-1, keepdims=True)
    inv_std = lax.rsqrt(jnp.mean(center * center, axis=-1, keepdims=True) + 1e-05)
    return (center * inv_std, inv_std)


def norm_back(upstream, normed, inv_std):
    return inv_std * (
        upstream
        - jnp.mean(upstream, axis=-1, keepdims=True)
        - normed * jnp.mean(upstream * normed, axis=-1, keepdims=True)
    )


def silu_slope(values):
    sigma = jax.nn.sigmoid(values)
    return sigma * (1.0 + values * (1.0 - sigma))


def exact_dot(left, right):
    return jnp.dot(left, right, precision=lax.Precision.HIGHEST, preferred_element_type=jnp.float32)


def inner_rows(left, right):
    return lax.dot_general(
        left, right, (((0,), (0,)), ((), ())), preferred_element_type=jnp.float32
    )


def column_term(left, right):
    return inner_rows(left, right)


def trade(rows):
    return lax.all_to_all(rows, "patch", split_axis=0, concat_axis=0, tiled=True)


def give_back(rows):
    return lax.all_to_all(
        rows.astype(jnp.bfloat16), "patch", split_axis=0, concat_axis=0, tiled=True
    ).astype(rows.dtype)


def edge_out_sum(zeta, edge_dy):
    return lax.psum_scatter(column_term(zeta, edge_dy), "patch", scatter_dimension=0, tiled=True)


def node_in_sum(node_inputs, node_db):
    return lax.psum_scatter(
        column_term(node_inputs, node_db), "patch", scatter_dimension=0, tiled=True
    )


def node_out_sum(node_zeta, node_dy):
    return lax.psum_scatter(
        column_term(node_zeta, node_dy), "patch", scatter_dimension=0, tiled=True
    )


def edge_in_sum(stacked):
    return lax.psum_scatter(stacked, "patch", scatter_dimension=0, tiled=True)


def body(
    nodes,
    edges,
    cot_nodes,
    w_edge_in,
    w_edge_out,
    w_node_in,
    w_node_out,
    send_rows,
    edge_sender,
    edge_receiver,
):
    width = nodes.shape[1]
    owned = nodes.shape[0]
    w_self = w_edge_in[:width]
    w_send = w_edge_in[width : 2 * width]
    w_recv = w_edge_in[2 * width :]
    w_host = w_node_in[:width]
    w_inbox = w_node_in[width:]
    chosen = send_rows[0]
    proj_own = jnp.dot(nodes, w_send, preferred_element_type=jnp.float32).astype(jnp.bfloat16)
    arrived = trade(proj_own[chosen])
    proj_all = jnp.concatenate([proj_own, arrived.reshape(-1, width)], axis=0)
    proj_recv = jnp.dot(nodes, w_recv, preferred_element_type=jnp.float32).astype(jnp.bfloat16)
    safe_recv = jnp.maximum(edge_receiver, 0)
    pre_act = (
        jnp.dot(edges, w_self, preferred_element_type=jnp.float32)
        + proj_all[edge_sender].astype(jnp.float32)
        + proj_recv[safe_recv].astype(jnp.float32)
    )
    zeta = jax.nn.silu(pre_act).astype(jnp.bfloat16)
    edge_normed, edge_inv = normalize(jnp.dot(zeta, w_edge_out, preferred_element_type=jnp.float32))
    message = edge_normed.astype(jnp.bfloat16)
    recv_table = (edge_receiver[None, :] == jnp.arange(owned, dtype=jnp.int32)[:, None]).astype(
        jnp.bfloat16
    )
    inbox = jnp.dot(recv_table, message, preferred_element_type=jnp.float32).astype(jnp.bfloat16)
    node_pre = jnp.dot(nodes, w_host, preferred_element_type=jnp.float32) + jnp.dot(
        inbox, w_inbox, preferred_element_type=jnp.float32
    )
    node_zeta = jax.nn.silu(node_pre).astype(jnp.bfloat16)
    node_normed, node_inv = normalize(
        jnp.dot(node_zeta, w_node_out, preferred_element_type=jnp.float32)
    )
    upstream = cot_nodes.astype(jnp.float32)
    node_dy = norm_back(upstream, node_normed, node_inv).astype(jnp.bfloat16)
    node_db = (
        jnp.dot(node_dy, w_node_out.T, preferred_element_type=jnp.float32) * silu_slope(node_pre)
    ).astype(jnp.bfloat16)
    node_inputs = jnp.concatenate([nodes, inbox], axis=1)
    inbox_grad = jnp.dot(node_db, w_inbox.T, preferred_element_type=jnp.float32).astype(
        jnp.bfloat16
    )
    node_grad = upstream + jnp.dot(node_db, w_host.T, preferred_element_type=jnp.float32)
    message_grad = inner_rows(recv_table, inbox_grad)
    edge_dy = norm_back(message_grad, edge_normed, edge_inv).astype(jnp.bfloat16)
    edge_da = (
        jnp.dot(edge_dy, w_edge_out.T, preferred_element_type=jnp.float32) * silu_slope(pre_act)
    ).astype(jnp.bfloat16)
    edge_grad = jnp.dot(edge_da, w_self.T, preferred_element_type=jnp.float32).astype(jnp.bfloat16)
    self_grad = inner_rows(edges, edge_da)
    send_table = (
        edge_sender[None, :] == jnp.arange(owned + chosen.size, dtype=jnp.int32)[:, None]
    ).astype(jnp.bfloat16)
    send_sums = jnp.dot(send_table, edge_da, preferred_element_type=jnp.float32)
    recv_sums = jnp.dot(recv_table, edge_da, preferred_element_type=jnp.float32)
    own_sums = send_sums[:owned]
    halo_sums = send_sums[owned:]
    send_float = w_send.astype(jnp.float32)
    recv_float = w_recv.astype(jnp.float32)
    nodes_float = nodes.astype(jnp.float32)
    flat_rows = chosen.reshape(-1)
    returned = give_back(halo_sums.reshape(chosen.shape + (width,)))
    own_sums = own_sums + jnp.zeros((owned, width), jnp.float32).at[flat_rows].add(
        returned.reshape(-1, width)
    )
    node_grad = node_grad + exact_dot(own_sums, send_float.T)
    send_wgrad = exact_dot(nodes_float.T, own_sums)
    node_grad = node_grad + exact_dot(recv_sums, recv_float.T)
    recv_wgrad = exact_dot(nodes_float.T, recv_sums)
    edge_in_local = jnp.concatenate([self_grad, send_wgrad, recv_wgrad], axis=0)
    node_out_grad = node_out_sum(node_zeta, node_dy)
    node_in_grad = node_in_sum(node_inputs, node_db)
    edge_out_grad = edge_out_sum(zeta, edge_dy)
    edge_in_grad = edge_in_sum(edge_in_local)
    return (
        node_grad.astype(jnp.bfloat16),
        edge_grad,
        edge_in_grad,
        edge_out_grad,
        node_in_grad,
        node_out_grad,
    )


def solution(mesh):
    return jax.shard_map(
        body,
        mesh=mesh,
        in_specs=(
            P(("groups", "patch"), None),
            P(("groups", "patch"), None),
            P(("groups", "patch"), None),
            P(),
            P(),
            P(),
            P(),
            P(("groups", "patch"), None, None),
            P(("groups", "patch")),
            P(("groups", "patch")),
        ),
        out_specs=(
            P(("groups", "patch"), None),
            P(("groups", "patch"), None),
            P(("groups", "patch"), None),
            P(("groups", "patch"), None),
            P(("groups", "patch"), None),
            P(("groups", "patch"), None),
        ),
        check_vma=False,
    )
```

profile of v0, /device:TPU:0, one launch (start us, length us, event | category | flops | bytes accessed | tf_op | source)
XLA Modules:
  0.0 319.0 jit_solution(1737759118961021243)
XLA Ops:
  7.2 0.8 compare_select_fusion.1
  8.1 0.1 copy.18
  8.1 0.1 reshape.128
  8.2 1.4 convolution_convert_fusion.3
  9.7 0.7 gather_fusion
  10.4 0.7 reshape.127
  11.0 7.4 %all-to-all-start = ((bf16[16,4,512]{2,1,0:T(4,128)(2,1)}), bf16[16,4,512]{2,1,0:T(4,128)(2,1)S(1)}, u32[]{:S(2)}, u32[]{:S(2)}) async-start(bf16[16,4,512]{2,1,0:T(4,128)(2,1)} %reshape.127), calls=%async_computation | async-start | bytes 131072 | tf_op jit(solution)/shard_map/all_to_all | solution.py:41
  18.4 0.0 reduce-scatter.11.cloned.1.call-start
  18.5 1.4 convolution_convert_fusion.2
  19.9 2.2 fusion.35
  22.1 9.2 %gather_fusion.2 = bf16[2048,512]{1,0:T(8,128)(2,1)} fusion(bf16[256,512]{1,0:T(8,128)(2,1)S(1)} %convolution_convert_fusion.2, s32[2048]{0:T(1024)S(1)} %maximum_clamp_fusion), kind=kCustom, calls=%fused_computation.2 | custom fusion | bytes 4202496 | tf_op jit(solution)/shard_map/gather | solution.py:98
  31.4 9.2 %gather_fusion.1 = bf16[2048,512]{1,0:T(8,128)(2,1)} fusion(bf16[320,512]{1,0:T(8,128)(2,1)S(1)} %pad_maximum_fusion.1, s32[2048]{0:T(1024)S(1)} %fusion.37), kind=kCustom, calls=%fused_computation.1 | custom fusion | bytes 4202496 | tf_op jit(solution)/shard_map/gather | solution.py:97
  40.6 6.4 %multiply_convert_fusion.2 = (bf16[2048,512]{1,0:T(8,128)(2,1)S(1)}, f32[2048,512]{1,0:T(8,128)}) fusion(bf16[2048,512]{1,0:T(8,128)(2,1)} %gather_fusion.2, bf16[2048,512]{1,0:T(8,128)(2,1)} %gather_fusion.1, bf16[2048,512]{1,0:T(8,128)(2,1)S(1)} %copy-done, bf16[1536,512]{1,0:T(8,128)(2,1)} %param.13), kind=kOutput, calls=%fused_computation.8 | convolution fusion | flops 1083179008 | bytes 13107200 | tf_op jit(solution)/shard_map/dot_general | solution.py:96
  47.0 1.3 fusion.45
  48.4 0.5 multiply_reduce_fusion.1
  48.9 1.4 copy-done.1
  50.4 0.8 fusion.11
  51.2 0.4 copy-done.6
  51.6 0.1 copy-done.11
  51.7 0.3 convolution_add_fusion.3
  52.0 0.4 fusion.46
  52.5 0.2 multiply_reduce_fusion.2
  52.7 0.5 copy-done.13
  53.2 0.2 convert_reduce_fusion
  53.5 1.5 fusion.40
  55.0 2.6 fusion.9
  57.6 0.0 reduce-scatter.11.cloned.1.call-update
  57.6 0.2 reduce-scatter.7.cloned.1.call-start
  57.9 5.6 %fusion.44 = (f32[2048]{0:T(1024)S(1)}, f32[2048]{0:T(1024)S(1)}, f32[2048,512]{0,1:T(8,128)}) fusion(f32[2048]{0:T(1024)S(1)} %add_rsqrt_fusion, f32[2048,512]{0,1:T(8,128)} %copy-done.1, f32[2048]{0:T(1024)S(1)} %broadcast_multiply_fusion.2, bf16[256,512]{1,0:T(8,128)(2,1)} %fusion.9, bf16[1024,512]{1,0:T(8,128)(2,1)S(1)} %copy-done.6, ...), kind=kOutput, calls=%fused_computation.86 | convolution fusion | flops 676982784 | bytes 9216000 | tf_op jit(solution)/shard_map/dot_general | solution.py:31
  63.5 4.8 %multiply_convert_fusion.1 = bf16[2048,512]{0,1:T(8,128)(2,1)S(1)} fusion(f32[2048,512]{0,1:T(8,128)} %get-tuple-element.16, f32[2048,512]{0,1:T(8,128)} %copy-done.1, f32[2048]{0:T(1024)S(1)} %broadcast_multiply_fusion, f32[2048]{0:T(1024)S(1)} %broadcast_multiply_fusion.1, f32[2048]{0:T(1024)S(1)} %add_rsqrt_fusion, f32[2048]{0:T(1024)S(1)} %broadcast_multiply_fusion.2), kind=kLoop, calls=%fused_computation.5 | loop fusion | flops 7340032 | bytes 10518528 | tf_op jit(solution)/shard_map/convert_element_type | solution.py:125
  68.3 1.3 copy-done.8
  69.6 2.4 fusion.49
  72.0 0.0 reduce-scatter.7.cloned.1.call-update
  72.0 0.0 reduce-scatter.9.cloned.1.call-start
  72.1 1.8 fusion.21
  73.9 0.0 reduce-scatter.9.cloned.1.call-update
  73.9 0.1 copy.19
  74.0 0.1 reshape_squeeze.3
  74.1 5.5 %multiply_convert_fusion = bf16[2048,512]{1,0:T(8,128)(2,1)S(1)} fusion(f32[2048,512]{1,0:T(8,128)} %get-tuple-element.11, bf16[2048,512]{0,1:T(8,128)(2,1)} %copy-done.8, bf16[512,512]{1,0:T(8,128)(2,1)} %param.14), kind=kOutput, calls=%fused_computation.4 | convolution fusion | flops 1083179008 | bytes 8912896 | tf_op jit(solution)/shard_map/dot_general | solution.py:127
  79.6 0.8 fusion.1
  80.5 0.5 copy-done.26
  80.9 0.8 copy-done.18
  81.8 0.7 convert_element_type.72
  82.5 6.0 %all-to-all-start.1 = ((bf16[16,4,512]{2,1,0:T(4,128)(2,1)}), bf16[16,4,512]{2,1,0:T(4,128)(2,1)S(1)}, u32[]{:S(2)}, u32[]{:S(2)}) async-start(bf16[16,4,512]{2,1,0:T(4,128)(2,1)} %convert_element_type.72), calls=%async_computation.1 | async-start | bytes 131072 | tf_op jit(solution)/shard_map/all_to_all | solution.py:45
  88.5 0.0 reduce-scatter.5.cloned.1.call-start
  88.5 2.4 fusion.6
  91.0 2.3 convolution_bitcast_fusion.2
  93.3 1.6 convolution_bitcast_fusion
  95.0 1.3 all-to-all-done.1
  96.3 1.4 scatter_fusion
  97.7 0.7 convolution_bitcast_fusion.1
  98.4 0.5 copy-done.5
  98.9 3.2 pad_maximum_fusion
  102.1 0.0 reduce-scatter.5.cloned.1.call-update
  102.1 0.9 copy-done.14
  103.0 1.4 convolution_add_fusion.2
  104.4 4.4 %convolution_convert_fusion = bf16[2048,512]{1,0:T(8,128)(2,1)} fusion(bf16[2048,512]{1,0:T(8,128)(2,1)} %copy-done.26, bf16[1536,512]{1,0:T(8,128)(2,1)} %param.13), kind=kOutput, calls=%fused_computation.14 | convolution fusion | flops 1074790400 | bytes 4718592 | tf_op jit(solution)/shard_map/dot_general | solution.py:129
  108.8 0.6 convolution_add_fusion.1
  109.5 0.4 copy-done.10
  109.9 1.3 fusion.10
  111.2 5.4 %reduce-scatter.11.cloned.1.call-done = f32[32,512]{1,0:T(8,128)} async-done(((f32[512,512]{1,0:T(8,128)}), f32[32,512]{1,0:T(8,128)}) %reduce-scatter.11.cloned.1.call-update) | async-done | bytes 65552 | tf_op jit(solution)/shard_map/reduce_scatter | solution.py:61
  116.6 61.0 %reduce-scatter.7.cloned.1.call-done = f32[32,512]{1,0:T(8,128)} async-done(((f32[512,512]{1,0:T(8,128)}), f32[32,512]{1,0:T(8,128)}) %reduce-scatter.7.cloned.1.call-update) | async-done | bytes 65552 | tf_op jit(solution)/shard_map/reduce_scatter | solution.py:51
  177.5 65.0 %reduce-scatter.9.cloned.1.call-done = f32[64,512]{1,0:T(8,128)} async-done(((f32[1024,512]{1,0:T(8,128)}), f32[64,512]{1,0:T(8,128)}) %reduce-scatter.9.cloned.1.call-update) | async-done | bytes 131088 | tf_op jit(solution)/shard_map/reduce_scatter | solution.py:55
  242.5 69.9 %reduce-scatter.5.cloned.1.call-done = f32[96,512]{1,0:T(8,128)} async-done(((f32[1536,512]{1,0:T(8,128)}), f32[96,512]{1,0:T(8,128)}) %reduce-scatter.5.cloned.1.call-update) | async-done | bytes 196624 | tf_op jit(solution)/shard_map/reduce_scatter | solution.py:67
  (63 shorter events, 0.3 us)
Async XLA Ops:
  7.2 33.4 %copy-start = (bf16[2048,512]{1,0:T(8,128)(2,1)S(1)}, bf16[2048,512]{1,0:T(8,128)(2,1)}, u32[]{:S(2)}) copy-start(bf16[2048,512]{1,0:T(8,128)(2,1)} %param.11) | copy-start | bytes 6291460
  7.2 12.7 %copy-start.4 = (bf16[256,512]{1,0:T(8,128)(2,1)S(1)}, bf16[256,512]{1,0:T(8,128)(2,1)}, u32[]{:S(2)}) copy-start(bf16[256,512]{1,0:T(8,128)(2,1)} %param.10) | copy-start | bytes 786436
  7.2 12.7 %copy-start.22 = (s32[2048]{0:T(1024)S(1)}, s32[2048]{0:T(1024)}, u32[]{:S(2)}) copy-start(s32[2048]{0:T(1024)} %param.19) | copy-start | bytes 24580
  11.0 20.3 %all-to-all-start = ((bf16[16,4,512]{2,1,0:T(4,128)(2,1)}), bf16[16,4,512]{2,1,0:T(4,128)(2,1)S(1)}, u32[]{:S(2)}, u32[]{:S(2)}) async-start(bf16[16,4,512]{2,1,0:T(4,128)(2,1)} %reshape.127), calls=%async_computation | async-start | bytes 131072 | tf_op jit(solution)/shard_map/all_to_all | solution.py:41
  18.4 98.1 %reduce-scatter.11.cloned.1.call-start = ((), (), s32[]{:S(2)}) async-start(), calls=%async_computation.9 | async-start | bytes 1114112 | tf_op jit(solution)/shard_map/reduce_scatter | solution.py:61
  22.1 9.2 %copy-start.24 = (s32[2048]{0:T(1024)S(1)}, s32[2048]{0:T(1024)}, u32[]{:S(2)}) copy-start(s32[2048]{0:T(1024)} %param.18) | copy-start | bytes 24580
  40.6 6.5 %copy-start.20 = (bf16[512,512]{1,0:T(8,128)(2,1)S(1)}, bf16[512,512]{1,0:T(8,128)(2,1)}, u32[]{:S(2)}) copy-start(bf16[512,512]{1,0:T(8,128)(2,1)} %param.14) | copy-start | bytes 1572868
  47.0 1.4 copy-start.2
  48.4 2.0 copy-start.1
  50.4 1.2 copy-start.6
  50.4 1.4 copy-start.11
  50.4 1.7 copy-start.25
  51.7 0.8 copy-start.15
  52.0 1.4 copy-start.21
  52.0 1.1 copy-start.13
  52.5 1.0 copy-start.12
  57.6 119.9 %reduce-scatter.7.cloned.1.call-start = ((), (), s32[]{:S(2)}) async-start(), calls=%async_computation.7 | async-start | bytes 1114112 | tf_op jit(solution)/shard_map/reduce_scatter | solution.py:51
  63.5 6.1 %copy-start.3 = (bf16[2048,512]{1,0:T(8,128)(2,1)S(1)}, bf16[2048,512]{1,0:T(8,128)(2,1)}, u32[]{:S(2)}) copy-start(bf16[2048,512]{1,0:T(8,128)(2,1)} %copy-done.2) | copy-start | bytes 6291460
  68.3 1.3 copy-start.8
  69.6 2.4 copy-start.7
  69.6 2.5 copy-start.16
  72.0 1.9 copy-start.23
  72.0 170.5 %reduce-scatter.9.cloned.1.call-start = ((), (), s32[]{:S(2)}) async-start(), calls=%async_computation.8 | async-start | bytes 2228224 | tf_op jit(solution)/shard_map/reduce_scatter | solution.py:55
  79.6 1.3 copy-start.26
  80.9 0.8 copy-start.18
  82.5 13.8 %all-to-all-start.1 = ((bf16[16,4,512]{2,1,0:T(4,128)(2,1)}), bf16[16,4,512]{2,1,0:T(4,128)(2,1)S(1)}, u32[]{:S(2)}, u32[]{:S(2)}) async-start(bf16[16,4,512]{2,1,0:T(4,128)(2,1)} %convert_element_type.72), calls=%async_computation.1 | async-start | bytes 131072 | tf_op jit(solution)/shard_map/all_to_all | solution.py:45
  88.5 223.9 %reduce-scatter.5.cloned.1.call-start = ((), (), s32[]{:S(2)}) async-start(), calls=%async_computation.6 | async-start | bytes 3342336 | tf_op jit(solution)/shard_map/reduce_scatter | solution.py:67
  88.5 2.5 copy-start.27
  91.0 2.3 copy-start.9
  93.3 1.6 copy-start.19
  97.7 1.2 copy-start.5
  102.1 0.9 copy-start.14
  104.4 4.4 %copy-start.17 = (bf16[1536,512]{1,0:T(8,128)(2,1)S(1)}, bf16[1536,512]{1,0:T(8,128)(2,1)}, u32[]{:S(2)}) copy-start(bf16[1536,512]{1,0:T(8,128)(2,1)} %param.13) | copy-start | bytes 4718596
  108.8 1.0 copy-start.10
Sparse Core Ops, SparseCore 0:
  57.7 58.7 reduce-scatter.10
  121.2 56.3 reduce-scatter.6
  181.9 60.5 reduce-scatter.8
  247.2 65.1 reduce-scatter.4
where the time goes:
time: 320 us; the launch traced here: 319 us
  waiting for transfers between devices  203 us (63%)
  matrix products  49.4 us (15%)
  local copies, waits for them, and re-layouts  27.8 us (9%)
  between operations  14.2 us (4%)
  starting transfers between devices  13.8 us (4%)
  other arithmetic  11.3 us (4%)
    reduce_scatter x1, waiting for transfers between devices, edge_in_sum(): return lax.psum_scatter(stacked, 'patch', scatter_dimension=0, tiled=True)  69.9 us
    reduce_scatter x1, waiting for transfers between devices, node_in_sum(): lax.psum_scatter(column_term(node_inputs, node_db), 'patch', scatter_dime...  65 us
    reduce_scatter x1, waiting for transfers between devices, edge_out_sum(): lax.psum_scatter(column_term(zeta, edge_dy), 'patch', scatter_dimension=0...  61 us
    dot_general x5, matrix products, inner_rows(): lax.dot_general(left, right, (((0,), (0,)), ((), ())), preferred_element_...  13.6 us
    gather x1, local copies, waits for them, and re-layouts, body(): proj_recv[safe_recv].astype(jnp.float32)  9.2 us
    gather x1, local copies, waits for them, and re-layouts, body(): proj_all[edge_sender].astype(jnp.float32)  9.19 us
    all_to_all x1, starting transfers between devices, trade(): lax.all_to_all(rows, 'patch', split_axis=0, concat_axis=0, tiled=True)  7.39 us
    unnamed x57, local copies, waits for them, and re-layouts  7.08 us
  transfers between devices with their start and end apart: 6, of which 5 were waited for; matrix products, arithmetic and copies ran while one was open for 17% of the time, Pallas kernels for 0%

commit v1 on v0

v1 whole, which is shorter than its diff:
```python
import functools

import jax
import jax.numpy as jnp
from jax import lax
from jax.experimental import pallas as pl
from jax.experimental.pallas import tpu as pltpu
from jax.sharding import PartitionSpec as P

BF16 = jnp.bfloat16
F32 = jnp.float32
EPS = 1e-05
LANES = 128
BLOCK = 256


def mm(left, right):
    return jnp.dot(left, right, preferred_element_type=F32)


def mm_rows(left, right):
    return lax.dot_general(left, right, (((0,), (0,)), ((), ())), preferred_element_type=F32)


def mm_cols(left, right):
    return lax.dot_general(left, right, (((1,), (1,)), ((), ())), preferred_element_type=F32)


def sigmoid(values):
    return 0.5 * jnp.tanh(0.5 * values) + 0.5


def normalize(values):
    center = values - jnp.mean(values, axis=-1, keepdims=True)
    inv_std = lax.rsqrt(jnp.mean(center * center, axis=-1, keepdims=True) + EPS)
    return center * inv_std, inv_std


def norm_back(upstream, normed, inv_std):
    return inv_std * (
        upstream
        - jnp.mean(upstream, axis=-1, keepdims=True)
        - normed * jnp.mean(upstream * normed, axis=-1, keepdims=True)
    )


def cube_masks(count):
    bits = count.bit_length() - 1
    masks = [1 << i for i in range(bits)]
    if bits >= 3:
        masks[-1] |= masks[-2]
    return masks


def cube_orders(count):
    rest = list(range(1, count.bit_length() - 1))
    return [0] + rest, [0] + rest[1:] + rest[:1]


def cube_position(target, me, count):
    bits = count.bit_length() - 1
    apart = target ^ me
    coords = [(apart >> i) & 1 for i in range(bits)]
    if bits >= 3:
        coords[-2] = coords[-2] ^ coords[-1]
    even, odd = [sum(coords[dim] << (bits - 1 - j) for j, dim in enumerate(order)) for order in cube_orders(count)]
    return jnp.where((target & 1) == 0, even, odd)


def cube_reduce(blocks, count):
    masks, orders = cube_masks(count), cube_orders(count)
    for step in range(count.bit_length() - 1):
        half = blocks.shape[0] // 2
        pairs = [(i, i ^ masks[orders[i & 1][step]]) for i in range(count)]
        arrived = lax.ppermute(blocks[half:], "patch", pairs)
        total = blocks[:half].astype(F32) + arrived.astype(F32)
        blocks = total if half == 1 else total.astype(BF16)
    return blocks[0]


def one_hot_cols(ids, width):
    rows = ids.shape[1]
    spread = jnp.transpose(jnp.broadcast_to(ids, (LANES, rows)))
    lane = lax.broadcasted_iota(jnp.int32, (rows, LANES), 1)
    tiles = [jnp.where(spread == lane + start, 1.0, 0.0).astype(BF16) for start in range(0, width, LANES)]
    return jnp.concatenate(tiles, axis=1)[:, :width]


def hot_cols(first, second, width):
    rows = first.shape[1]
    left = jnp.transpose(jnp.broadcast_to(first, (LANES, rows)))
    right = jnp.transpose(jnp.broadcast_to(second, (LANES, rows)))
    lane = lax.broadcasted_iota(jnp.int32, (rows, LANES), 1)
    tiles = [
        jnp.where((left == lane + start) | (right == lane + start), 1.0, 0.0).astype(BF16)
        for start in range(0, width, LANES)
    ]
    return jnp.concatenate(tiles, axis=1)


def hot_rows(first, second, width):
    row = lax.broadcasted_iota(jnp.int32, (width, first.shape[1]), 0)
    return jnp.where((row == first) | (row == second), 1.0, 0.0).astype(BF16)


def layer_kernel(
    count,
    me_ref,
    nodes_ref,
    halo_ref,
    edges_ref,
    cot_ref,
    w_edge_in_ref,
    w_edge_out_ref,
    w_node_in_ref,
    w_node_out_ref,
    send_ref,
    recv_ref,
    blocks_ref,
    da_ref,
    sums_ref,
    node_part_ref,
    table,
    zeta,
    slope,
    normed,
    inv,
    agg,
    dagg,
    grads_no,
    grads_ni,
    grads_eo,
    grads_ei,
):
    owned, width = nodes_ref.shape
    n_halo = halo_ref.shape[0]
    n_edges = edges_ref.shape[0]
    n_table = table.shape[0]
    n_blocks = n_edges // BLOCK
    w_self = w_edge_in_ref.at[:width]
    w_send = w_edge_in_ref.at[width : 2 * width]
    w_recv = w_edge_in_ref.at[2 * width :]
    w_host = w_node_in_ref.at[:width]
    w_inbox = w_node_in_ref.at[width:]

    table[:owned] = mm(nodes_ref[...], w_send[...]).astype(BF16)
    table[owned : 2 * owned] = mm(nodes_ref[...], w_recv[...]).astype(BF16)
    table[2 * owned : 2 * owned + n_halo] = mm(halo_ref[...], w_send[...]).astype(BF16)
    if n_table > 2 * owned + n_halo:
        table[2 * owned + n_halo :] = jnp.zeros((n_table - 2 * owned - n_halo, width), BF16)
    agg[...] = jnp.zeros_like(agg)

    def ids(block):
        cols = pl.ds(pl.multiple_of(block * BLOCK, BLOCK), BLOCK)
        sender = send_ref[:, cols]
        receiver = recv_ref[:, cols]
        sender = jnp.where(sender < owned, sender, sender + owned)
        return sender, jnp.maximum(receiver, 0) + owned, receiver

    @pl.loop(0, n_blocks)
    def _(block):
        rows = pl.ds(pl.multiple_of(block * BLOCK, BLOCK), BLOCK)
        sender, safe, receiver = ids(block)
        pre = mm(edges_ref[rows], w_self[...]) + mm(hot_cols(sender, safe, n_table), table[...])
        sigma = sigmoid(pre)
        zed = (pre * sigma).astype(BF16)
        zeta[rows] = zed
        slope[rows] = (sigma * (1.0 + pre * (1.0 - sigma))).astype(BF16)
        unit, inv_std = normalize(mm(zed, w_edge_out_ref[...]))
        message = unit.astype(BF16)
        normed[rows] = message
        inv[rows] = inv_std
        agg[...] += mm(hot_rows(receiver, receiver, owned), message)

    inbox = agg[...].astype(BF16)
    nodes = nodes_ref[...]
    pre = mm(nodes, w_host[...]) + mm(inbox, w_inbox[...])
    sigma = sigmoid(pre)
    zed = (pre * sigma).astype(BF16)
    unit, inv_std = normalize(mm(zed, w_node_out_ref[...]))
    upstream = cot_ref[...].astype(F32)
    dy = norm_back(upstream, unit, inv_std).astype(BF16)
    db = (mm_cols(dy, w_node_out_ref[...]) * (sigma * (1.0 + pre * (1.0 - sigma)))).astype(BF16)
    dagg[...] = mm_cols(db, w_inbox[...]).astype(BF16)
    node_part_ref[...] = upstream + mm_cols(db, w_host[...])
    grads_no[...] = mm_rows(zed, dy)
    grads_ni[:width] = mm_rows(nodes, db)
    grads_ni[width:] = mm_rows(inbox, db)

    sums_ref[...] = jnp.zeros_like(sums_ref)
    grads_eo[...] = jnp.zeros_like(grads_eo)
    grads_ei[:width] = jnp.zeros((width, width), F32)

    @pl.loop(0, n_blocks)
    def _(block):
        rows = pl.ds(pl.multiple_of(block * BLOCK, BLOCK), BLOCK)
        sender, safe, receiver = ids(block)
        up = mm(one_hot_cols(receiver, owned), dagg[...])
        dye = norm_back(up, normed[rows].astype(F32), inv[rows]).astype(BF16)
        grads_eo[...] += mm_rows(zeta[rows], dye)
        da = (mm_cols(dye, w_edge_out_ref[...]) * slope[rows].astype(F32)).astype(BF16)
        da_ref[rows] = da
        grads_ei[:width] += mm_rows(edges_ref[rows], da)
        sums_ref[...] += mm(hot_rows(sender, safe, n_table), da)

    own = sums_ref[:owned].astype(BF16)
    far = sums_ref[2 * owned : 2 * owned + n_halo].astype(BF16)
    grads_ei[width : 2 * width] = mm_rows(nodes, own) + mm_rows(halo_ref[...], far)
    grads_ei[2 * width :] = mm_rows(nodes, sums_ref[owned : 2 * owned].astype(BF16))

    me = me_ref[0]
    sources = (grads_no, grads_ni, grads_eo, grads_ei)
    shares = [source.shape[0] // count for source in sources]
    spare = blocks_ref.shape[1] - sum(shares)

    @pl.loop(0, count)
    def _(target):
        parts = [
            source[pl.ds(pl.multiple_of(target * share, share), share)] for source, share in zip(sources, shares)
        ]
        if spare:
            parts.append(jnp.zeros((spare, width), F32))
        blocks_ref[cube_position(target, me, count)] = jnp.concatenate(parts, axis=0).astype(BF16)


def layer(count, me, nodes, halo, edges, cot, w_edge_in, w_edge_out, w_node_in, w_node_out, sender, receiver):
    owned, width = nodes.shape
    n_edges = edges.shape[0]
    n_table = -(-(2 * owned + halo.shape[0]) // LANES) * LANES
    share = sum(r * width // count for r in (1, 2, 1, 3))
    share = -(-share // 16) * 16
    vmem = pl.BlockSpec(memory_space=pltpu.VMEM)
    smem = pl.BlockSpec(memory_space=pltpu.SMEM)
    return pl.pallas_call(
        functools.partial(layer_kernel, count),
        out_shape=(
            jax.ShapeDtypeStruct((count, share, width), BF16),
            jax.ShapeDtypeStruct((n_edges, width), BF16),
            jax.ShapeDtypeStruct((n_table, width), F32),
            jax.ShapeDtypeStruct((owned, width), F32),
        ),
        in_specs=[smem] + [vmem] * 10,
        out_specs=(vmem,) * 4,
        scratch_shapes=[
            pltpu.VMEM((n_table, width), BF16),
            pltpu.VMEM((n_edges, width), BF16),
            pltpu.VMEM((n_edges, width), BF16),
            pltpu.VMEM((n_edges, width), BF16),
            pltpu.VMEM((n_edges, 1), F32),
            pltpu.VMEM((owned, width), F32),
            pltpu.VMEM((owned, width), BF16),
            pltpu.VMEM((width, width), F32),
            pltpu.VMEM((2 * width, width), F32),
            pltpu.VMEM((width, width), F32),
            pltpu.VMEM((3 * width, width), F32),
        ],
        compiler_params=pltpu.CompilerParams(vmem_limit_bytes=56 << 20),
        name="layer",
    )(me, nodes, halo, edges, cot, w_edge_in, w_edge_out, w_node_in, w_node_out, sender, receiver)


def trade(rows):
    return lax.all_to_all(rows, "patch", split_axis=0, concat_axis=0, tiled=True)


def body(
    count,
    nodes,
    edges,
    cot_nodes,
    w_edge_in,
    w_edge_out,
    w_node_in,
    w_node_out,
    send_rows,
    edge_sender,
    edge_receiver,
):
    owned, width = nodes.shape
    flat = send_rows.reshape(-1)
    pick = (flat[:, None] == jnp.arange(owned, dtype=jnp.int32)[None, :]).astype(BF16)
    halo = trade(mm(pick, nodes).astype(BF16))
    me = lax.axis_index("patch").astype(jnp.int32).reshape(1)
    blocks, edge_da, sums, node_part = layer(
        count,
        me,
        nodes,
        halo,
        edges,
        cot_nodes,
        w_edge_in,
        w_edge_out,
        w_node_in,
        w_node_out,
        edge_sender.reshape(1, -1),
        edge_receiver.reshape(1, -1),
    )
    total = cube_reduce(blocks, count)
    returned = trade(sums[2 * owned : 2 * owned + flat.size].astype(BF16))
    edge_grad = mm_cols(edge_da, w_edge_in[:width]).astype(BF16)
    own_sums = (sums[:owned] + mm_rows(pick, returned)).astype(BF16)
    node_grad = (
        node_part
        + mm_cols(own_sums, w_edge_in[width : 2 * width])
        + mm_cols(sums[owned : 2 * owned].astype(BF16), w_edge_in[2 * width :])
    ).astype(BF16)
    cuts = [width // count * part for part in (1, 3, 4, 7)]
    return (
        node_grad,
        edge_grad,
        total[cuts[2] : cuts[3]],
        total[cuts[1] : cuts[2]],
        total[cuts[0] : cuts[1]],
        total[: cuts[0]],
    )


def solution(mesh):
    rows = P(("groups", "patch"), None)
    flat = P(("groups", "patch"))
    return jax.shard_map(
        functools.partial(body, mesh.shape["patch"]),
        mesh=mesh,
        in_specs=(rows, rows, rows, P(), P(), P(), P(), P(("groups", "patch"), None, None), flat, flat),
        out_specs=(rows,) * 6,
        check_vma=False,
    )
```

time: 320 us -> 98.7 us (0.31)
  waiting for transfers between devices: 203 us -> 31.8 us
  matrix products: 49.4 us -> 7.36 us
  Pallas kernels: 0 us -> 30.3 us
  local copies, waits for them, and re-layouts: 27.8 us -> 12.3 us
  between operations: 14.2 us -> 0.77 us
  other arithmetic: 11.3 us -> 3.3 us
    reduce_scatter x4 -> x0, waiting for transfers between devices: 201 us -> none  [the longest x1 69.9 us: edge_in_sum(): return lax.psum_scatter(stacked, 'patch', scatter_dimension=0, tiled=True)]
    dot_general x23 -> x4, matrix products: 49.4 us -> 7.36 us  [the longest x3 6.2 us: mm_cols(): lax.dot_general(left, right, (((1,), (1,)), ((), ())), preferred_element_...]
    pallas_call x0 -> x1, Pallas kernels: none -> 30.3 us  [layer(): pl.pallas_call(functools.partial(layer_kernel, count), out_shape=(jax.Sha...]
    ppermute x0 -> x4, waiting for transfers between devices: none -> 24.9 us  [cube_reduce(): arrived = lax.ppermute(blocks[half:], 'patch', pairs)]
    gather x4 -> x0, local copies, waits for them, and re-layouts: 19.7 us -> none  [the longest x1 9.2 us: body(): proj_recv[safe_recv].astype(jnp.float32)]
    all_to_all x1 -> x2, waiting for transfers between devices: 0.01 us -> 6.89 us  [trade(): lax.all_to_all(rows, 'patch', split_axis=0, concat_axis=0, tiled=True)]
    all_to_all x1 -> x0, starting transfers between devices: 6.02 us -> none  [give_back(): lax.all_to_all(rows.astype(jnp.bfloat16), 'patch', split_axis=0, concat_a...]
    slice x2 -> x8, local copies, waits for them, and re-layouts: 0.05 us -> 5.65 us  [the longest x4 3.63 us: cube_reduce(): arrived = lax.ppermute(blocks[half:], 'patch', pairs)]
  transfers between devices with their start and end apart: 6 -> 6, of which waited for: 5 -> 5; matrix products, arithmetic and copies ran while one was open for 17% -> 9% of each run, Pallas kernels for 0% -> 0%
where the time goes in v1:
time: 98.7 us; the launch traced here: 98.2 us
  waiting for transfers between devices  31.8 us (32%)
  Pallas kernels  30.3 us (31%)
  local copies, waits for them, and re-layouts  12.3 us (12%)
  starting transfers between devices  12.3 us (12%)
  matrix products  7.36 us (7%)
  other arithmetic  3.3 us (3%)
    pallas_call x1, Pallas kernels, layer(): pl.pallas_call(functools.partial(layer_kernel, count), out_shape=(jax.Sha...  30.3 us
    ppermute x4, waiting for transfers between devices, cube_reduce(): arrived = lax.ppermute(blocks[half:], 'patch', pairs)  24.9 us
    all_to_all x2, starting transfers between devices, trade(): lax.all_to_all(rows, 'patch', split_axis=0, concat_axis=0, tiled=True)  11.5 us
    all_to_all x2, waiting for transfers between devices, trade(): lax.all_to_all(rows, 'patch', split_axis=0, concat_axis=0, tiled=True)  6.89 us
    dot_general x3, matrix products, mm_cols(): lax.dot_general(left, right, (((1,), (1,)), ((), ())), preferred_element_...  6.2 us
    slice x4, local copies, waits for them, and re-layouts, cube_reduce(): arrived = lax.ppermute(blocks[half:], 'patch', pairs)  3.63 us
    all_to_all x4, local copies, waits for them, and re-layouts, trade(): lax.all_to_all(rows, 'patch', split_axis=0, concat_axis=0, tiled=True)  3.53 us
    convert_element_type x3, other arithmetic, cube_reduce(): blocks = total if half == 1 else total.astype(BF16)  3.16 us
  transfers between devices with their start and end apart: 6, of which 5 were waited for; matrix products, arithmetic and copies ran while one was open for 9% of the time, Pallas kernels for 0%

profile of v1, /device:TPU:0, one launch (start us, length us, event | category | flops | bytes accessed | tf_op | source)
XLA Modules:
  0.0 98.2 jit_solution(420259685769974982)
XLA Ops:
  0.6 0.8 copy.17
  1.4 0.1 eq.15
  1.5 1.2 %convolution_convert_fusion.1 = bf16[64,512]{1,0:T(8,128)(2,1)S(1)} fusion(bf16[256,512]{1,0:T(8,128)(2,1)} %nodes_ref.1, s32[64]{0:T(128)S(1)} %eq.15), kind=kOutput, calls=%fused_computation.8 | convolution fusion | flops 16826368 | bytes 327936 | tf_op jit(solution)/shard_map/dot_general | solution.py:18
  2.6 0.7 all_to_all.15
  3.3 7.4 %all-to-all-start = ((bf16[16,4,512]{2,1,0:T(4,128)(2,1)}), bf16[16,4,512]{2,1,0:T(4,128)(2,1)S(1)}, u32[]{:S(2)}, u32[]{:S(2)}) async-start(bf16[16,4,512]{2,1,0:T(4,128)(2,1)} %all_to_all.15), calls=%async_computation | async-start | bytes 131072 | tf_op jit(solution)/shard_map/all_to_all | solution.py:263
  10.7 6.9 %all-to-all-done = bf16[16,4,512]{2,1,0:T(4,128)(2,1)S(1)} async-done(((bf16[16,4,512]{2,1,0:T(4,128)(2,1)}), bf16[16,4,512]{2,1,0:T(4,128)(2,1)S(1)}, u32[]{:S(2)}, u32[]{:S(2)}) %all-to-all-start) | async-done | bytes 65568 | tf_op jit(solution)/shard_map/all_to_all | solution.py:263
  17.6 0.6 all_to_all.17.halo_ref
  18.2 30.3 %layer.1 = (bf16[16,224,512]{2,1,0:T(8,128)(2,1)}, bf16[2048,512]{1,0:T(8,128)(2,1)}, f32[640,512]{1,0:T(8,128)}, f32[256,512]{1,0:T(8,128)}) custom-call(s32[1]{0:T(128)} %bitcast.me_ref, bf16[256,512]{1,0:T(8,128)(2,1)} %nodes_ref.1, bf16[64,512]{1,0:T(8,128)(2,1)} %all_to_all.17.halo_ref, bf16[2048,512]{1,0:T(8,128)(2,1)} %edges_ref.1, ...), custom_call_target="tpu_custom_call" | custom-call | tf_op jit(solution)/shard_map/layer/pallas_call | solution.py:234
  48.5 0.0 copy-start.1
  48.6 1.8 %slice.75 = bf16[8,224,512]{2,1,0:T(8,128)(2,1)S(1)} slice(bf16[16,224,512]{2,1,0:T(8,128)(2,1)} %get-tuple-element.13), slice={[8:16], [0:224], [0:512]} | slice | bytes 3670016 | tf_op jit(solution)/shard_map/slice | solution.py:75
  50.4 0.1 collective-permute-start
  50.5 3.8 %collective-permute-done = bf16[8,224,512]{2,1,0:T(8,128)(2,1)S(1)} collective-permute-done((bf16[8,224,512]{2,1,0:T(8,128)(2,1)S(1)}, bf16[8,224,512]{2,1,0:T(8,128)(2,1)S(1)}, u32[]{:S(2)}, u32[]{:S(2)}) %collective-permute-start) | collective-permute-done | bytes 1835040 | tf_op jit(solution)/shard_map/ppermute | solution.py:75
  54.2 0.0 copy-done.1
  54.3 0.6 add_convert_fusion
  54.9 0.0 copy-start.4
  54.9 1.0 slice.93
  55.8 0.1 collective-permute-start.1
  56.0 0.5 copy-done.4
  56.5 0.1 convert.4
  56.6 0.0 copy-start.5
  56.6 0.8 copy-done.5
  57.4 0.7 all_to_all.18
  58.1 4.2 %all-to-all-start.1 = ((bf16[16,4,512]{2,1,0:T(4,128)(2,1)}), bf16[16,4,512]{2,1,0:T(4,128)(2,1)}, u32[]{:S(2)}, u32[]{:S(2)}) async-start(bf16[16,4,512]{2,1,0:T(4,128)(2,1)} %all_to_all.18), calls=%async_computation.1 | async-start | bytes 131072 | tf_op jit(solution)/shard_map/all_to_all | solution.py:263
  62.3 0.0 copy-start
  62.3 0.0 copy-start.7
  62.3 7.9 %collective-permute-done.1 = bf16[4,224,512]{2,1,0:T(8,128)(2,1)} collective-permute-done((bf16[4,224,512]{2,1,0:T(8,128)(2,1)}, bf16[4,224,512]{2,1,0:T(8,128)(2,1)}, u32[]{:S(2)}, u32[]{:S(2)}) %collective-permute-start.1) | collective-permute-done | bytes 917536 | tf_op jit(solution)/shard_map/ppermute | solution.py:75
  70.2 1.4 %add_convert_fusion.1 = bf16[4,224,512]{2,1,0:T(8,128)(2,1)S(1)} fusion(bf16[4,224,512]{2,1,0:T(8,128)(2,1)} %collective-permute-done.1, bf16[8,224,512]{2,1,0:T(8,128)(2,1)S(1)} %add_convert_fusion), kind=kLoop, calls=%fused_computation.2 | loop fusion | flops 1835008 | bytes 2752512 | tf_op jit(solution)/shard_map/convert_element_type | solution.py:77
  71.6 0.0 copy-start.2
  71.6 0.9 copy-done.2
  72.5 0.8 slice.95
  73.3 0.1 collective-permute-start.2
  73.4 0.0 copy-done
  73.4 0.0 copy-done.7
  73.4 0.0 copy-start.6
  73.4 2.6 %convolution_convert_fusion = bf16[2048,512]{1,0:T(8,128)(2,1)} fusion(bf16[2048,512]{1,0:T(8,128)(2,1)S(1)} %copy-done.7, bf16[1536,512]{1,0:T(8,128)(2,1)S(1)} %copy-done), kind=kOutput, calls=%fused_computation.1 | convolution fusion | flops 1074790400 | bytes 4718592 | tf_op jit(solution)/shard_map/dot_general | solution.py:26
  76.0 0.0 copy-start.3
  76.0 0.0 all-to-all-done.1
  76.0 1.6 %all_to_all.20 = bf16[64,512]{1,0:T(8,128)(2,1)} reshape(bf16[16,4,512]{2,1,0:T(4,128)(2,1)} %all-to-all-done.1) | data formatting | bytes 131072 | tf_op jit(solution)/shard_map/all_to_all | solution.py:263
  77.6 0.0 copy-done.6
  77.6 1.6 %convolution_add_fusion.2 = f32[256,512]{1,0:T(8,128)S(1)} fusion(f32[256,512]{1,0:T(8,128)S(1)} %copy-done.6, bf16[64,512]{1,0:T(8,128)(2,1)} %all_to_all.20, bf16[1536,512]{1,0:T(8,128)(2,1)S(1)} %copy-done, f32[640,512]{1,0:T(8,128)} %get-tuple-element.11, s32[64]{0:T(128)S(1)} %eq.15), kind=kOutput, calls=%fused_computation.5 | convolution fusion | flops 151404544 | bytes 2163200 | tf_op jit(solution)/shard_map/dot_general | solution.py:26
  79.2 7.8 %collective-permute-done.2 = bf16[2,224,512]{2,1,0:T(8,128)(2,1)} collective-permute-done((bf16[2,224,512]{2,1,0:T(8,128)(2,1)}, bf16[2,224,512]{2,1,0:T(8,128)(2,1)}, u32[]{:S(2)}, u32[]{:S(2)}) %collective-permute-start.2) | collective-permute-done | bytes 458784 | tf_op jit(solution)/shard_map/ppermute | solution.py:75
  87.0 0.0 copy-done.3
  87.0 1.1 %add_convert_fusion.2 = bf16[2,224,512]{2,1,0:T(8,128)(2,1)S(1)} fusion(bf16[2,224,512]{2,1,0:T(8,128)(2,1)} %collective-permute-done.2, bf16[4,224,512]{2,1,0:T(8,128)(2,1)S(1)} %copy-done.3), kind=kLoop, calls=%fused_computation.9 | loop fusion | flops 917504 | bytes 1376256 | tf_op jit(solution)/shard_map/convert_element_type | solution.py:77
  88.2 0.5 collective-permute-start.3
  88.7 2.0 %fusion = bf16[256,512]{1,0:T(8,128)(2,1)} fusion(f32[256,512]{1,0:T(8,128)S(1)} %convolution_add_fusion.2, bf16[1536,512]{1,0:T(8,128)(2,1)S(1)} %copy-done, bf16[640,512]{1,0:T(8,128)(2,1)} %copy-done.5), kind=kOutput, calls=%fused_computation.6 | convolution fusion | flops 134479872 | bytes 1572864 | tf_op jit(solution)/shard_map/dot_general | solution.py:26
  90.7 5.4 %collective-permute-done.3 = bf16[1,224,512]{2,1,0:T(8,128)(2,1)S(1)} collective-permute-done((bf16[1,224,512]{2,1,0:T(8,128)(2,1)S(1)}, bf16[1,224,512]{2,1,0:T(8,128)(2,1)S(1)}, u32[]{:S(2)}, u32[]{:S(2)}) %collective-permute-start.3) | collective-permute-done | bytes 229408 | tf_op jit(solution)/shard_map/ppermute | solution.py:75
  96.1 0.1 convert_add_fusion
  96.1 0.7 slice_bitcast_fusion.1
  96.8 0.7 slice_bitcast_fusion.2
  97.5 0.7 slice_bitcast_fusion
  (2 shorter events, 0.0 us)
Async XLA Ops:
  3.3 14.3 %all-to-all-start = ((bf16[16,4,512]{2,1,0:T(4,128)(2,1)}), bf16[16,4,512]{2,1,0:T(4,128)(2,1)S(1)}, u32[]{:S(2)}, u32[]{:S(2)}) async-start(bf16[16,4,512]{2,1,0:T(4,128)(2,1)} %all_to_all.15), calls=%async_computation | async-start | bytes 131072 | tf_op jit(solution)/shard_map/all_to_all | solution.py:263
  48.5 5.7 %copy-start.1 = (bf16[16,224,512]{2,1,0:T(8,128)(2,1)S(1)}, bf16[16,224,512]{2,1,0:T(8,128)(2,1)}, u32[]{:S(2)}) copy-start(bf16[16,224,512]{2,1,0:T(8,128)(2,1)} %get-tuple-element.13) | copy-start | bytes 11010052
  50.4 3.9 %collective-permute-start = (bf16[8,224,512]{2,1,0:T(8,128)(2,1)S(1)}, bf16[8,224,512]{2,1,0:T(8,128)(2,1)S(1)}, u32[]{:S(2)}, u32[]{:S(2)}) collective-permute-start(bf16[8,224,512]{2,1,0:T(8,128)(2,1)S(1)} %slice.75), channel_id=1, source_target_pairs={{0,1},{1,0},{2,3},{3,2},{4,5},{5,4},{6,7},{7,6},{8,9},{9,8},{10,11... | collective-permute-start | bytes 5505032 | tf_op jit(solution)/shard_map/ppermute | solution.py:75
  54.9 1.6 %copy-start.4 = (f32[640,512]{1,0:T(8,128)S(1)}, f32[640,512]{1,0:T(8,128)}, u32[]{:S(2)}) copy-start(f32[640,512]{1,0:T(8,128)} %get-tuple-element.11) | copy-start | bytes 3932164
  55.8 14.3 %collective-permute-start.1 = (bf16[4,224,512]{2,1,0:T(8,128)(2,1)}, bf16[4,224,512]{2,1,0:T(8,128)(2,1)}, u32[]{:S(2)}, u32[]{:S(2)}) collective-permute-start(bf16[4,224,512]{2,1,0:T(8,128)(2,1)} %slice.93), channel_id=1, source_target_pairs={{0,2},{1,5},{2,0},{3,7},{4,6},{5,1},{6,4},{7,3},{8,10},{9,13},{10,... | collective-permute-start | bytes 2752520 | tf_op jit(solution)/shard_map/ppermute | solution.py:75
  56.6 0.8 copy-start.5
  58.1 17.9 %all-to-all-start.1 = ((bf16[16,4,512]{2,1,0:T(4,128)(2,1)}), bf16[16,4,512]{2,1,0:T(4,128)(2,1)}, u32[]{:S(2)}, u32[]{:S(2)}) async-start(bf16[16,4,512]{2,1,0:T(4,128)(2,1)} %all_to_all.18), calls=%async_computation.1 | async-start | bytes 131072 | tf_op jit(solution)/shard_map/all_to_all | solution.py:263
  62.3 11.1 %copy-start = (bf16[1536,512]{1,0:T(8,128)(2,1)S(1)}, bf16[1536,512]{1,0:T(8,128)(2,1)}, u32[]{:S(2)}) copy-start(bf16[1536,512]{1,0:T(8,128)(2,1)} %w_edge_in_ref.1) | copy-start | bytes 4718596
  62.3 11.1 %copy-start.7 = (bf16[2048,512]{1,0:T(8,128)(2,1)S(1)}, bf16[2048,512]{1,0:T(8,128)(2,1)}, u32[]{:S(2)}) copy-start(bf16[2048,512]{1,0:T(8,128)(2,1)} %get-tuple-element.12) | copy-start | bytes 6291460
  71.6 0.9 copy-start.2
  73.3 13.7 %collective-permute-start.2 = (bf16[2,224,512]{2,1,0:T(8,128)(2,1)}, bf16[2,224,512]{2,1,0:T(8,128)(2,1)}, u32[]{:S(2)}, u32[]{:S(2)}) collective-permute-start(bf16[2,224,512]{2,1,0:T(8,128)(2,1)} %slice.95), channel_id=1, source_target_pairs={{0,4},{1,13},{2,6},{3,15},{4,0},{5,9},{6,2},{7,11},{8,12},{9,5},{1... | collective-permute-start | bytes 1376264 | tf_op jit(solution)/shard_map/ppermute | solution.py:75
  73.4 4.2 %copy-start.6 = (f32[256,512]{1,0:T(8,128)S(1)}, f32[256,512]{1,0:T(8,128)}, u32[]{:S(2)}) copy-start(f32[256,512]{1,0:T(8,128)} %get-tuple-element.10) | copy-start | bytes 1572868
  76.0 11.0 %copy-start.3 = (bf16[4,224,512]{2,1,0:T(8,128)(2,1)S(1)}, bf16[4,224,512]{2,1,0:T(8,128)(2,1)}, u32[]{:S(2)}) copy-start(bf16[4,224,512]{2,1,0:T(8,128)(2,1)} %copy-done.2) | copy-start | bytes 2752516
  88.2 7.9 %collective-permute-start.3 = (bf16[1,224,512]{2,1,0:T(8,128)(2,1)S(1)}, bf16[1,224,512]{2,1,0:T(8,128)(2,1)S(1)}, u32[]{:S(2)}, u32[]{:S(2)}) collective-permute-start(bf16[1,224,512]{2,1,0:T(8,128)(2,1)S(1)} %slice.97), channel_id=1, source_target_pairs={{0,12},{1,3},{2,14},{3,1},{4,8},{5,7},{6,10},{7,5},{8,4},{9,11},{1... | collective-permute-start | bytes 688136 | tf_op jit(solution)/shard_map/ppermute | solution.py:75

commit v2 on v0

v2 whole, which is shorter than its diff:
```python
import functools

import jax
import jax.numpy as jnp
from jax import lax
from jax.experimental import pallas as pl
from jax.experimental.pallas import tpu as pltpu
from jax.sharding import PartitionSpec as P

BF16 = jnp.bfloat16
F32 = jnp.float32
EPS = 1e-05
LANES = 128
BLOCK = 1024
TILE = 256
HALO_ROWS = 8
GRID_BLOCK = 1024


def mm(left, right):
    return jnp.dot(left, right, preferred_element_type=F32)


def mm_rows(left, right):
    return lax.dot_general(left, right, (((0,), (0,)), ((), ())), preferred_element_type=F32)


def mm_cols(left, right):
    return lax.dot_general(left, right, (((1,), (1,)), ((), ())), preferred_element_type=F32)


def sigmoid(values):
    return 0.5 * jnp.tanh(0.5 * values) + 0.5


def normalize(values):
    center = values - jnp.mean(values, axis=-1, keepdims=True)
    inv_std = lax.rsqrt(jnp.mean(center * center, axis=-1, keepdims=True) + EPS)
    return center * inv_std, inv_std


def norm_back(upstream, normed, inv_std):
    return inv_std * (
        upstream
        - jnp.mean(upstream, axis=-1, keepdims=True)
        - normed * jnp.mean(upstream * normed, axis=-1, keepdims=True)
    )


def cube_masks(count):
    return [1 << i for i in range(count.bit_length() - 1)]


def cube_orders(count):
    rest = list(range(1, count.bit_length() - 1))
    return [0] + rest, [0] + rest[:2][::-1] + rest[2:]


def cube_place(apart, parity, count):
    bits = count.bit_length() - 1
    coords = [(apart >> i) & 1 for i in range(bits)]
    even, odd = [sum(coords[dim] << (bits - 1 - j) for j, dim in enumerate(order)) for order in cube_orders(count)]
    return jnp.where(parity == 0, even, odd)


def cube_permute(blocks, step, count):
    mask, orders = cube_masks(count), cube_orders(count)
    pairs = [(i, i ^ mask[orders[i & 1][step]]) for i in range(count)]
    return lax.ppermute(blocks, "patch", pairs)


def one_hot_cols(ids, width):
    rows = ids.shape[1]
    spread = jnp.transpose(jnp.broadcast_to(ids, (LANES, rows)))
    lane = lax.broadcasted_iota(jnp.int32, (rows, LANES), 1)
    tiles = [jnp.where(spread == lane + start, 1.0, 0.0).astype(BF16) for start in range(0, width, LANES)]
    return jnp.concatenate(tiles, axis=1)[:, :width]


def hot_cols(first, second, width):
    rows = first.shape[1]
    left = jnp.transpose(jnp.broadcast_to(first, (LANES, rows)))
    right = jnp.transpose(jnp.broadcast_to(second, (LANES, rows)))
    lane = lax.broadcasted_iota(jnp.int32, (rows, LANES), 1)
    tiles = [
        jnp.where((left == lane + start) | (right == lane + start), 1.0, 0.0).astype(BF16)
        for start in range(0, width, LANES)
    ]
    return jnp.concatenate(tiles, axis=1)


def hot_rows(first, second, width):
    row = lax.broadcasted_iota(jnp.int32, (width, first.shape[1]), 0)
    return jnp.where((row == first) | (row == second), 1.0, 0.0).astype(BF16)


def edge_ids(rows, owned, slot, send_ref, recv_ref, block_of):
    sender = send_ref[:, rows]
    receiver = recv_ref[:, rows]
    far = sender - owned
    sender = jnp.where(far < 0, sender, 2 * owned + block_of(far // slot) + far % slot)
    return sender, jnp.maximum(receiver, 0) + owned, receiver


def take_rows(step, count, slot):
    weight = count >> (step + 1)
    shape = (count // 2 * slot, count * slot)
    out = lax.broadcasted_iota(jnp.int32, shape, 0)
    block, row = out // slot, out % slot
    place = block // weight * 2 * weight + weight + block % weight
    return jnp.where(lax.broadcasted_iota(jnp.int32, shape, 1) == place * slot + row, 1.0, 0.0).astype(BF16)


def put_blocks(sources, me, count, keep_ref, send_ref):
    shares = [source.shape[0] // count for source in sources]
    half = count // 2
    size = keep_ref.shape[0] // half
    spare = size - sum(shares)

    @pl.loop(0, count)
    def _(target):
        parts = [
            source[pl.ds(pl.multiple_of(target * share, share), share)] for source, share in zip(sources, shares)
        ]
        if spare:
            parts.append(jnp.zeros((spare, keep_ref.shape[1]), F32))
        block = jnp.concatenate(parts, axis=0).astype(BF16)
        place = cube_place(target ^ me, target & 1, count)

        @pl.when(place < half)
        def _():
            keep_ref[pl.ds(pl.multiple_of(place * size, size), size)] = block

        @pl.when(place >= half)
        def _():
            send_ref[pl.ds(pl.multiple_of((place - half) * size, size), size)] = block


def pick_kernel(count, me_ref, picks_ref, nodes_ref, pick_ref, rows_ref):
    slot = picks_ref.shape[0]
    owned = nodes_ref.shape[0]
    me = me_ref[0]

    def choose(rows, start):
        shape = (rows, count)
        row = lax.broadcasted_iota(jnp.int32, shape, 0)
        first = start(lax.broadcasted_iota(jnp.int32, shape, 1))
        ids = jnp.zeros(shape, jnp.int32)
        for place in range(slot):
            ids = ids + jnp.where(row == first + place, picks_ref[place : place + 1] + 1, 0)
        ids = jnp.sum(ids.astype(F32), axis=1, keepdims=True).astype(jnp.int32) - 1
        node = lax.broadcasted_iota(jnp.int32, (rows, owned), 1)
        return jnp.where(node == ids, 1.0, 0.0).astype(BF16)

    rows_ref[...] = mm(choose(count * HALO_ROWS, lambda device: device * HALO_ROWS), nodes_ref[...]).astype(BF16)
    pick_ref[...] = choose(count * slot, lambda device: cube_place(device ^ me, me & 1, count) * slot)


def local_kernel(send_ref, recv_ref, nodes_ref, w_edge_in_ref, edges_ref, base_ref, table):
    owned, width = nodes_ref.shape

    @pl.when(pl.program_id(0) == 0)
    def _():
        nodes = nodes_ref[...]
        table[:owned] = mm(nodes, w_edge_in_ref[width : 2 * width]).astype(BF16)
        table[owned:] = mm(nodes, w_edge_in_ref[2 * width :]).astype(BF16)

    sender = send_ref[...]
    sender = jnp.where(sender < owned, sender, -1)
    hot = hot_cols(sender, jnp.maximum(recv_ref[...], 0) + owned, 2 * owned)
    base_ref[...] = mm(edges_ref[...], w_edge_in_ref[:width]) + mm(hot, table[...])


def forward_kernel(
    count,
    slot,
    me_ref,
    send_ref,
    recv_ref,
    halo_ref,
    w_edge_in_far,
    base_far,
    w_edge_out_far,
    nodes_far,
    w_node_in_far,
    w_node_out_far,
    cot_far,
    edges_far,
    keep_ref,
    away_ref,
    zeta_ref,
    slope_ref,
    normed_ref,
    inv_ref,
    dagg_ref,
    node_part_ref,
    nodes_ref,
    w_edge_out_ref,
    edges_ref,
    w_send,
    w_recv,
    base,
    w_node_in_ref,
    w_node_out_ref,
    cot_ref,
    table,
    agg,
    grads_no,
    grads_ni,
    base_sems,
    sems,
):
    owned, width = nodes_ref.shape
    n_table = table.shape[0]
    n_blocks = base.shape[0] // BLOCK

    def block_rows(block):
        return pl.ds(pl.multiple_of(block * BLOCK, BLOCK), BLOCK)

    def base_copy(block):
        rows = block_rows(block)
        return pltpu.make_async_copy(base_far.at[rows], base.at[rows], base_sems.at[block])

    pairs = (
        (w_edge_in_far.at[width : 2 * width], w_send),
        (w_edge_out_far, w_edge_out_ref),
        (nodes_far, nodes_ref),
        (w_node_in_far, w_node_in_ref),
        (w_node_out_far, w_node_out_ref),
        (cot_far, cot_ref),
        (edges_far, edges_ref),
        (w_edge_in_far.at[2 * width :], w_recv),
    )
    copies = [pltpu.make_async_copy(src, dst, sems.at[i]) for i, (src, dst) in enumerate(pairs)]
    copies[0].start()
    base_copy(0).start()
    copies[1].start()

    @pl.loop(1, n_blocks)
    def _(block):
        base_copy(block).start()

    for copy in copies[2:]:
        copy.start()
    agg[...] = jnp.zeros_like(agg)
    copies[0].wait()
    table[...] = mm(halo_ref[...], w_send[...]).astype(BF16)
    copies[1].wait()

    @pl.loop(0, n_blocks)
    def _(block):
        rows = block_rows(block)
        base_copy(block).wait()
        sender, _, receiver = edge_ids(rows, owned, slot, send_ref, recv_ref, lambda device: device * HALO_ROWS)
        pre = base[rows] + mm(one_hot_cols(sender - 2 * owned, n_table), table[...])
        sigma = sigmoid(pre)
        zed = (pre * sigma).astype(BF16)
        zeta_ref[rows] = zed
        slope_ref[rows] = (sigma * (1.0 + pre * (1.0 - sigma))).astype(BF16)
        unit, inv_std = normalize(mm(zed, w_edge_out_ref[...]))
        message = unit.astype(BF16)
        normed_ref[rows] = message
        inv_ref[rows] = inv_std
        agg[...] += mm(hot_rows(receiver, receiver, owned), message)

    for copy in copies[2:]:
        copy.wait()
    nodes = nodes_ref[...]
    inbox = agg[...].astype(BF16)
    pre = mm(nodes, w_node_in_ref[:width]) + mm(inbox, w_node_in_ref[width:])
    sigma = sigmoid(pre)
    zed = (pre * sigma).astype(BF16)
    unit, inv_std = normalize(mm(zed, w_node_out_ref[...]))
    upstream = cot_ref[...].astype(F32)
    dy = norm_back(upstream, unit, inv_std).astype(BF16)
    db = (mm_cols(dy, w_node_out_ref[...]) * (sigma * (1.0 + pre * (1.0 - sigma)))).astype(BF16)
    dagg_ref[...] = mm_cols(db, w_node_in_ref[width:]).astype(BF16)
    node_part_ref[...] = upstream + mm_cols(db, w_node_in_ref[:width])
    grads_no[...] = mm_rows(zed, dy)
    grads_ni[:width] = mm_rows(nodes, db)
    grads_ni[width:] = mm_rows(inbox, db)
    put_blocks((grads_no, grads_ni), me_ref[0], count, keep_ref, away_ref)


def backward_kernel(
    recv_ref, zeta_ref, slope_ref, normed_ref, inv_ref, dagg_ref, w_edge_out_ref, dye_ref, da_ref
):
    @pl.loop(0, zeta_ref.shape[0] // BLOCK)
    def _(block):
        rows = pl.ds(pl.multiple_of(block * BLOCK, BLOCK), BLOCK)
        up = mm(one_hot_cols(recv_ref[:, rows], dagg_ref.shape[0]), dagg_ref[...])
        dye = norm_back(up, normed_ref[rows].astype(F32), inv_ref[rows]).astype(BF16)
        dye_ref[rows] = dye
        da_ref[rows] = (mm_cols(dye, w_edge_out_ref[...]) * slope_ref[rows].astype(F32)).astype(BF16)


def weights_kernel(
    count,
    slot,
    me_ref,
    send_ref,
    recv_ref,
    halo_ref,
    nodes_ref,
    edges_ref,
    zeta_ref,
    dye_ref,
    da_ref,
    keep_ref,
    away_ref,
    own_ref,
    recv_sums_ref,
    far_ref,
    sums,
    grads_eo,
    grads_ei,
):
    owned, width = nodes_ref.shape
    n_table = sums.shape[0]
    n_far = count * slot
    me = me_ref[0]
    sums[...] = jnp.zeros_like(sums)

    def block_of(device):
        return cube_place(device ^ me, device & 1, count) * slot

    @pl.loop(0, edges_ref.shape[0] // BLOCK)
    def _(block):
        rows = pl.ds(pl.multiple_of(block * BLOCK, BLOCK), BLOCK)
        sender, safe, receiver = edge_ids(rows, owned, slot, send_ref, recv_ref, block_of)
        sums[...] += mm(hot_rows(sender, safe, n_table), da_ref[rows])

    own = sums[:owned].astype(BF16)
    recv = sums[owned : 2 * owned].astype(BF16)
    far = sums[2 * owned : 2 * owned + n_far].astype(BF16)
    own_ref[...] = own
    recv_sums_ref[...] = recv
    far_ref[...] = far
    away_ref[keep_ref.shape[0] :] = far[n_far // 2 :]
    shape = (n_far, count * HALO_ROWS)
    column = lax.broadcasted_iota(jnp.int32, shape, 1)
    device = column // HALO_ROWS
    there = (column % HALO_ROWS < slot) & (
        block_of(device) + column % HALO_ROWS == lax.broadcasted_iota(jnp.int32, shape, 0)
    )
    halo = mm(jnp.where(there, 1.0, 0.0).astype(BF16), halo_ref[...]).astype(BF16)
    nodes = nodes_ref[...]
    for start in range(0, width, TILE):
        cols = slice(start, start + TILE)
        grads_eo[cols] = mm_rows(zeta_ref[:, cols], dye_ref[...])
        grads_ei[cols] = mm_rows(edges_ref[:, cols], da_ref[...])
    grads_ei[width : 2 * width] = mm_rows(nodes, own) + mm_rows(halo, far)
    grads_ei[2 * width :] = mm_rows(nodes, recv)
    put_blocks((grads_eo, grads_ei), me, count, keep_ref, away_ref)


def ride_kernel(step, count, slot, keep_ref, arrived_ref, far_ref, next_keep_ref, next_away_ref, next_far_ref):
    size, half = keep_ref.shape[0], next_keep_ref.shape[0]
    next_keep_ref[...] = keep_ref[:half] + arrived_ref[:half]
    next_away_ref[:half] = keep_ref[half:] + arrived_ref[half:size]
    far = swap_rows(step, count, slot, far_ref[...], arrived_ref[size:])
    next_far_ref[...] = far
    next_away_ref[half:] = mm(take_rows(step + 1, count, slot), far).astype(BF16)


def swap_rows(step, count, slot, far, arrived):
    take = take_rows(step, count, slot)
    stays = 1.0 - jnp.sum(take.astype(F32), axis=0, keepdims=True)
    rows = far.shape[0]
    square = lax.broadcasted_iota(jnp.int32, (rows, rows), 0) == lax.broadcasted_iota(jnp.int32, (rows, rows), 1)
    stay = jnp.where(square, stays, 0.0).astype(BF16)
    return (mm(stay, far) + mm_rows(take, arrived)).astype(BF16)


def node_kernel(own_ref, recv_ref, part_ref, w_send_ref, w_recv_ref, out_ref):
    out_ref[...] = part_ref[...] + mm_cols(own_ref[...], w_send_ref[...]) + mm_cols(recv_ref[...], w_recv_ref[...])


def last_kernel(
    step, count, slot, keep_ref, arrived_ref, far_ref, pick_ref, node_ref, w_send_ref, first_ref, rest_ref, grad_ref
):
    share, rest = first_ref.shape[0], rest_ref.shape[0]
    size = keep_ref.shape[0]
    far = swap_rows(step, count, slot, far_ref[...], arrived_ref[size:])
    total = keep_ref[...].astype(F32) + arrived_ref[:size].astype(F32)
    first_ref[...] = total[:share]
    rest_ref[...] = total[share : share + rest]
    sums = mm_rows(pick_ref[...], far).astype(BF16)
    grad_ref[...] = (node_ref[...] + mm_cols(sums, w_send_ref[...])).astype(BF16)


def add_kernel(keep_ref, arrived_ref, next_keep_ref, next_send_ref):
    half = next_keep_ref.shape[0]
    next_send_ref[...] = keep_ref[half:] + arrived_ref[half:]
    next_keep_ref[...] = keep_ref[:half] + arrived_ref[:half]


def total_kernel(kept_ref, came_ref, first_ref, rest_ref):
    share = first_ref.shape[0]
    total = kept_ref[...].astype(F32) + came_ref[...].astype(F32)
    first_ref[...] = total[:share]
    rest_ref[...] = total[share : share + rest_ref.shape[0]]


VMEM = pl.BlockSpec(memory_space=pltpu.VMEM)
SMEM = pl.BlockSpec(memory_space=pltpu.SMEM)
HBM = pl.BlockSpec(memory_space=pltpu.HBM)
COST = pl.CostEstimate(flops=1 << 10, bytes_accessed=1 << 10, transcendentals=0)


def kernel_call(kernel, name, outs, scratch, args, near=(), far=(), limit=16):
    specs = [SMEM if arg.shape == (1,) else VMEM for arg in args] + [VMEM] * len(near) + [HBM] * len(far)
    near = [pltpu.with_memory_space_constraint(array, pltpu.VMEM) for array in near]
    far = [pltpu.with_memory_space_constraint(array, pltpu.HBM) for array in far]
    return pl.pallas_call(
        kernel,
        out_shape=tuple(outs),
        in_specs=specs,
        out_specs=(VMEM,) * len(outs),
        scratch_shapes=scratch,
        compiler_params=pltpu.CompilerParams(vmem_limit_bytes=limit << 20),
        cost_estimate=COST,
        name=name,
    )(*args, *near, *far)


def in_order(first, then):
    return lax.optimization_barrier((first, then))


def trade(rows):
    return lax.all_to_all(rows, "patch", split_axis=0, concat_axis=0, tiled=True)


def body(
    count,
    nodes,
    edges,
    cot_nodes,
    w_edge_in,
    w_edge_out,
    w_node_in,
    w_node_out,
    send_rows,
    edge_sender,
    edge_receiver,
):
    owned, width = nodes.shape
    n_edges = edges.shape[0]
    slot = send_rows.shape[2]
    share = width // count
    n_halo = count * HALO_ROWS
    me = lax.axis_index("patch").astype(jnp.int32).reshape(1)
    sender = edge_sender.reshape(1, -1)
    receiver = edge_receiver.reshape(1, -1)

    def space(*shape, dtype=BF16):
        return pltpu.VMEM(shape, dtype)

    def block_pair(rows, riders=0):
        size = count // 2 * (-(-(rows * share) // 16) * 16)
        return [space(size, width), space(size + riders, width)]

    n_far = count * slot
    pick, halo_out = kernel_call(
        functools.partial(pick_kernel, count),
        "pick",
        [jax.ShapeDtypeStruct((n_far, owned), BF16), jax.ShapeDtypeStruct((n_halo, width), BF16)],
        [],
        (me, send_rows[0].T, nodes),
        limit=60,
    )
    halo = trade(halo_out)
    base = pl.pallas_call(
        local_kernel,
        out_shape=jax.ShapeDtypeStruct((n_edges, width), F32),
        grid=(n_edges // GRID_BLOCK,),
        in_specs=[
            pl.BlockSpec((1, GRID_BLOCK), lambda i: (0, i)),
            pl.BlockSpec((1, GRID_BLOCK), lambda i: (0, i)),
            pl.BlockSpec((owned, width), lambda i: (0, 0)),
            pl.BlockSpec((3 * width, width), lambda i: (0, 0)),
            pl.BlockSpec((GRID_BLOCK, width), lambda i: (i, 0)),
        ],
        out_specs=pl.BlockSpec((GRID_BLOCK, width), lambda i: (i, 0)),
        scratch_shapes=[space(2 * owned, width)],
        compiler_params=pltpu.CompilerParams(vmem_limit_bytes=60 << 20),
        cost_estimate=COST,
        name="local",
    )(sender, receiver, nodes, w_edge_in, edges)
    rows, square = space(n_edges, width), space(width, width)
    keep1, away1, zeta, slope, normed, inv, dagg, node_part, near_nodes, near_out, near_edges, w_send, w_recv = kernel_call(
        functools.partial(forward_kernel, count, slot),
        "forward",
        block_pair(3)
        + [rows, rows, rows, space(n_edges, 1, dtype=F32)]
        + [space(owned, width), space(owned, width, dtype=F32), space(owned, width), square, rows, square, square],
        [space(n_edges, width, dtype=F32), space(2 * width, width), square, space(owned, width)]
        + [space(n_halo, width)]
        + [space(r, width, dtype=F32) for r in (owned, width, 2 * width)]
        + [pltpu.SemaphoreType.DMA((n_edges // BLOCK,)), pltpu.SemaphoreType.DMA((8,))],
        (me, sender, receiver, halo),
        far=(w_edge_in, base, w_edge_out, nodes, w_node_in, w_node_out, cot_nodes, edges),
        limit=36,
    )

    def add(keep, arrived):
        half = [space(keep.shape[0] // 2, width)] * 2
        return kernel_call(add_kernel, "add", half, [], (keep, arrived), limit=8)

    def ride(step, keep, arrived, far):
        half = keep.shape[0] // 2
        outs = [space(half, width), space(half + n_far // 2, width), space(n_far, width)]
        kernel = functools.partial(ride_kernel, step, count, slot)
        return kernel_call(kernel, "ride", outs, [], (keep, arrived, far), limit=8)

    came1 = cube_permute(away1, 0, count)
    dye, da = kernel_call(
        backward_kernel, "backward", [rows, rows], [], (receiver,), (zeta, slope, normed, inv, dagg, near_out)
    )
    came1, dye = in_order(came1, dye)
    keep1, away1 = add(keep1, came1)
    away1, da = in_order(away1, da)
    came1 = cube_permute(away1, 1, count)
    keep2, away2, own_sums, recv_sums, far_sums = kernel_call(
        functools.partial(weights_kernel, count, slot),
        "weights",
        block_pair(4, n_far // 2) + [space(owned, width), space(owned, width), space(n_far, width)],
        [space(r, width, dtype=F32) for r in (2 * owned + -(-n_far // LANES) * LANES, width, 3 * width)],
        (me, sender, receiver, halo),
        (near_nodes, near_edges, zeta, dye, da),
    )
    keep1, away1 = add(keep1, came1)
    away1, away2 = in_order(away1, away2)
    came1 = cube_permute(away1, 2, count)
    came2 = cube_permute(away2, 0, count)
    keep2, away2, far_sums = ride(0, keep2, came2, far_sums)
    came2 = cube_permute(away2, 1, count)
    steps = count.bit_length() - 1
    for step in range(3, steps):
        keep1, away1 = add(keep1, came1)
        came1 = cube_permute(away1, step, count)
    _, da = in_order(away1, da)
    edge_grad = mm_cols(da, w_edge_in[:width]).astype(BF16)
    edge_grad, came2 = in_order(edge_grad, came2)
    for step in range(2, steps):
        keep2, away2, far_sums = ride(step - 1, keep2, came2, far_sums)
        came2 = cube_permute(away2, step, count)
    away2, own_sums = in_order(away2, own_sums)
    node_sum = kernel_call(
        node_kernel, "node", [space(owned, width, dtype=F32)], [], (own_sums, recv_sums, node_part, w_send, w_recv)
    )[0]

    def whole(*parts):
        return [jax.ShapeDtypeStruct((part * share, width), F32) for part in parts]

    node_out, node_in = kernel_call(total_kernel, "node_total", whole(1, 2), [], (keep1, came1), limit=8)
    node_out, came2 = in_order(node_out, came2)
    edge_out, edge_in, node_grad = kernel_call(
        functools.partial(last_kernel, steps - 1, count, slot),
        "last",
        whole(1, 3) + [jax.ShapeDtypeStruct((owned, width), BF16)],
        [],
        (keep2, came2, far_sums, pick, node_sum, w_send),
        limit=8,
    )
    return node_grad, edge_grad, edge_in, edge_out, node_in, node_out


def solution(mesh):
    rows = P(("groups", "patch"), None)
    flat = P(("groups", "patch"))
    return jax.shard_map(
        functools.partial(body, mesh.shape["patch"]),
        mesh=mesh,
        in_specs=(rows, rows, rows, P(), P(), P(), P(), P(("groups", "patch"), None, None), flat, flat),
        out_specs=(rows,) * 6,
        check_vma=False,
    )
```

time: 320 us -> 77 us (0.24)
  waiting for transfers between devices: 203 us -> 27.9 us
  matrix products: 49.4 us -> 3.65 us
  Pallas kernels: 0 us -> 30 us
  local copies, waits for them, and re-layouts: 27.8 us -> 0.02 us
  between operations: 14.2 us -> 0.76 us
  other arithmetic: 11.3 us -> 0 us
    reduce_scatter x4 -> x0, waiting for transfers between devices: 201 us -> none  [the longest x1 69.9 us: edge_in_sum(): return lax.psum_scatter(stacked, 'patch', scatter_dimension=0, tiled=True)]
    dot_general x23 -> x1, matrix products: 49.4 us -> 3.65 us  [mm_cols(): lax.dot_general(left, right, (((1,), (1,)), ((), ())), preferred_element_...]
    pallas_call x0 -> x14, Pallas kernels: none -> 30 us  [the longest x13 23.7 us: kernel_call(): pl.pallas_call(kernel, out_shape=tuple(outs), in_specs=specs, out_specs=(...]
    ppermute x0 -> x8, waiting for transfers between devices: none -> 26.3 us  [cube_permute(): return lax.ppermute(blocks, 'patch', pairs)]
    gather x4 -> x0, local copies, waits for them, and re-layouts: 19.7 us -> none  [the longest x1 9.2 us: body(): proj_recv[safe_recv].astype(jnp.float32)]
    unnamed x57 -> x6, local copies, waits for them, and re-layouts: 7.08 us -> 0.02 us
    ppermute x0 -> x8, starting transfers between devices: none -> 7.04 us  [cube_permute(): return lax.ppermute(blocks, 'patch', pairs)]
    all_to_all x1 -> x0, starting transfers between devices: 6.02 us -> none  [give_back(): lax.all_to_all(rows.astype(jnp.bfloat16), 'patch', split_axis=0, concat_a...]
  transfers between devices with their start and end apart: 6 -> 9, of which waited for: 5 -> 6; matrix products, arithmetic and copies ran while one was open for 17% -> 5% of each run, Pallas kernels for 0% -> 21%
where the time goes in v2:
time: 77 us; the launch traced here: 76.7 us
  Pallas kernels  30 us (39%)
  waiting for transfers between devices  27.9 us (36%)
  starting transfers between devices  14.4 us (19%)
  matrix products  3.65 us (5%)
    ppermute x8, waiting for transfers between devices, cube_permute(): return lax.ppermute(blocks, 'patch', pairs)  26.3 us
    pallas_call x13, Pallas kernels, kernel_call(): pl.pallas_call(kernel, out_shape=tuple(outs), in_specs=specs, out_specs=(...  23.7 us
    all_to_all x1, starting transfers between devices, trade(): lax.all_to_all(rows, 'patch', split_axis=0, concat_axis=0, tiled=True)  7.39 us
    ppermute x8, starting transfers between devices, cube_permute(): return lax.ppermute(blocks, 'patch', pairs)  7.04 us
    pallas_call x1, Pallas kernels, body(): pl.pallas_call(local_kernel, out_shape=jax.ShapeDtypeStruct((n_edges, wid...  6.27 us
    dot_general x1, matrix products, mm_cols(): lax.dot_general(left, right, (((1,), (1,)), ((), ())), preferred_element_...  3.65 us
    all_to_all x1, waiting for transfers between devices, trade(): lax.all_to_all(rows, 'patch', split_axis=0, concat_axis=0, tiled=True)  1.64 us
  transfers between devices with their start and end apart: 9, of which 6 were waited for; matrix products, arithmetic and copies ran while one was open for 5% of the time, Pallas kernels for 21%

profile of v2, /device:TPU:0, one launch (start us, length us, event | category | flops | bytes accessed | tf_op | source)
XLA Modules:
  0.0 76.7 jit_solution(12478732780141712193)
XLA Ops:
  0.6 1.9 %pick.1 = (bf16[64,256]{1,0:T(8,128)(2,1)}, bf16[128,512]{1,0:T(8,128)(2,1)}) custom-call(s32[1]{0:T(128)} %bitcast.me_ref, s32[4,16]{1,0:T(4,128)} %bitcast.19, bf16[256,512]{1,0:T(8,128)(2,1)} %nodes_far.1), custom_call_target="tpu_custom_call" | custom-call | flops 1024 | bytes 1024 | tf_op jit(solution)/shard_map/pick/pallas_call | solution.py:415
  2.5 7.4 %all-to-all-start = ((bf16[16,8,512]{2,1,0:T(8,128)(2,1)}), bf16[16,8,512]{2,1,0:T(8,128)(2,1)S(1)}, u32[]{:S(2)}, u32[]{:S(2)}) async-start(bf16[16,8,512]{2,1,0:T(8,128)(2,1)} %bitcast.18), calls=%async_computation | async-start | bytes 262144 | tf_op jit(solution)/shard_map/all_to_all | solution.py:432
  9.9 0.0 copy-start
  9.9 0.0 copy-start.1
  9.9 6.3 %local.1.base_far = f32[2048,512]{1,0:T(8,128)} custom-call(s32[1,2048]{1,0:T(1,128)} %bitcast.15, s32[1,2048]{1,0:T(1,128)} %bitcast.11, bf16[256,512]{1,0:T(8,128)(2,1)} %nodes_far.1, bf16[1536,512]{1,0:T(8,128)(2,1)} %w_edge_in_far.1, bf16[2048,512]{1,0:T(8,128)(2,1)} %edges_far.1), custom_call_target="tpu_custom_call" | custom-call | flops 1024 | bytes 1024 | tf_op jit(solution)/shard_map/local/pallas_call | solution.py:474
  16.2 1.6 %all-to-all-done = bf16[16,8,512]{2,1,0:T(8,128)(2,1)S(1)} async-done(((bf16[16,8,512]{2,1,0:T(8,128)(2,1)}), bf16[16,8,512]{2,1,0:T(8,128)(2,1)S(1)}, u32[]{:S(2)}, u32[]{:S(2)}) %all-to-all-start) | async-done | bytes 131104 | tf_op jit(solution)/shard_map/all_to_all | solution.py:432
  17.8 0.0 copy-done
  17.8 0.0 copy-done.1
  17.8 9.6 %forward.1 = (bf16[768,512]{1,0:T(8,128)(2,1)S(1)}, bf16[768,512]{1,0:T(8,128)(2,1)S(1)}, bf16[2048,512]{1,0:T(8,128)(2,1)S(1)}, bf16[2048,512]{1,0:T(8,128)(2,1...) custom-call(s32[1]{0:T(128)} %bitcast.me_ref, ...), custom_call_target="tpu_custom_call" | custom-call | flops 1024 | bytes 1024 | tf_op jit(solution)/shard_map/forward/pallas_call | solution.py:415
  27.4 0.1 collective-permute-start
  27.5 3.2 %backward.1 = (bf16[2048,512]{1,0:T(8,128)(2,1)S(1)}, bf16[2048,512]{1,0:T(8,128)(2,1)S(1)}) custom-call(s32[1,2048]{1,0:T(1,128)S(1)} %bitcast.13, bf16[2048,512]{1,0:T(8,128)(2,1)S(1)} %get-tuple-element.63.zeta_ref, bf16[2048,512]{1,0:T(8,128)(2,1)S(1)} %get-tuple-element.65.slope_ref, bf16[2048,512]{1,0:T(8,128)(2,1)S(1)} %get-tuple-element.66.normed_ref, ...), custom_call_target="tpu_custom_call" | custom-call | flops 1024 | bytes 1024 | tf_op jit(solution)/shard_map/backward/pallas_call | solution.py:415
  30.7 0.0 collective-permute-done.arrived_ref
  30.7 0.1 add.3
  30.8 0.5 collective-permute-start.1
  31.3 5.3 %weights.1 = (bf16[1024,512]{1,0:T(8,128)(2,1)S(1)}, bf16[1056,512]{1,0:T(8,128)(2,1)S(1)}, bf16[256,512]{1,0:T(8,128)(2,1)S(1)}, bf16[256,512]{1,0:T(8,128)(2,1)S(1)}, bf16[64,512]{1,0:T(8,128)(2,1)S(1)}) custom-call(s32[1]{0:T(128)} %bitcast.me_ref, s32[1,2048]{1,0:T(1,128)S(1)} %bitcast.17, s32[1,2048]{1,0:T(1,128)S(1)} %bitcast.14, ...), custom_call_target="tpu_custom_call" | custom-call | flops 1024 | bytes 1024 | tf_op jit(solution)/shard_map/weights/pallas_call | solution.py:415
  36.6 2.0 %collective-permute-done.1.arrived_ref = bf16[384,512]{1,0:T(8,128)(2,1)S(1)} collective-permute-done((bf16[384,512]{1,0:T(8,128)(2,1)S(1)}, bf16[384,512]{1,0:T(8,128)(2,1)S(1)}, u32[]{:S(2)}, u32[]{:S(2)}) %collective-permute-start.1) | collective-permute-done | bytes 393248 | tf_op jit(solution)/shard_map/ppermute | solution.py:69
  38.7 0.1 add.4
  38.7 0.1 collective-permute-start.2
  38.8 2.7 %collective-permute-done.2.arrived_ref = bf16[1056,512]{1,0:T(8,128)(2,1)S(1)} collective-permute-done((bf16[1056,512]{1,0:T(8,128)(2,1)S(1)}, bf16[1056,512]{1,0:T(8,128)(2,1)S(1)}, u32[]{:S(2)}, u32[]{:S(2)}) %collective-permute-start.2) | collective-permute-done | bytes 1081376 | tf_op jit(solution)/shard_map/ppermute | solution.py:69
  41.5 0.4 ride.3
  41.9 0.5 collective-permute-start.4
  42.4 1.5 %collective-permute-start.3 = (bf16[192,512]{1,0:T(8,128)(2,1)S(1)}, bf16[192,512]{1,0:T(8,128)(2,1)S(1)}, u32[]{:S(2)}, u32[]{:S(2)}) collective-permute-start(bf16[192,512]{1,0:T(8,128)(2,1)S(1)} %get-tuple-element.86), channel_id=1, source_target_pairs={{0,4},{1,3},{2,6},{3,1},{4,0},{5,7},{6,2},{7,5},{8,12},{9,11},{10,... | collective-permute-start | bytes 589832 | tf_op jit(solution)/shard_map/ppermute | solution.py:69
  43.8 6.4 %collective-permute-done.3.arrived_ref = bf16[192,512]{1,0:T(8,128)(2,1)S(1)} collective-permute-done((bf16[192,512]{1,0:T(8,128)(2,1)S(1)}, bf16[192,512]{1,0:T(8,128)(2,1)S(1)}, u32[]{:S(2)}, u32[]{:S(2)}) %collective-permute-start.3) | collective-permute-done | bytes 196640 | tf_op jit(solution)/shard_map/ppermute | solution.py:69
  50.2 3.6 %convolution_convert_fusion = bf16[2048,512]{1,0:T(8,128)(2,1)} fusion(bf16[2048,512]{1,0:T(8,128)(2,1)S(1)} %get-tuple-element.88.da_ref, bf16[1536,512]{1,0:T(8,128)(2,1)} %w_edge_in_far.1), kind=kOutput, calls=%fused_computation | convolution fusion | flops 1074790400 | bytes 4718592 | tf_op jit(solution)/shard_map/dot_general | solution.py:29
  53.9 0.0 collective-permute-done.4.arrived_ref
  53.9 0.0 copy-start.2
  53.9 0.3 ride.4
  54.2 1.5 %collective-permute-start.5 = (bf16[288,512]{1,0:T(8,128)(2,1)S(1)}, bf16[288,512]{1,0:T(8,128)(2,1)S(1)}, u32[]{:S(2)}, u32[]{:S(2)}) collective-permute-start(bf16[288,512]{1,0:T(8,128)(2,1)S(1)} %get-tuple-element.93), channel_id=1, source_target_pairs={{0,4},{1,3},{2,6},{3,1},{4,0},{5,7},{6,2},{7,5},{8,12},{9,11},{10,... | collective-permute-start | bytes 884744 | tf_op jit(solution)/shard_map/ppermute | solution.py:69
  55.7 5.2 %collective-permute-done.5.arrived_ref = bf16[288,512]{1,0:T(8,128)(2,1)S(1)} collective-permute-done((bf16[288,512]{1,0:T(8,128)(2,1)S(1)}, bf16[288,512]{1,0:T(8,128)(2,1)S(1)}, u32[]{:S(2)}, u32[]{:S(2)}) %collective-permute-start.5) | collective-permute-done | bytes 294944 | tf_op jit(solution)/shard_map/ppermute | solution.py:69
  61.0 0.3 ride.5
  61.3 2.4 %collective-permute-start.7 = (bf16[160,512]{1,0:T(8,128)(2,1)S(1)}, bf16[160,512]{1,0:T(8,128)(2,1)S(1)}, u32[]{:S(2)}, u32[]{:S(2)}) collective-permute-start(bf16[160,512]{1,0:T(8,128)(2,1)S(1)} %get-tuple-element.98), channel_id=1, source_target_pairs={{0,8},{1,9},{2,10},{3,11},{4,12},{5,13},{6,14},{7,15},{8,0},{9,1},... | collective-permute-start | bytes 491528 | tf_op jit(solution)/shard_map/ppermute | solution.py:69
  63.7 0.5 collective-permute-start.6
  64.2 9.9 %collective-permute-done.6.came_ref = bf16[96,512]{1,0:T(8,128)(2,1)S(1)} collective-permute-done((bf16[96,512]{1,0:T(8,128)(2,1)S(1)}, bf16[96,512]{1,0:T(8,128)(2,1)S(1)}, u32[]{:S(2)}, u32[]{:S(2)}) %collective-permute-start.6) | collective-permute-done | bytes 98336 | tf_op jit(solution)/shard_map/ppermute | solution.py:69
  74.2 0.7 node_total.1
  74.8 0.5 node.1.node_ref
  75.3 0.0 collective-permute-done.7.arrived_ref
  75.3 0.0 copy-done.2
  75.3 1.4 %last.1 = (f32[32,512]{1,0:T(8,128)}, f32[96,512]{1,0:T(8,128)}, bf16[256,512]{1,0:T(8,128)(2,1)}) custom-call(bf16[128,512]{1,0:T(8,128)(2,1)S(1)} %get-tuple-element.95.keep_ref, bf16[160,512]{1,0:T(8,128)(2,1)S(1)} %collective-permute-done.7.arrived_ref, bf16[64,512]{1,0:T(8,128)(2,1)S(1)} %get-tuple-element.100.far_ref, bf16[64,256]{1,0:T(8,128)(2,1)S(1)} %copy-done.2, ...), custom_call_target="tpu_custom_call" | custom-call | flops 1024 | bytes 1024 | tf_op jit(solution)/shard_map/last/pallas_call | solution.py:415
  (1 shorter events, 0.0 us)
Async XLA Ops:
  2.5 15.3 %all-to-all-start = ((bf16[16,8,512]{2,1,0:T(8,128)(2,1)}), bf16[16,8,512]{2,1,0:T(8,128)(2,1)S(1)}, u32[]{:S(2)}, u32[]{:S(2)}) async-start(bf16[16,8,512]{2,1,0:T(8,128)(2,1)} %bitcast.18), calls=%async_computation | async-start | bytes 262144 | tf_op jit(solution)/shard_map/all_to_all | solution.py:432
  9.9 7.9 %copy-start = (s32[2048]{0:T(1024)S(1)}, s32[2048]{0:T(1024)}, u32[]{:S(2)}) copy-start(s32[2048]{0:T(1024)} %param.19) | copy-start | bytes 24580
  9.9 7.9 %copy-start.1 = (s32[2048]{0:T(1024)S(1)}, s32[2048]{0:T(1024)}, u32[]{:S(2)}) copy-start(s32[2048]{0:T(1024)} %param.18) | copy-start | bytes 24580
  27.4 3.3 %collective-permute-start = (bf16[768,512]{1,0:T(8,128)(2,1)S(1)}, bf16[768,512]{1,0:T(8,128)(2,1)S(1)}, u32[]{:S(2)}, u32[]{:S(2)}) collective-permute-start(bf16[768,512]{1,0:T(8,128)(2,1)S(1)} %get-tuple-element.64), channel_id=1, source_target_pairs={{0,1},{1,0},{2,3},{3,2},{4,5},{5,4},{6,7},{7,6},{8,9},{9,8},{10,11... | collective-permute-start | bytes 2359304 | tf_op jit(solution)/shard_map/ppermute | solution.py:69
  30.8 7.8 %collective-permute-start.1 = (bf16[384,512]{1,0:T(8,128)(2,1)S(1)}, bf16[384,512]{1,0:T(8,128)(2,1)S(1)}, u32[]{:S(2)}, u32[]{:S(2)}) collective-permute-start(bf16[384,512]{1,0:T(8,128)(2,1)S(1)} %get-tuple-element.79), channel_id=1, source_target_pairs={{0,2},{1,5},{2,0},{3,7},{4,6},{5,1},{6,4},{7,3},{8,10},{9,13},{10,... | collective-permute-start | bytes 1179656 | tf_op jit(solution)/shard_map/ppermute | solution.py:69
  38.7 2.8 %collective-permute-start.2 = (bf16[1056,512]{1,0:T(8,128)(2,1)S(1)}, bf16[1056,512]{1,0:T(8,128)(2,1)S(1)}, u32[]{:S(2)}, u32[]{:S(2)}) collective-permute-start(bf16[1056,512]{1,0:T(8,128)(2,1)S(1)} %get-tuple-element.82), channel_id=1, source_target_pairs={{0,1},{1,0},{2,3},{3,2},{4,5},{5,4},{6,7},{7,6},{8,9},{9,8},{10,11... | collective-permute-start | bytes 3244040 | tf_op jit(solution)/shard_map/ppermute | solution.py:69
  41.9 12.0 %collective-permute-start.4 = (bf16[544,512]{1,0:T(8,128)(2,1)S(1)}, bf16[544,512]{1,0:T(8,128)(2,1)S(1)}, u32[]{:S(2)}, u32[]{:S(2)}) collective-permute-start(bf16[544,512]{1,0:T(8,128)(2,1)S(1)} %get-tuple-element.89), channel_id=1, source_target_pairs={{0,2},{1,5},{2,0},{3,7},{4,6},{5,1},{6,4},{7,3},{8,10},{9,13},{10,... | collective-permute-start | bytes 1671176 | tf_op jit(solution)/shard_map/ppermute | solution.py:69
  42.4 7.8 %collective-permute-start.3 = (bf16[192,512]{1,0:T(8,128)(2,1)S(1)}, bf16[192,512]{1,0:T(8,128)(2,1)S(1)}, u32[]{:S(2)}, u32[]{:S(2)}) collective-permute-start(bf16[192,512]{1,0:T(8,128)(2,1)S(1)} %get-tuple-element.86), channel_id=1, source_target_pairs={{0,4},{1,3},{2,6},{3,1},{4,0},{5,7},{6,2},{7,5},{8,12},{9,11},{10,... | collective-permute-start | bytes 589832 | tf_op jit(solution)/shard_map/ppermute | solution.py:69
  53.9 21.5 %copy-start.2 = (bf16[64,256]{1,0:T(8,128)(2,1)S(1)}, bf16[64,256]{1,0:T(8,128)(2,1)}, u32[]{:S(2)}) copy-start(bf16[64,256]{1,0:T(8,128)(2,1)} %get-tuple-element.101.pick_ref) | copy-start | bytes 98308
  54.2 6.7 %collective-permute-start.5 = (bf16[288,512]{1,0:T(8,128)(2,1)S(1)}, bf16[288,512]{1,0:T(8,128)(2,1)S(1)}, u32[]{:S(2)}, u32[]{:S(2)}) collective-permute-start(bf16[288,512]{1,0:T(8,128)(2,1)S(1)} %get-tuple-element.93), channel_id=1, source_target_pairs={{0,4},{1,3},{2,6},{3,1},{4,0},{5,7},{6,2},{7,5},{8,12},{9,11},{10,... | collective-permute-start | bytes 884744 | tf_op jit(solution)/shard_map/ppermute | solution.py:69
  61.3 14.0 %collective-permute-start.7 = (bf16[160,512]{1,0:T(8,128)(2,1)S(1)}, bf16[160,512]{1,0:T(8,128)(2,1)S(1)}, u32[]{:S(2)}, u32[]{:S(2)}) collective-permute-start(bf16[160,512]{1,0:T(8,128)(2,1)S(1)} %get-tuple-element.98), channel_id=1, source_target_pairs={{0,8},{1,9},{2,10},{3,11},{4,12},{5,13},{6,14},{7,15},{8,0},{9,1},... | collective-permute-start | bytes 491528 | tf_op jit(solution)/shard_map/ppermute | solution.py:69
  63.7 10.5 %collective-permute-start.6 = (bf16[96,512]{1,0:T(8,128)(2,1)S(1)}, bf16[96,512]{1,0:T(8,128)(2,1)S(1)}, u32[]{:S(2)}, u32[]{:S(2)}) collective-permute-start(bf16[96,512]{1,0:T(8,128)(2,1)S(1)} %get-tuple-element.87), channel_id=1, source_target_pairs={{0,8},{1,9},{2,10},{3,11},{4,12},{5,13},{6,14},{7,15},{8,0},{9,1},... | collective-permute-start | bytes 294920 | tf_op jit(solution)/shard_map/ppermute | solution.py:69

commit v3 on v2

--- a/solution.py
+++ b/solution.py
@@ -14,7 +14,6 @@
 BLOCK = 1024
 TILE = 256
 HALO_ROWS = 8
-GRID_BLOCK = 1024
 
 
 def mm(left, right):
@@ -116,30 +115,26 @@
     half = count // 2
     size = keep_ref.shape[0] // half
     spare = size - sum(shares)
-
-    @pl.loop(0, count)
-    def _(target):
+    bits = count.bit_length() - 1
+    for place in range(count):
+        apart = [
+            sum(((place >> (bits - 1 - j)) & 1) << dim for j, dim in enumerate(order)) for order in cube_orders(count)
+        ]
+        odd_target = (me ^ (place // half)) & 1
+        target = me ^ jnp.where(odd_target == 0, *apart)
         parts = [
             source[pl.ds(pl.multiple_of(target * share, share), share)] for source, share in zip(sources, shares)
         ]
         if spare:
             parts.append(jnp.zeros((spare, keep_ref.shape[1]), F32))
-        block = jnp.concatenate(parts, axis=0).astype(BF16)
-        place = cube_place(target ^ me, target & 1, count)
-
-        @pl.when(place < half)
-        def _():
-            keep_ref[pl.ds(pl.multiple_of(place * size, size), size)] = block
-
-        @pl.when(place >= half)
-        def _():
-            send_ref[pl.ds(pl.multiple_of((place - half) * size, size), size)] = block
-
-
-def pick_kernel(count, me_ref, picks_ref, nodes_ref, pick_ref, rows_ref):
+        start = place % half * size
+        (keep_ref if place < half else send_ref)[start : start + size] = jnp.concatenate(parts, axis=0).astype(BF16)
+
+
+def pick_kernel(count, picks_ref, nodes_ref, pick_ref, rows_ref):
     slot = picks_ref.shape[0]
     owned = nodes_ref.shape[0]
-    me = me_ref[0]
+    me = lax.axis_index("patch")
 
     def choose(rows, start):
         shape = (rows, count)
@@ -156,36 +151,46 @@
     pick_ref[...] = choose(count * slot, lambda device: cube_place(device ^ me, me & 1, count) * slot)
 
 
-def local_kernel(send_ref, recv_ref, nodes_ref, w_edge_in_ref, edges_ref, base_ref, table):
+def local_kernel(
+    nodes_far, w_edge_in_far, w_edge_out_far, nodes_ref, w_send, w_self, w_edge_out_ref, table, w_recv, sems
+):
     owned, width = nodes_ref.shape
-
-    @pl.when(pl.program_id(0) == 0)
-    def _():
-        nodes = nodes_ref[...]
-        table[:owned] = mm(nodes, w_edge_in_ref[width : 2 * width]).astype(BF16)
-        table[owned:] = mm(nodes, w_edge_in_ref[2 * width :]).astype(BF16)
-
-    sender = send_ref[...]
-    sender = jnp.where(sender < owned, sender, -1)
-    hot = hot_cols(sender, jnp.maximum(recv_ref[...], 0) + owned, 2 * owned)
-    base_ref[...] = mm(edges_ref[...], w_edge_in_ref[:width]) + mm(hot, table[...])
+    pairs = (
+        (nodes_far, nodes_ref),
+        (w_edge_in_far.at[width : 2 * width], w_send),
+        (w_edge_in_far.at[2 * width :], w_recv),
+        (w_edge_in_far.at[:width], w_self),
+        (w_edge_out_far, w_edge_out_ref),
+    )
+    copies = [pltpu.make_async_copy(src, dst, sems.at[i]) for i, (src, dst) in enumerate(pairs)]
+    for copy in copies:
+        copy.start()
+    copies[0].wait()
+    nodes = nodes_ref[...]
+    copies[1].wait()
+    table[:owned] = mm(nodes, w_send[...]).astype(BF16)
+    copies[2].wait()
+    table[owned:] = mm(nodes, w_recv[...]).astype(BF16)
+    for copy in copies[3:]:
+        copy.wait()
 
 
 def forward_kernel(
     count,
     slot,
-    me_ref,
-    send_ref,
-    recv_ref,
     halo_ref,
-    w_edge_in_far,
-    base_far,
-    w_edge_out_far,
-    nodes_far,
+    nodes_ref,
+    w_send,
+    w_self,
+    w_edge_out_ref,
+    own_table,
+    edges_far,
+    send_far,
+    recv_far,
     w_node_in_far,
     w_node_out_far,
     cot_far,
-    edges_far,
+    w_edge_in_far,
     keep_ref,
     away_ref,
     zeta_ref,
@@ -194,12 +199,10 @@
     inv_ref,
     dagg_ref,
     node_part_ref,
-    nodes_ref,
-    w_edge_out_ref,
     edges_ref,
-    w_send,
     w_recv,
-    base,
+    send_ref,
+    recv_ref,
     w_node_in_ref,
     w_node_out_ref,
     cot_ref,
@@ -207,52 +210,51 @@
     agg,
     grads_no,
     grads_ni,
-    base_sems,
+    edge_sems,
     sems,
 ):
     owned, width = nodes_ref.shape
     n_table = table.shape[0]
-    n_blocks = base.shape[0] // BLOCK
+    n_blocks = edges_ref.shape[0] // BLOCK
 
     def block_rows(block):
         return pl.ds(pl.multiple_of(block * BLOCK, BLOCK), BLOCK)
 
-    def base_copy(block):
+    def edge_copy(block):
         rows = block_rows(block)
-        return pltpu.make_async_copy(base_far.at[rows], base.at[rows], base_sems.at[block])
+        return pltpu.make_async_copy(edges_far.at[rows], edges_ref.at[rows], edge_sems.at[block])
 
     pairs = (
-        (w_edge_in_far.at[width : 2 * width], w_send),
-        (w_edge_out_far, w_edge_out_ref),
-        (nodes_far, nodes_ref),
+        (send_far, send_ref),
+        (recv_far, recv_ref),
         (w_node_in_far, w_node_in_ref),
         (w_node_out_far, w_node_out_ref),
         (cot_far, cot_ref),
-        (edges_far, edges_ref),
         (w_edge_in_far.at[2 * width :], w_recv),
     )
     copies = [pltpu.make_async_copy(src, dst, sems.at[i]) for i, (src, dst) in enumerate(pairs)]
-    copies[0].start()
-    base_copy(0).start()
-    copies[1].start()
-
-    @pl.loop(1, n_blocks)
+    for copy in copies[:2]:
+        copy.start()
+
+    @pl.loop(0, n_blocks)
     def _(block):
-        base_copy(block).start()
+        edge_copy(block).start()
 
     for copy in copies[2:]:
         copy.start()
     agg[...] = jnp.zeros_like(agg)
-    copies[0].wait()
-    table[...] = mm(halo_ref[...], w_send[...]).astype(BF16)
-    copies[1].wait()
+    nodes = nodes_ref[...]
+    table[: 2 * owned] = own_table[...]
+    table[2 * owned :] = mm(halo_ref[...], w_send[...]).astype(BF16)
+    for copy in copies[:2]:
+        copy.wait()
 
     @pl.loop(0, n_blocks)
     def _(block):
         rows = block_rows(block)
-        base_copy(block).wait()
-        sender, _, receiver = edge_ids(rows, owned, slot, send_ref, recv_ref, lambda device: device * HALO_ROWS)
-        pre = base[rows] + mm(one_hot_cols(sender - 2 * owned, n_table), table[...])
+        edge_copy(block).wait()
+        sender, safe, receiver = edge_ids(rows, owned, slot, send_ref, recv_ref, lambda device: device * HALO_ROWS)
+        pre = mm(edges_ref[rows], w_self[...]) + mm(hot_cols(sender, safe, n_table), table[...])
         sigma = sigmoid(pre)
         zed = (pre * sigma).astype(BF16)
         zeta_ref[rows] = zed
@@ -265,7 +267,6 @@
 
     for copy in copies[2:]:
         copy.wait()
-    nodes = nodes_ref[...]
     inbox = agg[...].astype(BF16)
     pre = mm(nodes, w_node_in_ref[:width]) + mm(inbox, w_node_in_ref[width:])
     sigma = sigmoid(pre)
@@ -279,7 +280,7 @@
     grads_no[...] = mm_rows(zed, dy)
     grads_ni[:width] = mm_rows(nodes, db)
     grads_ni[width:] = mm_rows(inbox, db)
-    put_blocks((grads_no, grads_ni), me_ref[0], count, keep_ref, away_ref)
+    put_blocks((grads_no, grads_ni), lax.axis_index("patch"), count, keep_ref, away_ref)
 
 
 def backward_kernel(
@@ -297,10 +298,9 @@
 def weights_kernel(
     count,
     slot,
-    me_ref,
+    halo_ref,
     send_ref,
     recv_ref,
-    halo_ref,
     nodes_ref,
     edges_ref,
     zeta_ref,
@@ -318,17 +318,13 @@
     owned, width = nodes_ref.shape
     n_table = sums.shape[0]
     n_far = count * slot
-    me = me_ref[0]
-    sums[...] = jnp.zeros_like(sums)
+    me = lax.axis_index("patch")
 
     def block_of(device):
         return cube_place(device ^ me, device & 1, count) * slot
 
-    @pl.loop(0, edges_ref.shape[0] // BLOCK)
-    def _(block):
-        rows = pl.ds(pl.multiple_of(block * BLOCK, BLOCK), BLOCK)
-        sender, safe, receiver = edge_ids(rows, owned, slot, send_ref, recv_ref, block_of)
-        sums[...] += mm(hot_rows(sender, safe, n_table), da_ref[rows])
+    sender, safe, _ = edge_ids(slice(None), owned, slot, send_ref, recv_ref, block_of)
+    sums[...] = mm(hot_rows(sender, safe, n_table), da_ref[...])
 
     own = sums[:owned].astype(BF16)
     recv = sums[owned : 2 * owned].astype(BF16)
@@ -385,8 +381,8 @@
     total = keep_ref[...].astype(F32) + arrived_ref[:size].astype(F32)
     first_ref[...] = total[:share]
     rest_ref[...] = total[share : share + rest]
-    sums = mm_rows(pick_ref[...], far).astype(BF16)
-    grad_ref[...] = (node_ref[...] + mm_cols(sums, w_send_ref[...])).astype(BF16)
+    far = mm_cols(far, w_send_ref[...]).astype(BF16)
+    grad_ref[...] = (node_ref[...] + mm_rows(pick_ref[...], far)).astype(BF16)
 
 
 def add_kernel(keep_ref, arrived_ref, next_keep_ref, next_send_ref):
@@ -403,23 +399,23 @@
 
 
 VMEM = pl.BlockSpec(memory_space=pltpu.VMEM)
-SMEM = pl.BlockSpec(memory_space=pltpu.SMEM)
 HBM = pl.BlockSpec(memory_space=pltpu.HBM)
 COST = pl.CostEstimate(flops=1 << 10, bytes_accessed=1 << 10, transcendentals=0)
-
-
-def kernel_call(kernel, name, outs, scratch, args, near=(), far=(), limit=16):
-    specs = [SMEM if arg.shape == (1,) else VMEM for arg in args] + [VMEM] * len(near) + [HBM] * len(far)
+LARGE_COST = pl.CostEstimate(flops=1 << 10, bytes_accessed=1 << 26, transcendentals=0)
+
+
+def kernel_call(kernel, name, outs, scratch, args, near=(), far=(), limit=16, cost=COST, out_spec=None):
+    specs = [VMEM] * (len(args) + len(near)) + [HBM] * len(far)
     near = [pltpu.with_memory_space_constraint(array, pltpu.VMEM) for array in near]
     far = [pltpu.with_memory_space_constraint(array, pltpu.HBM) for array in far]
     return pl.pallas_call(
         kernel,
         out_shape=tuple(outs),
         in_specs=specs,
-        out_specs=(VMEM,) * len(outs),
+        out_specs=(out_spec or VMEM,) * len(outs),
         scratch_shapes=scratch,
         compiler_params=pltpu.CompilerParams(vmem_limit_bytes=limit << 20),
-        cost_estimate=COST,
+        cost_estimate=cost,
         name=name,
     )(*args, *near, *far)
 
@@ -450,7 +446,6 @@
     slot = send_rows.shape[2]
     share = width // count
     n_halo = count * HALO_ROWS
-    me = lax.axis_index("patch").astype(jnp.int32).reshape(1)
     sender = edge_sender.reshape(1, -1)
     receiver = edge_receiver.reshape(1, -1)
 
@@ -467,46 +462,38 @@
         "pick",
         [jax.ShapeDtypeStruct((n_far, owned), BF16), jax.ShapeDtypeStruct((n_halo, width), BF16)],
         [],
-        (me, send_rows[0].T, nodes),
+        (send_rows[0].T, nodes),
         limit=60,
     )
     halo = trade(halo_out)
-    base = pl.pallas_call(
+    rows, square, ids = space(n_edges, width), space(width, width), space(1, n_edges, dtype=jnp.int32)
+    near = kernel_call(
         local_kernel,
-        out_shape=jax.ShapeDtypeStruct((n_edges, width), F32),
-        grid=(n_edges // GRID_BLOCK,),
-        in_specs=[
-            pl.BlockSpec((1, GRID_BLOCK), lambda i: (0, i)),
-            pl.BlockSpec((1, GRID_BLOCK), lambda i: (0, i)),
-            pl.BlockSpec((owned, width), lambda i: (0, 0)),
-            pl.BlockSpec((3 * width, width), lambda i: (0, 0)),
-            pl.BlockSpec((GRID_BLOCK, width), lambda i: (i, 0)),
-        ],
-        out_specs=pl.BlockSpec((GRID_BLOCK, width), lambda i: (i, 0)),
-        scratch_shapes=[space(2 * owned, width)],
-        compiler_params=pltpu.CompilerParams(vmem_limit_bytes=60 << 20),
-        cost_estimate=COST,
-        name="local",
-    )(sender, receiver, nodes, w_edge_in, edges)
-    rows, square = space(n_edges, width), space(width, width)
-    keep1, away1, zeta, slope, normed, inv, dagg, node_part, near_nodes, near_out, near_edges, w_send, w_recv = kernel_call(
+        "local",
+        [space(owned, width), square, square, square, space(2 * owned, width)],
+        [square, pltpu.SemaphoreType.DMA((5,))],
+        (),
+        far=(nodes, w_edge_in, w_edge_out),
+    )
+    near_nodes, w_send, _, near_out, _ = near
+    keep1, away1, zeta, slope, normed, inv, dagg, node_part, near_edges, w_recv, sender, receiver = kernel_call(
         functools.partial(forward_kernel, count, slot),
         "forward",
         block_pair(3)
         + [rows, rows, rows, space(n_edges, 1, dtype=F32)]
-        + [space(owned, width), space(owned, width, dtype=F32), space(owned, width), square, rows, square, square],
-        [space(n_edges, width, dtype=F32), space(2 * width, width), square, space(owned, width)]
-        + [space(n_halo, width)]
+        + [space(owned, width), space(owned, width, dtype=F32), rows, square, ids, ids],
+        [space(2 * width, width), square, space(owned, width), space(2 * owned + n_halo, width)]
         + [space(r, width, dtype=F32) for r in (owned, width, 2 * width)]
-        + [pltpu.SemaphoreType.DMA((n_edges // BLOCK,)), pltpu.SemaphoreType.DMA((8,))],
-        (me, sender, receiver, halo),
-        far=(w_edge_in, base, w_edge_out, nodes, w_node_in, w_node_out, cot_nodes, edges),
+        + [pltpu.SemaphoreType.DMA((n_edges // BLOCK,)), pltpu.SemaphoreType.DMA((6,))],
+        (halo,),
+        near=near,
+        far=(edges, sender, receiver, w_node_in, w_node_out, cot_nodes, w_edge_in),
         limit=36,
     )
 
     def add(keep, arrived):
         half = [space(keep.shape[0] // 2, width)] * 2
-        return kernel_call(add_kernel, "add", half, [], (keep, arrived), limit=8)
+        return kernel_call(add_kernel, "add", half, [], (keep, arrived), limit=8, cost=LARGE_COST)
 
     def ride(step, keep, arrived, far):
         half = keep.shape[0] // 2
@@ -516,7 +503,7 @@
 
     came1 = cube_permute(away1, 0, count)
     dye, da = kernel_call(
-        backward_kernel, "backward", [rows, rows], [], (receiver,), (zeta, slope, normed, inv, dagg, near_out)
+        backward_kernel, "backward", [rows, rows], [], (), (receiver, zeta, slope, normed, inv, dagg, near_out)
     )
     came1, dye = in_order(came1, dye)
     keep1, away1 = add(keep1, came1)
@@ -527,26 +514,25 @@
         "weights",
         block_pair(4, n_far // 2) + [space(owned, width), space(owned, width), space(n_far, width)],
         [space(r, width, dtype=F32) for r in (2 * owned + -(-n_far // LANES) * LANES, width, 3 * width)],
-        (me, sender, receiver, halo),
-        (near_nodes, near_edges, zeta, dye, da),
-    )
-    keep1, away1 = add(keep1, came1)
-    away1, away2 = in_order(away1, away2)
-    came1 = cube_permute(away1, 2, count)
-    came2 = cube_permute(away2, 0, count)
-    keep2, away2, far_sums = ride(0, keep2, came2, far_sums)
-    came2 = cube_permute(away2, 1, count)
+        (halo,),
+        (sender, receiver, near_nodes, near_edges, zeta, dye, da),
+    )
     steps = count.bit_length() - 1
-    for step in range(3, steps):
+    for step in range(1, steps - 1):
         keep1, away1 = add(keep1, came1)
-        came1 = cube_permute(away1, step, count)
-    _, da = in_order(away1, da)
-    edge_grad = mm_cols(da, w_edge_in[:width]).astype(BF16)
-    edge_grad, came2 = in_order(edge_grad, came2)
-    for step in range(2, steps):
+        if step == 1:
+            away1, away2 = in_order(away1, away2)
+            came2 = cube_permute(away2, 0, count)
+        else:
+            away1, came2 = in_order(away1, came2)
+        came1 = cube_permute(away1, step + 1, count)
         keep2, away2, far_sums = ride(step - 1, keep2, came2, far_sums)
         came2 = cube_permute(away2, step, count)
-    away2, own_sums = in_order(away2, own_sums)
+    keep2, away2, far_sums = ride(steps - 2, keep2, came2, far_sums)
+    came1, away2 = in_order(came1, away2)
+    _, (da, own_sums) = in_order(away2, (da, own_sums))
+    came2 = cube_permute(away2, steps - 1, count)
+    edge_grad = mm_cols(da, w_edge_in[:width]).astype(BF16)
     node_sum = kernel_call(
         node_kernel, "node", [space(owned, width, dtype=F32)], [], (own_sums, recv_sums, node_part, w_send, w_recv)
     )[0]
@@ -555,7 +541,6 @@
         return [jax.ShapeDtypeStruct((part * share, width), F32) for part in parts]
 
     node_out, node_in = kernel_call(total_kernel, "node_total", whole(1, 2), [], (keep1, came1), limit=8)
-    node_out, came2 = in_order(node_out, came2)
     edge_out, edge_in, node_grad = kernel_call(
         functools.partial(last_kernel, steps - 1, count, slot),
         "last",

time: 77 us -> 71.5 us (0.929)
  Pallas kernels: 30 us -> 24.4 us
  starting transfers between devices: 14.4 us -> 10.9 us
  waiting for transfers between devices: 27.9 us -> 31.4 us
    pallas_call x1 -> x0, Pallas kernels: 6.27 us -> none  [body(): pl.pallas_call(local_kernel, out_shape=jax.ShapeDtypeStruct((n_edges, wid...]
    all_to_all x1, waiting for transfers between devices: 1.64 us -> 6.15 us  [trade(): lax.all_to_all(rows, 'patch', split_axis=0, concat_axis=0, tiled=True)]
    ppermute x8, starting transfers between devices: 7.04 us -> 3.53 us  [cube_permute(): return lax.ppermute(blocks, 'patch', pairs)]
    ppermute x8, waiting for transfers between devices: 26.3 us -> 25.3 us  [cube_permute(): return lax.ppermute(blocks, 'patch', pairs)]
    pallas_call x13 -> x14, Pallas kernels: 23.7 us -> 24.4 us  [kernel_call(): pl.pallas_call(kernel, out_shape=tuple(outs), in_specs=specs, out_specs=(...]
  transfers between devices with their start and end apart: 9 -> 9, of which waited for: 6 -> 7; matrix products, arithmetic and copies ran while one was open for 5% -> 5% of each run, Pallas kernels for 21% -> 15%
where the time goes in v3:
time: 71.5 us; the launch traced here: 71.2 us
  waiting for transfers between devices  31.4 us (44%)
  Pallas kernels  24.4 us (34%)
  starting transfers between devices  10.9 us (15%)
  matrix products  3.64 us (5%)
  between operations  0.75 us (1%)
    ppermute x8, waiting for transfers between devices, cube_permute(): return lax.ppermute(blocks, 'patch', pairs)  25.3 us
    pallas_call x14, Pallas kernels, kernel_call(): pl.pallas_call(kernel, out_shape=tuple(outs), in_specs=specs, out_specs=(...  24.4 us
    all_to_all x1, starting transfers between devices, trade(): lax.all_to_all(rows, 'patch', split_axis=0, concat_axis=0, tiled=True)  7.38 us
    all_to_all x1, waiting for transfers between devices, trade(): lax.all_to_all(rows, 'patch', split_axis=0, concat_axis=0, tiled=True)  6.15 us
    dot_general x1, matrix products, mm_cols(): lax.dot_general(left, right, (((1,), (1,)), ((), ())), preferred_element_...  3.64 us
    ppermute x8, starting transfers between devices, cube_permute(): return lax.ppermute(blocks, 'patch', pairs)  3.53 us
  transfers between devices with their start and end apart: 9, of which 7 were waited for; matrix products, arithmetic and copies ran while one was open for 5% of the time, Pallas kernels for 15%

profile of v3, /device:TPU:0, one launch (start us, length us, event | category | flops | bytes accessed | tf_op | source)
XLA Modules:
  0.0 71.2 jit_solution(14795575262619687077)
XLA Ops:
  0.6 1.9 %pick.1 = (bf16[64,256]{1,0:T(8,128)(2,1)}, bf16[128,512]{1,0:T(8,128)(2,1)}) custom-call(s32[4,16]{1,0:T(4,128)} %bitcast.13, bf16[256,512]{1,0:T(8,128)(2,1)} %nodes_far.1), custom_call_target="tpu_custom_call" | custom-call | flops 1024 | bytes 1024 | tf_op jit(solution)/shard_map/pick/pallas_call | solution.py:411
  2.5 7.4 %all-to-all-start = ((bf16[16,8,512]{2,1,0:T(8,128)(2,1)}), bf16[16,8,512]{2,1,0:T(8,128)(2,1)S(1)}, u32[]{:S(2)}, u32[]{:S(2)}) async-start(bf16[16,8,512]{2,1,0:T(8,128)(2,1)} %bitcast.10), calls=%async_computation | async-start | bytes 262144 | tf_op jit(solution)/shard_map/all_to_all | solution.py:428
  9.9 1.8 %local.1 = (bf16[256,512]{1,0:T(8,128)(2,1)S(1)}, bf16[512,512]{1,0:T(8,128)(2,1)S(1)}, bf16[512,512]{1,0:T(8,128)(2,1)S(1)}, bf16[512,512]{1,0:T(8,128)(2,1)S(1)}, bf16[512,512]{1,0:T(8,128)(2,1)S(1)}) custom-call(bf16[256,512]{1,0:T(8,128)(2,1)} %nodes_far.1, bf16[1536,512]{1,0:T(8,128)(2,1)} %w_edge_in_far.3, bf16[512,512]{1,0:T(8,128)(2,1)} %w_edge_out_far.1), custom_call_target="tpu_custom_call" | custom-call | flops 1024 | bytes 1024 | tf_op jit(solution)/shard_map/local/pallas_call | solution.py:411
  11.7 6.1 %all-to-all-done = bf16[16,8,512]{2,1,0:T(8,128)(2,1)S(1)} async-done(((bf16[16,8,512]{2,1,0:T(8,128)(2,1)}), bf16[16,8,512]{2,1,0:T(8,128)(2,1)S(1)}, u32[]{:S(2)}, u32[]{:S(2)}) %all-to-all-start) | async-done | bytes 131104 | tf_op jit(solution)/shard_map/all_to_all | solution.py:428
  17.8 9.3 %forward.1 = (bf16[768,512]{1,0:T(8,128)(2,1)S(1)}, bf16[768,512]{1,0:T(8,128)(2,1)S(1)}, bf16[2048,512]{1,0:T(8,128)(2,1)S(1)}, bf16[2048,512]{1,0:T(8,128)(2,1...) custom-call(bf16[128,512]{1,0:T(8,128)(2,1)S(1)} %bitcast.8, ...), custom_call_target="tpu_custom_call" | custom-call | flops 1024 | bytes 1024 | tf_op jit(solution)/shard_map/forward/pallas_call | solution.py:411
  27.2 0.1 collective-permute-start
  27.3 3.4 %backward.1 = (bf16[2048,512]{1,0:T(8,128)(2,1)S(1)}, bf16[2048,512]{1,0:T(8,128)(2,1)S(1)}) custom-call(s32[1,2048]{1,0:T(1,128)S(1)} %get-tuple-element.71.recv_ref, bf16[2048,512]{1,0:T(8,128)(2,1)S(1)} %get-tuple-element.73.zeta_ref, bf16[2048,512]{1,0:T(8,128)(2,1)S(1)} %get-tuple-element.75.slope_ref, ...), custom_call_target="tpu_custom_call" | custom-call | flops 1024 | bytes 1024 | tf_op jit(solution)/shard_map/backward/pallas_call | solution.py:411
  30.6 0.0 collective-permute-done.arrived_ref
  30.6 0.1 add.3
  30.7 0.1 collective-permute-start.1
  30.8 4.4 %weights.1 = (bf16[1024,512]{1,0:T(8,128)(2,1)S(1)}, bf16[1056,512]{1,0:T(8,128)(2,1)S(1)}, bf16[256,512]{1,0:T(8,128)(2,1)S(1)}, bf16[256,512]{1,0:T(8,128)(2,1)S(1)}, bf16[64,512]{1,0:T(8,128)(2,1)S(1)}) custom-call(bf16[128,512]{1,0:T(8,128)(2,1)S(1)} %bitcast.9, s32[1,2048]{1,0:T(1,128)S(1)} %get-tuple-element.70.send_ref, ...), custom_call_target="tpu_custom_call" | custom-call | flops 1024 | bytes 1024 | tf_op jit(solution)/shard_map/weights/pallas_call | solution.py:411
  35.2 3.4 %collective-permute-done.1.arrived_ref = bf16[384,512]{1,0:T(8,128)(2,1)S(1)} collective-permute-done((bf16[384,512]{1,0:T(8,128)(2,1)S(1)}, bf16[384,512]{1,0:T(8,128)(2,1)S(1)}, u32[]{:S(2)}, u32[]{:S(2)}) %collective-permute-start.1) | collective-permute-done | bytes 393248 | tf_op jit(solution)/shard_map/ppermute | solution.py:68
  38.6 0.1 collective-permute-start.2
  38.7 2.7 %collective-permute-done.2.arrived_ref = bf16[1056,512]{1,0:T(8,128)(2,1)S(1)} collective-permute-done((bf16[1056,512]{1,0:T(8,128)(2,1)S(1)}, bf16[1056,512]{1,0:T(8,128)(2,1)S(1)}, u32[]{:S(2)}, u32[]{:S(2)}) %collective-permute-start.2) | collective-permute-done | bytes 1081376 | tf_op jit(solution)/shard_map/ppermute | solution.py:68
  41.4 0.4 ride.3
  41.8 0.1 collective-permute-start.4
  41.8 0.8 %collective-permute-start.3 = (bf16[192,512]{1,0:T(8,128)(2,1)S(1)}, bf16[192,512]{1,0:T(8,128)(2,1)S(1)}, u32[]{:S(2)}, u32[]{:S(2)}) collective-permute-start(bf16[192,512]{1,0:T(8,128)(2,1)S(1)} %get-tuple-element.95), channel_id=1, source_target_pairs={{0,4},{1,3},{2,6},{3,1},{4,0},{5,7},{6,2},{7,5},{8,12},{9,11},{10,... | collective-permute-start | bytes 589832 | tf_op jit(solution)/shard_map/ppermute | solution.py:68
  42.6 7.1 %collective-permute-done.3.arrived_ref = bf16[192,512]{1,0:T(8,128)(2,1)S(1)} collective-permute-done((bf16[192,512]{1,0:T(8,128)(2,1)S(1)}, bf16[192,512]{1,0:T(8,128)(2,1)S(1)}, u32[]{:S(2)}, u32[]{:S(2)}) %collective-permute-start.3) | collective-permute-done | bytes 196640 | tf_op jit(solution)/shard_map/ppermute | solution.py:68
  49.7 3.0 %collective-permute-done.4.arrived_ref = bf16[544,512]{1,0:T(8,128)(2,1)S(1)} collective-permute-done((bf16[544,512]{1,0:T(8,128)(2,1)S(1)}, bf16[544,512]{1,0:T(8,128)(2,1)S(1)}, u32[]{:S(2)}, u32[]{:S(2)}) %collective-permute-start.4) | collective-permute-done | bytes 557088 | tf_op jit(solution)/shard_map/ppermute | solution.py:68
  52.7 0.3 ride.4
  53.0 0.8 %collective-permute-start.5 = (bf16[288,512]{1,0:T(8,128)(2,1)S(1)}, bf16[288,512]{1,0:T(8,128)(2,1)S(1)}, u32[]{:S(2)}, u32[]{:S(2)}) collective-permute-start(bf16[288,512]{1,0:T(8,128)(2,1)S(1)} %get-tuple-element.101), channel_id=1, source_target_pairs={{0,4},{1,3},{2,6},{3,1},{4,0},{5,7},{6,2},{7,5},{8,12},{9,11},{10,... | collective-permute-start | bytes 884744 | tf_op jit(solution)/shard_map/ppermute | solution.py:68
  53.8 1.4 %collective-permute-start.6 = (bf16[96,512]{1,0:T(8,128)(2,1)S(1)}, bf16[96,512]{1,0:T(8,128)(2,1)S(1)}, u32[]{:S(2)}, u32[]{:S(2)}) collective-permute-start(bf16[96,512]{1,0:T(8,128)(2,1)S(1)} %get-tuple-element.104), channel_id=1, source_target_pairs={{0,8},{1,9},{2,10},{3,11},{4,12},{5,13},{6,14},{7,15},{8,0},{9,1},... | collective-permute-start | bytes 294920 | tf_op jit(solution)/shard_map/ppermute | solution.py:68
  55.2 6.7 %collective-permute-done.5.arrived_ref = bf16[288,512]{1,0:T(8,128)(2,1)S(1)} collective-permute-done((bf16[288,512]{1,0:T(8,128)(2,1)S(1)}, bf16[288,512]{1,0:T(8,128)(2,1)S(1)}, u32[]{:S(2)}, u32[]{:S(2)}) %collective-permute-start.5) | collective-permute-done | bytes 294944 | tf_op jit(solution)/shard_map/ppermute | solution.py:68
  61.9 0.3 ride.5
  62.2 0.0 collective-permute-done.6.came_ref
  62.2 0.3 collective-permute-start.7
  62.6 3.6 %convolution_convert_fusion = bf16[2048,512]{1,0:T(8,128)(2,1)} fusion(bf16[2048,512]{1,0:T(8,128)(2,1)S(1)} %get-tuple-element.115.da_ref, bf16[1536,512]{1,0:T(8,128)(2,1)} %w_edge_in_far.3), kind=kOutput, calls=%fused_computation | convolution fusion | flops 1074790400 | bytes 4718592 | tf_op jit(solution)/shard_map/dot_general | solution.py:28
  66.2 0.0 copy-start
  66.2 0.7 node_total.1
  66.9 0.5 node.1.node_ref
  67.4 2.4 %collective-permute-done.7.arrived_ref = bf16[160,512]{1,0:T(8,128)(2,1)S(1)} collective-permute-done((bf16[160,512]{1,0:T(8,128)(2,1)S(1)}, bf16[160,512]{1,0:T(8,128)(2,1)S(1)}, u32[]{:S(2)}, u32[]{:S(2)}) %collective-permute-start.7) | collective-permute-done | bytes 163872 | tf_op jit(solution)/shard_map/ppermute | solution.py:68
  69.8 0.0 copy-done
  69.8 1.4 %last.1 = (f32[32,512]{1,0:T(8,128)}, f32[96,512]{1,0:T(8,128)}, bf16[256,512]{1,0:T(8,128)(2,1)}) custom-call(bf16[128,512]{1,0:T(8,128)(2,1)S(1)} %get-tuple-element.103.keep_ref, bf16[160,512]{1,0:T(8,128)(2,1)S(1)} %collective-permute-done.7.arrived_ref, bf16[64,512]{1,0:T(8,128)(2,1)S(1)} %get-tuple-element.107.far_ref, bf16[64,256]{1,0:T(8,128)(2,1)S(1)} %copy-done, ...), custom_call_target="tpu_custom_call" | custom-call | flops 1024 | bytes 1024 | tf_op jit(solution)/shard_map/last/pallas_call | solution.py:411
  (2 shorter events, 0.1 us)
Async XLA Ops:
  2.5 15.3 %all-to-all-start = ((bf16[16,8,512]{2,1,0:T(8,128)(2,1)}), bf16[16,8,512]{2,1,0:T(8,128)(2,1)S(1)}, u32[]{:S(2)}, u32[]{:S(2)}) async-start(bf16[16,8,512]{2,1,0:T(8,128)(2,1)} %bitcast.10), calls=%async_computation | async-start | bytes 262144 | tf_op jit(solution)/shard_map/all_to_all | solution.py:428
  27.2 3.5 %collective-permute-start = (bf16[768,512]{1,0:T(8,128)(2,1)S(1)}, bf16[768,512]{1,0:T(8,128)(2,1)S(1)}, u32[]{:S(2)}, u32[]{:S(2)}) collective-permute-start(bf16[768,512]{1,0:T(8,128)(2,1)S(1)} %get-tuple-element.74), channel_id=1, source_target_pairs={{0,1},{1,0},{2,3},{3,2},{4,5},{5,4},{6,7},{7,6},{8,9},{9,8},{10,11... | collective-permute-start | bytes 2359304 | tf_op jit(solution)/shard_map/ppermute | solution.py:68
  30.7 7.8 %collective-permute-start.1 = (bf16[384,512]{1,0:T(8,128)(2,1)S(1)}, bf16[384,512]{1,0:T(8,128)(2,1)S(1)}, u32[]{:S(2)}, u32[]{:S(2)}) collective-permute-start(bf16[384,512]{1,0:T(8,128)(2,1)S(1)} %get-tuple-element.88), channel_id=1, source_target_pairs={{0,2},{1,5},{2,0},{3,7},{4,6},{5,1},{6,4},{7,3},{8,10},{9,13},{10,... | collective-permute-start | bytes 1179656 | tf_op jit(solution)/shard_map/ppermute | solution.py:68
  38.6 2.8 %collective-permute-start.2 = (bf16[1056,512]{1,0:T(8,128)(2,1)S(1)}, bf16[1056,512]{1,0:T(8,128)(2,1)S(1)}, u32[]{:S(2)}, u32[]{:S(2)}) collective-permute-start(bf16[1056,512]{1,0:T(8,128)(2,1)S(1)} %get-tuple-element.91), channel_id=1, source_target_pairs={{0,1},{1,0},{2,3},{3,2},{4,5},{5,4},{6,7},{7,6},{8,9},{9,8},{10,11... | collective-permute-start | bytes 3244040 | tf_op jit(solution)/shard_map/ppermute | solution.py:68
  41.8 10.9 %collective-permute-start.4 = (bf16[544,512]{1,0:T(8,128)(2,1)S(1)}, bf16[544,512]{1,0:T(8,128)(2,1)S(1)}, u32[]{:S(2)}, u32[]{:S(2)}) collective-permute-start(bf16[544,512]{1,0:T(8,128)(2,1)S(1)} %get-tuple-element.97), channel_id=1, source_target_pairs={{0,2},{1,5},{2,0},{3,7},{4,6},{5,1},{6,4},{7,3},{8,10},{9,13},{10,... | collective-permute-start | bytes 1671176 | tf_op jit(solution)/shard_map/ppermute | solution.py:68
  41.8 7.8 %collective-permute-start.3 = (bf16[192,512]{1,0:T(8,128)(2,1)S(1)}, bf16[192,512]{1,0:T(8,128)(2,1)S(1)}, u32[]{:S(2)}, u32[]{:S(2)}) collective-permute-start(bf16[192,512]{1,0:T(8,128)(2,1)S(1)} %get-tuple-element.95), channel_id=1, source_target_pairs={{0,4},{1,3},{2,6},{3,1},{4,0},{5,7},{6,2},{7,5},{8,12},{9,11},{10,... | collective-permute-start | bytes 589832 | tf_op jit(solution)/shard_map/ppermute | solution.py:68
  53.0 8.8 %collective-permute-start.5 = (bf16[288,512]{1,0:T(8,128)(2,1)S(1)}, bf16[288,512]{1,0:T(8,128)(2,1)S(1)}, u32[]{:S(2)}, u32[]{:S(2)}) collective-permute-start(bf16[288,512]{1,0:T(8,128)(2,1)S(1)} %get-tuple-element.101), channel_id=1, source_target_pairs={{0,4},{1,3},{2,6},{3,1},{4,0},{5,7},{6,2},{7,5},{8,12},{9,11},{10,... | collective-permute-start | bytes 884744 | tf_op jit(solution)/shard_map/ppermute | solution.py:68
  53.8 8.4 %collective-permute-start.6 = (bf16[96,512]{1,0:T(8,128)(2,1)S(1)}, bf16[96,512]{1,0:T(8,128)(2,1)S(1)}, u32[]{:S(2)}, u32[]{:S(2)}) collective-permute-start(bf16[96,512]{1,0:T(8,128)(2,1)S(1)} %get-tuple-element.104), channel_id=1, source_target_pairs={{0,8},{1,9},{2,10},{3,11},{4,12},{5,13},{6,14},{7,15},{8,0},{9,1},... | collective-permute-start | bytes 294920 | tf_op jit(solution)/shard_map/ppermute | solution.py:68
  62.2 7.5 %collective-permute-start.7 = (bf16[160,512]{1,0:T(8,128)(2,1)S(1)}, bf16[160,512]{1,0:T(8,128)(2,1)S(1)}, u32[]{:S(2)}, u32[]{:S(2)}) collective-permute-start(bf16[160,512]{1,0:T(8,128)(2,1)S(1)} %get-tuple-element.106), channel_id=1, source_target_pairs={{0,8},{1,9},{2,10},{3,11},{4,12},{5,13},{6,14},{7,15},{8,0},{9,1},... | collective-permute-start | bytes 491528 | tf_op jit(solution)/shard_map/ppermute | solution.py:68
  66.2 3.6 %copy-start = (bf16[64,256]{1,0:T(8,128)(2,1)S(1)}, bf16[64,256]{1,0:T(8,128)(2,1)}, u32[]{:S(2)}) copy-start(bf16[64,256]{1,0:T(8,128)(2,1)} %get-tuple-element.108.pick_ref) | copy-start | bytes 98308

commit v4 on v3

--- a/solution.py
+++ b/solution.py
@@ -11,7 +11,6 @@
 F32 = jnp.float32
 EPS = 1e-05
 LANES = 128
-BLOCK = 1024
 TILE = 256
 HALO_ROWS = 8
 
@@ -152,7 +151,18 @@
 
 
 def local_kernel(
-    nodes_far, w_edge_in_far, w_edge_out_far, nodes_ref, w_send, w_self, w_edge_out_ref, table, w_recv, sems
+    nodes_far,
+    w_edge_in_far,
+    w_edge_out_far,
+    edges_far,
+    nodes_ref,
+    w_send,
+    w_self,
+    w_edge_out_ref,
+    table,
+    edges1_ref,
+    w_recv,
+    sems,
 ):
     owned, width = nodes_ref.shape
     pairs = (
@@ -161,6 +171,7 @@
         (w_edge_in_far.at[2 * width :], w_recv),
         (w_edge_in_far.at[:width], w_self),
         (w_edge_out_far, w_edge_out_ref),
+        (edges_far.at[: edges1_ref.shape[0]], edges1_ref),
     )
     copies = [pltpu.make_async_copy(src, dst, sems.at[i]) for i, (src, dst) in enumerate(pairs)]
     for copy in copies:
@@ -184,6 +195,7 @@
     w_self,
     w_edge_out_ref,
     own_table,
+    edges1_ref,
     edges_far,
     send_far,
     recv_far,
@@ -199,7 +211,7 @@
     inv_ref,
     dagg_ref,
     node_part_ref,
-    edges_ref,
+    edges2_ref,
     w_recv,
     send_ref,
     recv_ref,
@@ -210,51 +222,34 @@
     agg,
     grads_no,
     grads_ni,
-    edge_sems,
     sems,
 ):
     owned, width = nodes_ref.shape
     n_table = table.shape[0]
-    n_blocks = edges_ref.shape[0] // BLOCK
-
-    def block_rows(block):
-        return pl.ds(pl.multiple_of(block * BLOCK, BLOCK), BLOCK)
-
-    def edge_copy(block):
-        rows = block_rows(block)
-        return pltpu.make_async_copy(edges_far.at[rows], edges_ref.at[rows], edge_sems.at[block])
-
+    half = edges1_ref.shape[0]
     pairs = (
         (send_far, send_ref),
         (recv_far, recv_ref),
+        (edges_far.at[half:], edges2_ref),
         (w_node_in_far, w_node_in_ref),
         (w_node_out_far, w_node_out_ref),
         (cot_far, cot_ref),
         (w_edge_in_far.at[2 * width :], w_recv),
     )
     copies = [pltpu.make_async_copy(src, dst, sems.at[i]) for i, (src, dst) in enumerate(pairs)]
-    for copy in copies[:2]:
+    for copy in copies:
         copy.start()
-
-    @pl.loop(0, n_blocks)
-    def _(block):
-        edge_copy(block).start()
-
-    for copy in copies[2:]:
-        copy.start()
-    agg[...] = jnp.zeros_like(agg)
     nodes = nodes_ref[...]
     table[: 2 * owned] = own_table[...]
     table[2 * owned :] = mm(halo_ref[...], w_send[...]).astype(BF16)
     for copy in copies[:2]:
         copy.wait()
-
-    @pl.loop(0, n_blocks)
-    def _(block):
-        rows = block_rows(block)
-        edge_copy(block).wait()
+    for part, edges_ref in enumerate((edges1_ref, edges2_ref)):
+        if part:
+            copies[2].wait()
+        rows = slice(part * half, (part + 1) * half)
         sender, safe, receiver = edge_ids(rows, owned, slot, send_ref, recv_ref, lambda device: device * HALO_ROWS)
-        pre = mm(edges_ref[rows], w_self[...]) + mm(hot_cols(sender, safe, n_table), table[...])
+        pre = mm(edges_ref[...], w_self[...]) + mm(hot_cols(sender, safe, n_table), table[...])
         sigma = sigmoid(pre)
         zed = (pre * sigma).astype(BF16)
         zeta_ref[rows] = zed
@@ -263,9 +258,10 @@
         message = unit.astype(BF16)
         normed_ref[rows] = message
         inv_ref[rows] = inv_std
-        agg[...] += mm(hot_rows(receiver, receiver, owned), message)
-
-    for copy in copies[2:]:
+        gathered = mm(hot_rows(receiver, receiver, owned), message)
+        agg[...] = agg[...] + gathered if part else gathered
+
+    for copy in copies[3:]:
         copy.wait()
     inbox = agg[...].astype(BF16)
     pre = mm(nodes, w_node_in_ref[:width]) + mm(inbox, w_node_in_ref[width:])
@@ -284,15 +280,13 @@
 
 
 def backward_kernel(
-    recv_ref, zeta_ref, slope_ref, normed_ref, inv_ref, dagg_ref, w_edge_out_ref, dye_ref, da_ref
+    first, recv_ref, zeta_ref, slope_ref, normed_ref, inv_ref, dagg_ref, w_edge_out_ref, dye_ref, da_ref
 ):
-    @pl.loop(0, zeta_ref.shape[0] // BLOCK)
-    def _(block):
-        rows = pl.ds(pl.multiple_of(block * BLOCK, BLOCK), BLOCK)
-        up = mm(one_hot_cols(recv_ref[:, rows], dagg_ref.shape[0]), dagg_ref[...])
-        dye = norm_back(up, normed_ref[rows].astype(F32), inv_ref[rows]).astype(BF16)
-        dye_ref[rows] = dye
-        da_ref[rows] = (mm_cols(dye, w_edge_out_ref[...]) * slope_ref[rows].astype(F32)).astype(BF16)
+    rows = slice(first, first + dye_ref.shape[0])
+    up = mm(one_hot_cols(recv_ref[:, rows], dagg_ref.shape[0]), dagg_ref[...])
+    dye = norm_back(up, normed_ref[rows].astype(F32), inv_ref[rows]).astype(BF16)
+    dye_ref[...] = dye
+    da_ref[...] = (mm_cols(dye, w_edge_out_ref[...]) * slope_ref[rows].astype(F32)).astype(BF16)
 
 
 def weights_kernel(
@@ -302,10 +296,13 @@
     send_ref,
     recv_ref,
     nodes_ref,
-    edges_ref,
+    edges1_ref,
+    edges2_ref,
     zeta_ref,
-    dye_ref,
-    da_ref,
+    dye1_ref,
+    dye2_ref,
+    da1_ref,
+    da2_ref,
     keep_ref,
     away_ref,
     own_ref,
@@ -323,8 +320,10 @@
     def block_of(device):
         return cube_place(device ^ me, device & 1, count) * slot
 
+    half = da1_ref.shape[0]
     sender, safe, _ = edge_ids(slice(None), owned, slot, send_ref, recv_ref, block_of)
-    sums[...] = mm(hot_rows(sender, safe, n_table), da_ref[...])
+    hot = hot_rows(sender, safe, n_table)
+    sums[...] = mm(hot[:, :half], da1_ref[...]) + mm(hot[:, half:], da2_ref[...])
 
     own = sums[:owned].astype(BF16)
     recv = sums[owned : 2 * owned].astype(BF16)
@@ -343,8 +342,8 @@
     nodes = nodes_ref[...]
     for start in range(0, width, TILE):
         cols = slice(start, start + TILE)
-        grads_eo[cols] = mm_rows(zeta_ref[:, cols], dye_ref[...])
-        grads_ei[cols] = mm_rows(edges_ref[:, cols], da_ref[...])
+        grads_eo[cols] = mm_rows(zeta_ref[:half, cols], dye1_ref[...]) + mm_rows(zeta_ref[half:, cols], dye2_ref[...])
+        grads_ei[cols] = mm_rows(edges1_ref[:, cols], da1_ref[...]) + mm_rows(edges2_ref[:, cols], da2_ref[...])
     grads_ei[width : 2 * width] = mm_rows(nodes, own) + mm_rows(halo, far)
     grads_ei[2 * width :] = mm_rows(nodes, recv)
     put_blocks((grads_eo, grads_ei), me, count, keep_ref, away_ref)
@@ -368,21 +367,27 @@
     return (mm(stay, far) + mm_rows(take, arrived)).astype(BF16)
 
 
-def node_kernel(own_ref, recv_ref, part_ref, w_send_ref, w_recv_ref, out_ref):
-    out_ref[...] = part_ref[...] + mm_cols(own_ref[...], w_send_ref[...]) + mm_cols(recv_ref[...], w_recv_ref[...])
-
-
-def last_kernel(
-    step, count, slot, keep_ref, arrived_ref, far_ref, pick_ref, node_ref, w_send_ref, first_ref, rest_ref, grad_ref
+def node_kernel(
+    step, count, slot, own_ref, recv_ref, part_ref, w_send_ref, w_recv_ref, far_ref, pick_ref, out_ref, late_pick_ref
 ):
+    take = take_rows(step, count, slot)
+    stays = mm_rows(take, jnp.ones((take.shape[0], pick_ref.shape[1]), BF16)) == 0.0
+    early_pick = jnp.where(stays, pick_ref[...], jnp.zeros_like(pick_ref[...]))
+    late_pick_ref[...] = mm(take, pick_ref[...]).astype(BF16)
+    own = own_ref[...].astype(F32) + mm_rows(early_pick, far_ref[...])
+    out_ref[...] = (
+        part_ref[...] + mm_cols(own.astype(BF16), w_send_ref[...]) + mm_cols(recv_ref[...], w_recv_ref[...])
+    )
+
+
+def last_kernel(keep_ref, arrived_ref, late_pick_ref, node_ref, w_send_ref, first_ref, rest_ref, grad_ref):
     share, rest = first_ref.shape[0], rest_ref.shape[0]
     size = keep_ref.shape[0]
-    far = swap_rows(step, count, slot, far_ref[...], arrived_ref[size:])
+    far = mm_cols(arrived_ref[size:], w_send_ref[...]).astype(BF16)
     total = keep_ref[...].astype(F32) + arrived_ref[:size].astype(F32)
     first_ref[...] = total[:share]
     rest_ref[...] = total[share : share + rest]
-    far = mm_cols(far, w_send_ref[...]).astype(BF16)
-    grad_ref[...] = (node_ref[...] + mm_rows(pick_ref[...], far)).astype(BF16)
+    grad_ref[...] = (node_ref[...] + mm_rows(late_pick_ref[...], far)).astype(BF16)
 
 
 def add_kernel(keep_ref, arrived_ref, next_keep_ref, next_send_ref):
@@ -467,24 +472,25 @@
     )
     halo = trade(halo_out)
     rows, square, ids = space(n_edges, width), space(width, width), space(1, n_edges, dtype=jnp.int32)
+    half_rows = space(n_edges // 2, width)
     near = kernel_call(
         local_kernel,
         "local",
-        [space(owned, width), square, square, square, space(2 * owned, width)],
-        [square, pltpu.SemaphoreType.DMA((5,))],
+        [space(owned, width), square, square, square, space(2 * owned, width), half_rows],
+        [square, pltpu.SemaphoreType.DMA((6,))],
         (),
-        far=(nodes, w_edge_in, w_edge_out),
-    )
-    near_nodes, w_send, _, near_out, _ = near
-    keep1, away1, zeta, slope, normed, inv, dagg, node_part, near_edges, w_recv, sender, receiver = kernel_call(
+        far=(nodes, w_edge_in, w_edge_out, edges),
+    )
+    near_nodes, w_send, _, near_out, _, edges1 = near
+    keep1, away1, zeta, slope, normed, inv, dagg, node_part, edges2, w_recv, sender, receiver = kernel_call(
         functools.partial(forward_kernel, count, slot),
         "forward",
         block_pair(3)
         + [rows, rows, rows, space(n_edges, 1, dtype=F32)]
-        + [space(owned, width), space(owned, width, dtype=F32), rows, square, ids, ids],
+        + [space(owned, width), space(owned, width, dtype=F32), half_rows, square, ids, ids],
         [space(2 * width, width), square, space(owned, width), space(2 * owned + n_halo, width)]
         + [space(r, width, dtype=F32) for r in (owned, width, 2 * width)]
-        + [pltpu.SemaphoreType.DMA((n_edges // BLOCK,)), pltpu.SemaphoreType.DMA((6,))],
+        + [pltpu.SemaphoreType.DMA((7,))],
         (halo,),
         near=near,
         far=(edges, sender, receiver, w_node_in, w_node_out, cot_nodes, w_edge_in),
@@ -502,20 +508,22 @@
         return kernel_call(kernel, "ride", outs, [], (keep, arrived, far), limit=8)
 
     came1 = cube_permute(away1, 0, count)
-    dye, da = kernel_call(
-        backward_kernel, "backward", [rows, rows], [], (), (receiver, zeta, slope, normed, inv, dagg, near_out)
-    )
-    came1, dye = in_order(came1, dye)
+    halves = [half_rows] * 2
+    args = (receiver, zeta, slope, normed, inv, dagg, near_out)
+    dye1, da1 = kernel_call(functools.partial(backward_kernel, 0), "backward", halves, [], (), args)
+    came1, dye1 = in_order(came1, dye1)
     keep1, away1 = add(keep1, came1)
-    away1, da = in_order(away1, da)
+    away1, dagg = in_order(away1, dagg)
     came1 = cube_permute(away1, 1, count)
+    args = (receiver, zeta, slope, normed, inv, dagg, near_out)
+    dye2, da2 = kernel_call(functools.partial(backward_kernel, n_edges // 2), "backward", halves, [], (), args)
     keep2, away2, own_sums, recv_sums, far_sums = kernel_call(
         functools.partial(weights_kernel, count, slot),
         "weights",
         block_pair(4, n_far // 2) + [space(owned, width), space(owned, width), space(n_far, width)],
         [space(r, width, dtype=F32) for r in (2 * owned + -(-n_far // LANES) * LANES, width, 3 * width)],
         (halo,),
-        (sender, receiver, near_nodes, near_edges, zeta, dye, da),
+        (sender, receiver, near_nodes, edges1, edges2, zeta, dye1, dye2, da1, da2),
     )
     steps = count.bit_length() - 1
     for step in range(1, steps - 1):
@@ -530,23 +538,27 @@
         came2 = cube_permute(away2, step, count)
     keep2, away2, far_sums = ride(steps - 2, keep2, came2, far_sums)
     came1, away2 = in_order(came1, away2)
-    _, (da, own_sums) = in_order(away2, (da, own_sums))
+    _, (da1, da2, own_sums) = in_order(away2, (da1, da2, own_sums))
     came2 = cube_permute(away2, steps - 1, count)
-    edge_grad = mm_cols(da, w_edge_in[:width]).astype(BF16)
-    node_sum = kernel_call(
-        node_kernel, "node", [space(owned, width, dtype=F32)], [], (own_sums, recv_sums, node_part, w_send, w_recv)
-    )[0]
+    edge_grad = mm_cols(jnp.concatenate([da1, da2]), w_edge_in[:width]).astype(BF16)
+    node_sum, late_pick = kernel_call(
+        functools.partial(node_kernel, steps - 1, count, slot),
+        "node",
+        [space(owned, width, dtype=F32), space(n_far // 2, owned)],
+        [],
+        (own_sums, recv_sums, node_part, w_send, w_recv, far_sums, pick),
+    )
 
     def whole(*parts):
         return [jax.ShapeDtypeStruct((part * share, width), F32) for part in parts]
 
     node_out, node_in = kernel_call(total_kernel, "node_total", whole(1, 2), [], (keep1, came1), limit=8)
     edge_out, edge_in, node_grad = kernel_call(
-        functools.partial(last_kernel, steps - 1, count, slot),
+        last_kernel,
         "last",
         whole(1, 3) + [jax.ShapeDtypeStruct((owned, width), BF16)],
         [],
-        (keep2, came2, far_sums, pick, node_sum, w_send),
+        (keep2, came2, late_pick, node_sum, w_send),
         limit=8,
     )
     return node_grad, edge_grad, edge_in, edge_out, node_in, node_out

time: 71.5 us -> 69.6 us (0.973)
  waiting for transfers between devices: 31.4 us -> 30.2 us
    ppermute x8, waiting for transfers between devices: 25.3 us -> 24.2 us  [cube_permute(): return lax.ppermute(blocks, 'patch', pairs)]
    pallas_call x14 -> x15, Pallas kernels: 24.4 us -> 24.4 us  [kernel_call(): pl.pallas_call(kernel, out_shape=tuple(outs), in_specs=specs, out_specs=(...]
  transfers between devices with their start and end apart: 9 -> 9, of which waited for: 7 -> 8; matrix products, arithmetic and copies ran while one was open for 5% -> 5% of each run, Pallas kernels for 15% -> 17%
where the time goes in v4:
time: 69.6 us; the launch traced here: 69.3 us
  waiting for transfers between devices  30.2 us (43%)
  Pallas kernels  24.4 us (35%)
  starting transfers between devices  10.4 us (15%)
  matrix products  3.65 us (5%)
  between operations  0.74 us (1%)
    pallas_call x15, Pallas kernels, kernel_call(): pl.pallas_call(kernel, out_shape=tuple(outs), in_specs=specs, out_specs=(...  24.4 us
    ppermute x8, waiting for transfers between devices, cube_permute(): return lax.ppermute(blocks, 'patch', pairs)  24.2 us
    all_to_all x1, starting transfers between devices, trade(): lax.all_to_all(rows, 'patch', split_axis=0, concat_axis=0, tiled=True)  7.38 us
    all_to_all x1, waiting for transfers between devices, trade(): lax.all_to_all(rows, 'patch', split_axis=0, concat_axis=0, tiled=True)  5.93 us
    dot_general x1, matrix products, mm_cols(): lax.dot_general(left, right, (((1,), (1,)), ((), ())), preferred_element_...  3.65 us
    ppermute x8, starting transfers between devices, cube_permute(): return lax.ppermute(blocks, 'patch', pairs)  3 us
  transfers between devices with their start and end apart: 9, of which 8 were waited for; matrix products, arithmetic and copies ran while one was open for 5% of the time, Pallas kernels for 17%

profile of v4, /device:TPU:0, one launch (start us, length us, event | category | flops | bytes accessed | tf_op | source)
XLA Modules:
  0.0 69.3 jit_solution(13457586955842741143)
XLA Ops:
  0.6 1.9 %pick.1 = (bf16[64,256]{1,0:T(8,128)(2,1)}, bf16[128,512]{1,0:T(8,128)(2,1)}) custom-call(s32[4,16]{1,0:T(4,128)} %bitcast.12, bf16[256,512]{1,0:T(8,128)(2,1)} %nodes_far.1), custom_call_target="tpu_custom_call" | custom-call | flops 1024 | bytes 1024 | tf_op jit(solution)/shard_map/pick/pallas_call | solution.py:416
  2.5 7.4 %all-to-all-start = ((bf16[16,8,512]{2,1,0:T(8,128)(2,1)}), bf16[16,8,512]{2,1,0:T(8,128)(2,1)S(1)}, u32[]{:S(2)}, u32[]{:S(2)}) async-start(bf16[16,8,512]{2,1,0:T(8,128)(2,1)} %bitcast.9), calls=%async_computation | async-start | bytes 262144 | tf_op jit(solution)/shard_map/all_to_all | solution.py:433
  9.9 2.0 %local.1 = (bf16[256,512]{1,0:T(8,128)(2,1)S(1)}, bf16[512,512]{1,0:T(8,128)(2,1)S(1)}, bf16[512,512]{1,0:T(8,128)(2,1)S(1)}, bf16[512,512]{1,0:T(8,128)(2,1)S(1...) custom-call(bf16[256,512]{1,0:T(8,128)(2,1)} %nodes_far.1, bf16[1536,512]{1,0:T(8,128)(2,1)} %w_edge_in_far.3, ...), custom_call_target="tpu_custom_call" | custom-call | flops 1024 | bytes 1024 | tf_op jit(solution)/shard_map/local/pallas_call | solution.py:416
  11.9 5.9 %all-to-all-done = bf16[16,8,512]{2,1,0:T(8,128)(2,1)S(1)} async-done(((bf16[16,8,512]{2,1,0:T(8,128)(2,1)}), bf16[16,8,512]{2,1,0:T(8,128)(2,1)S(1)}, u32[]{:S(2)}, u32[]{:S(2)}) %all-to-all-start) | async-done | bytes 131104 | tf_op jit(solution)/shard_map/all_to_all | solution.py:433
  17.8 8.8 %forward.1 = (bf16[768,512]{1,0:T(8,128)(2,1)S(1)}, bf16[768,512]{1,0:T(8,128)(2,1)S(1)}, bf16[2048,512]{1,0:T(8,128)(2,1)S(1)}, bf16[2048,512]{1,0:T(8,128)(2,1...) custom-call(bf16[128,512]{1,0:T(8,128)(2,1)S(1)} %bitcast.7, ...), custom_call_target="tpu_custom_call" | custom-call | flops 1024 | bytes 1024 | tf_op jit(solution)/shard_map/forward/pallas_call | solution.py:416
  26.7 0.1 collective-permute-start
  26.8 1.6 %backward.2 = (bf16[1024,512]{1,0:T(8,128)(2,1)S(1)}, bf16[1024,512]{1,0:T(8,128)(2,1)S(1)}) custom-call(s32[1,2048]{1,0:T(1,128)S(1)} %get-tuple-element.78.recv_ref, bf16[2048,512]{1,0:T(8,128)(2,1)S(1)} %get-tuple-element.80.zeta_ref, bf16[2048,512]{1,0:T(8,128)(2,1)S(1)} %get-tuple-element.82.slope_ref, ...), custom_call_target="tpu_custom_call" | custom-call | flops 1024 | bytes 1024 | tf_op jit(solution)/shard_map/backward/pallas_call | solution.py:416
  28.4 0.6 collective-permute-done.arrived_ref
  29.0 0.1 add.3
  29.1 0.1 collective-permute-start.1
  29.2 1.6 %backward.3 = (bf16[1024,512]{1,0:T(8,128)(2,1)S(1)}, bf16[1024,512]{1,0:T(8,128)(2,1)S(1)}) custom-call(s32[1,2048]{1,0:T(1,128)S(1)} %get-tuple-element.78.recv_ref, bf16[2048,512]{1,0:T(8,128)(2,1)S(1)} %get-tuple-element.80.zeta_ref, bf16[2048,512]{1,0:T(8,128)(2,1)S(1)} %get-tuple-element.82.slope_ref, ...), custom_call_target="tpu_custom_call" | custom-call | flops 1024 | bytes 1024 | tf_op jit(solution)/shard_map/backward/pallas_call | solution.py:416
  30.8 4.5 %weights.1 = (bf16[1024,512]{1,0:T(8,128)(2,1)S(1)}, bf16[1056,512]{1,0:T(8,128)(2,1)S(1)}, bf16[256,512]{1,0:T(8,128)(2,1)S(1)}, bf16[256,512]{1,0:T(8,128)(2,1)S(1)}, bf16[64,512]{1,0:T(8,128)(2,1)S(1)}) custom-call(bf16[128,512]{1,0:T(8,128)(2,1)S(1)} %bitcast.8, s32[1,2048]{1,0:T(1,128)S(1)} %get-tuple-element.77.send_ref, ...), custom_call_target="tpu_custom_call" | custom-call | flops 1024 | bytes 1024 | tf_op jit(solution)/shard_map/weights/pallas_call | solution.py:416
  35.4 1.6 %collective-permute-done.1.arrived_ref = bf16[384,512]{1,0:T(8,128)(2,1)S(1)} collective-permute-done((bf16[384,512]{1,0:T(8,128)(2,1)S(1)}, bf16[384,512]{1,0:T(8,128)(2,1)S(1)}, u32[]{:S(2)}, u32[]{:S(2)}) %collective-permute-start.1) | collective-permute-done | bytes 393248 | tf_op jit(solution)/shard_map/ppermute | solution.py:67
  37.0 0.1 add.4
  37.0 0.1 collective-permute-start.2
  37.1 2.7 %collective-permute-done.2.arrived_ref = bf16[1056,512]{1,0:T(8,128)(2,1)S(1)} collective-permute-done((bf16[1056,512]{1,0:T(8,128)(2,1)S(1)}, bf16[1056,512]{1,0:T(8,128)(2,1)S(1)}, u32[]{:S(2)}, u32[]{:S(2)}) %collective-permute-start.2) | collective-permute-done | bytes 1081376 | tf_op jit(solution)/shard_map/ppermute | solution.py:67
  39.8 0.0 copy-start
  39.8 0.3 ride.3
  40.1 0.5 collective-permute-start.4
  40.6 0.0 collective-permute-start.3
  40.6 7.8 %collective-permute-done.3.arrived_ref = bf16[192,512]{1,0:T(8,128)(2,1)S(1)} collective-permute-done((bf16[192,512]{1,0:T(8,128)(2,1)S(1)}, bf16[192,512]{1,0:T(8,128)(2,1)S(1)}, u32[]{:S(2)}, u32[]{:S(2)}) %collective-permute-start.3) | collective-permute-done | bytes 196640 | tf_op jit(solution)/shard_map/ppermute | solution.py:67
  48.5 2.6 %collective-permute-done.4.arrived_ref = bf16[544,512]{1,0:T(8,128)(2,1)S(1)} collective-permute-done((bf16[544,512]{1,0:T(8,128)(2,1)S(1)}, bf16[544,512]{1,0:T(8,128)(2,1)S(1)}, u32[]{:S(2)}, u32[]{:S(2)}) %collective-permute-start.4) | collective-permute-done | bytes 557088 | tf_op jit(solution)/shard_map/ppermute | solution.py:67
  51.1 0.3 ride.4
  51.4 0.7 collective-permute-start.5
  52.1 1.4 %collective-permute-start.6 = (bf16[96,512]{1,0:T(8,128)(2,1)S(1)}, bf16[96,512]{1,0:T(8,128)(2,1)S(1)}, u32[]{:S(2)}, u32[]{:S(2)}) collective-permute-start(bf16[96,512]{1,0:T(8,128)(2,1)S(1)} %get-tuple-element.113), channel_id=1, source_target_pairs={{0,8},{1,9},{2,10},{3,11},{4,12},{5,13},{6,14},{7,15},{8,0},{9,1},... | collective-permute-start | bytes 294920 | tf_op jit(solution)/shard_map/ppermute | solution.py:67
  53.5 6.8 %collective-permute-done.5.arrived_ref = bf16[288,512]{1,0:T(8,128)(2,1)S(1)} collective-permute-done((bf16[288,512]{1,0:T(8,128)(2,1)S(1)}, bf16[288,512]{1,0:T(8,128)(2,1)S(1)}, u32[]{:S(2)}, u32[]{:S(2)}) %collective-permute-start.5) | collective-permute-done | bytes 294944 | tf_op jit(solution)/shard_map/ppermute | solution.py:67
  60.3 0.3 ride.5
  60.6 0.0 collective-permute-done.6.came_ref
  60.6 0.2 collective-permute-start.7
  60.9 0.7 node_total.1
  61.6 0.0 copy-done
  61.6 0.8 %node.1 = (f32[256,512]{1,0:T(8,128)S(1)}, bf16[32,256]{1,0:T(8,128)(2,1)S(1)}) custom-call(bf16[256,512]{1,0:T(8,128)(2,1)S(1)} %get-tuple-element.117.own_ref, bf16[256,512]{1,0:T(8,128)(2,1)S(1)} %get-tuple-element.118.recv_ref, f32[256,512]{1,0:T(8,128)S(1)} %get-tuple-element.119.part_ref, bf16[512,512]{1,0:T(8,128)(2,1)S(1)} %get-tuple-element.72.w_send.w_send_ref, ...), custom_call_target="tpu_custom_call" | custom-call | flops 1024 | bytes 1024 | tf_op jit(solution)/shard_map/node/pallas_call | solution.py:416
  62.3 3.6 %convolution_convert_fusion = bf16[2048,512]{1,0:T(8,128)(2,1)} fusion(bf16[1024,512]{1,0:T(8,128)(2,1)S(1)} %get-tuple-element.127.da2_ref, bf16[1024,512]{1,0:T(8,128)(2,1)S(1)} %get-tuple-element.126.da1_ref, bf16[1536,512]{1,0:T(8,128)(2,1)} %w_edge_in_far.3), kind=kOutput, calls=%fused_computation | convolution fusion | flops 1078984704 | bytes 4718592 | tf_op jit(solution)/shard_map/dot_general | solution.py:27
  66.0 2.1 %collective-permute-done.7.arrived_ref = bf16[160,512]{1,0:T(8,128)(2,1)S(1)} collective-permute-done((bf16[160,512]{1,0:T(8,128)(2,1)S(1)}, bf16[160,512]{1,0:T(8,128)(2,1)S(1)}, u32[]{:S(2)}, u32[]{:S(2)}) %collective-permute-start.7) | collective-permute-done | bytes 163872 | tf_op jit(solution)/shard_map/ppermute | solution.py:67
  68.1 1.2 %last.1 = (f32[32,512]{1,0:T(8,128)}, f32[96,512]{1,0:T(8,128)}, bf16[256,512]{1,0:T(8,128)(2,1)}) custom-call(bf16[128,512]{1,0:T(8,128)(2,1)S(1)} %get-tuple-element.112.keep_ref, bf16[160,512]{1,0:T(8,128)(2,1)S(1)} %collective-permute-done.7.arrived_ref, bf16[32,256]{1,0:T(8,128)(2,1)S(1)} %get-tuple-element.123.late_pick_ref, ...), custom_call_target="tpu_custom_call" | custom-call | flops 1024 | bytes 1024 | tf_op jit(solution)/shard_map/last/pallas_call | solution.py:416
  (1 shorter events, 0.0 us)
Async XLA Ops:
  2.5 15.3 %all-to-all-start = ((bf16[16,8,512]{2,1,0:T(8,128)(2,1)}), bf16[16,8,512]{2,1,0:T(8,128)(2,1)S(1)}, u32[]{:S(2)}, u32[]{:S(2)}) async-start(bf16[16,8,512]{2,1,0:T(8,128)(2,1)} %bitcast.9), calls=%async_computation | async-start | bytes 262144 | tf_op jit(solution)/shard_map/all_to_all | solution.py:433
  26.7 2.4 %collective-permute-start = (bf16[768,512]{1,0:T(8,128)(2,1)S(1)}, bf16[768,512]{1,0:T(8,128)(2,1)S(1)}, u32[]{:S(2)}, u32[]{:S(2)}) collective-permute-start(bf16[768,512]{1,0:T(8,128)(2,1)S(1)} %get-tuple-element.81), channel_id=1, source_target_pairs={{0,1},{1,0},{2,3},{3,2},{4,5},{5,4},{6,7},{7,6},{8,9},{9,8},{10,11... | collective-permute-start | bytes 2359304 | tf_op jit(solution)/shard_map/ppermute | solution.py:67
  29.1 7.8 %collective-permute-start.1 = (bf16[384,512]{1,0:T(8,128)(2,1)S(1)}, bf16[384,512]{1,0:T(8,128)(2,1)S(1)}, u32[]{:S(2)}, u32[]{:S(2)}) collective-permute-start(bf16[384,512]{1,0:T(8,128)(2,1)S(1)} %get-tuple-element.97), channel_id=1, source_target_pairs={{0,2},{1,5},{2,0},{3,7},{4,6},{5,1},{6,4},{7,3},{8,10},{9,13},{10,... | collective-permute-start | bytes 1179656 | tf_op jit(solution)/shard_map/ppermute | solution.py:67
  37.0 2.8 %collective-permute-start.2 = (bf16[1056,512]{1,0:T(8,128)(2,1)S(1)}, bf16[1056,512]{1,0:T(8,128)(2,1)S(1)}, u32[]{:S(2)}, u32[]{:S(2)}) collective-permute-start(bf16[1056,512]{1,0:T(8,128)(2,1)S(1)} %get-tuple-element.100), channel_id=1, source_target_pairs={{0,1},{1,0},{2,3},{3,2},{4,5},{5,4},{6,7},{7,6},{8,9},{9,8},{10,11... | collective-permute-start | bytes 3244040 | tf_op jit(solution)/shard_map/ppermute | solution.py:67
  39.8 21.8 %copy-start = (bf16[64,256]{1,0:T(8,128)(2,1)S(1)}, bf16[64,256]{1,0:T(8,128)(2,1)}, u32[]{:S(2)}) copy-start(bf16[64,256]{1,0:T(8,128)(2,1)} %get-tuple-element.122.pick_ref) | copy-start | bytes 98308
  40.1 10.9 %collective-permute-start.4 = (bf16[544,512]{1,0:T(8,128)(2,1)S(1)}, bf16[544,512]{1,0:T(8,128)(2,1)S(1)}, u32[]{:S(2)}, u32[]{:S(2)}) collective-permute-start(bf16[544,512]{1,0:T(8,128)(2,1)S(1)} %get-tuple-element.106), channel_id=1, source_target_pairs={{0,2},{1,5},{2,0},{3,7},{4,6},{5,1},{6,4},{7,3},{8,10},{9,13},{10,... | collective-permute-start | bytes 1671176 | tf_op jit(solution)/shard_map/ppermute | solution.py:67
  40.6 7.8 %collective-permute-start.3 = (bf16[192,512]{1,0:T(8,128)(2,1)S(1)}, bf16[192,512]{1,0:T(8,128)(2,1)S(1)}, u32[]{:S(2)}, u32[]{:S(2)}) collective-permute-start(bf16[192,512]{1,0:T(8,128)(2,1)S(1)} %get-tuple-element.104), channel_id=1, source_target_pairs={{0,4},{1,3},{2,6},{3,1},{4,0},{5,7},{6,2},{7,5},{8,12},{9,11},{10,... | collective-permute-start | bytes 589832 | tf_op jit(solution)/shard_map/ppermute | solution.py:67
  51.4 8.8 %collective-permute-start.5 = (bf16[288,512]{1,0:T(8,128)(2,1)S(1)}, bf16[288,512]{1,0:T(8,128)(2,1)S(1)}, u32[]{:S(2)}, u32[]{:S(2)}) collective-permute-start(bf16[288,512]{1,0:T(8,128)(2,1)S(1)} %get-tuple-element.110), channel_id=1, source_target_pairs={{0,4},{1,3},{2,6},{3,1},{4,0},{5,7},{6,2},{7,5},{8,12},{9,11},{10,... | collective-permute-start | bytes 884744 | tf_op jit(solution)/shard_map/ppermute | solution.py:67
  52.1 8.5 %collective-permute-start.6 = (bf16[96,512]{1,0:T(8,128)(2,1)S(1)}, bf16[96,512]{1,0:T(8,128)(2,1)S(1)}, u32[]{:S(2)}, u32[]{:S(2)}) collective-permute-start(bf16[96,512]{1,0:T(8,128)(2,1)S(1)} %get-tuple-element.113), channel_id=1, source_target_pairs={{0,8},{1,9},{2,10},{3,11},{4,12},{5,13},{6,14},{7,15},{8,0},{9,1},... | collective-permute-start | bytes 294920 | tf_op jit(solution)/shard_map/ppermute | solution.py:67
  60.6 7.5 %collective-permute-start.7 = (bf16[160,512]{1,0:T(8,128)(2,1)S(1)}, bf16[160,512]{1,0:T(8,128)(2,1)S(1)}, u32[]{:S(2)}, u32[]{:S(2)}) collective-permute-start(bf16[160,512]{1,0:T(8,128)(2,1)S(1)} %get-tuple-element.115), channel_id=1, source_target_pairs={{0,8},{1,9},{2,10},{3,11},{4,12},{5,13},{6,14},{7,15},{8,0},{9,1},... | collective-permute-start | bytes 491528 | tf_op jit(solution)/shard_map/ppermute | solution.py:67

commit v5 on v4

--- a/solution.py
+++ b/solution.py
@@ -151,16 +151,18 @@
 
 
 def local_kernel(
+    count,
+    slot,
     nodes_far,
     w_edge_in_far,
     w_edge_out_far,
     edges_far,
     nodes_ref,
     w_send,
-    w_self,
     w_edge_out_ref,
     table,
     edges1_ref,
+    moves_ref,
     w_recv,
     sems,
 ):
@@ -169,19 +171,21 @@
         (nodes_far, nodes_ref),
         (w_edge_in_far.at[width : 2 * width], w_send),
         (w_edge_in_far.at[2 * width :], w_recv),
-        (w_edge_in_far.at[:width], w_self),
+        (w_edge_in_far.at[:width], table.at[:width]),
         (w_edge_out_far, w_edge_out_ref),
         (edges_far.at[: edges1_ref.shape[0]], edges1_ref),
     )
     copies = [pltpu.make_async_copy(src, dst, sems.at[i]) for i, (src, dst) in enumerate(pairs)]
     for copy in copies:
         copy.start()
+    for step in range(moves_ref.shape[0]):
+        moves_ref[step] = move_rows(step, count, slot)
     copies[0].wait()
     nodes = nodes_ref[...]
     copies[1].wait()
-    table[:owned] = mm(nodes, w_send[...]).astype(BF16)
+    table[width : width + owned] = mm(nodes, w_send[...]).astype(BF16)
     copies[2].wait()
-    table[owned:] = mm(nodes, w_recv[...]).astype(BF16)
+    table[width + owned :] = mm(nodes, w_recv[...]).astype(BF16)
     for copy in copies[3:]:
         copy.wait()
 
@@ -192,7 +196,6 @@
     halo_ref,
     nodes_ref,
     w_send,
-    w_self,
     w_edge_out_ref,
     own_table,
     edges1_ref,
@@ -240,8 +243,8 @@
     for copy in copies:
         copy.start()
     nodes = nodes_ref[...]
-    table[: 2 * owned] = own_table[...]
-    table[2 * owned :] = mm(halo_ref[...], w_send[...]).astype(BF16)
+    table[: width + 2 * owned] = own_table[...]
+    table[width + 2 * owned :] = mm(halo_ref[...], w_send[...]).astype(BF16)
     for copy in copies[:2]:
         copy.wait()
     for part, edges_ref in enumerate((edges1_ref, edges2_ref)):
@@ -249,7 +252,8 @@
             copies[2].wait()
         rows = slice(part * half, (part + 1) * half)
         sender, safe, receiver = edge_ids(rows, owned, slot, send_ref, recv_ref, lambda device: device * HALO_ROWS)
-        pre = mm(edges_ref[...], w_self[...]) + mm(hot_cols(sender, safe, n_table), table[...])
+        hot = hot_cols(sender, safe, n_table - width)
+        pre = mm(jnp.concatenate([edges_ref[...], hot], axis=1), table[...])
         sigma = sigmoid(pre)
         zed = (pre * sigma).astype(BF16)
         zeta_ref[rows] = zed
@@ -349,22 +353,25 @@
     put_blocks((grads_eo, grads_ei), me, count, keep_ref, away_ref)
 
 
-def ride_kernel(step, count, slot, keep_ref, arrived_ref, far_ref, next_keep_ref, next_away_ref, next_far_ref):
+def move_rows(step, count, slot):
+    take = take_rows(step, count, slot)
+    rows = take.shape[1]
+    square = lax.broadcasted_iota(jnp.int32, (rows, rows), 0) == lax.broadcasted_iota(jnp.int32, (rows, rows), 1)
+    eye = jnp.where(square, 1.0, 0.0)
+    stay = (eye - mm_rows(take, take)).astype(BF16)
+    small = eye[: rows // 2, : rows // 2].astype(BF16)
+    after = jnp.concatenate([stay, mm_rows(take, small).astype(BF16)], axis=1)
+    return jnp.concatenate([mm(take_rows(step + 1, count, slot), after).astype(BF16), after], axis=0)
+
+
+def ride_kernel(step, keep_ref, arrived_ref, far_ref, moves_ref, next_keep_ref, next_away_ref, next_far_ref):
     size, half = keep_ref.shape[0], next_keep_ref.shape[0]
+    moved = mm(moves_ref[step], jnp.concatenate([far_ref[...], arrived_ref[size:]], axis=0)).astype(BF16)
     next_keep_ref[...] = keep_ref[:half] + arrived_ref[:half]
     next_away_ref[:half] = keep_ref[half:] + arrived_ref[half:size]
-    far = swap_rows(step, count, slot, far_ref[...], arrived_ref[size:])
-    next_far_ref[...] = far
-    next_away_ref[half:] = mm(take_rows(step + 1, count, slot), far).astype(BF16)
-
-
-def swap_rows(step, count, slot, far, arrived):
-    take = take_rows(step, count, slot)
-    stays = 1.0 - jnp.sum(take.astype(F32), axis=0, keepdims=True)
-    rows = far.shape[0]
-    square = lax.broadcasted_iota(jnp.int32, (rows, rows), 0) == lax.broadcasted_iota(jnp.int32, (rows, rows), 1)
-    stay = jnp.where(square, stays, 0.0).astype(BF16)
-    return (mm(stay, far) + mm_rows(take, arrived)).astype(BF16)
+    split = moved.shape[0] - next_far_ref.shape[0]
+    next_away_ref[half:] = moved[:split]
+    next_far_ref[...] = moved[split:]
 
 
 def node_kernel(
@@ -462,6 +469,7 @@
         return [space(size, width), space(size + riders, width)]
 
     n_far = count * slot
+    steps = count.bit_length() - 1
     pick, halo_out = kernel_call(
         functools.partial(pick_kernel, count),
         "pick",
@@ -473,22 +481,23 @@
     halo = trade(halo_out)
     rows, square, ids = space(n_edges, width), space(width, width), space(1, n_edges, dtype=jnp.int32)
     half_rows = space(n_edges // 2, width)
-    near = kernel_call(
-        local_kernel,
+    *near, moves = kernel_call(
+        functools.partial(local_kernel, count, slot),
         "local",
-        [space(owned, width), square, square, square, space(2 * owned, width), half_rows],
+        [space(owned, width), square, square, space(width + 2 * owned, width), half_rows]
+        + [space(steps - 1, n_far * 3 // 2, n_far * 3 // 2)],
         [square, pltpu.SemaphoreType.DMA((6,))],
         (),
         far=(nodes, w_edge_in, w_edge_out, edges),
     )
-    near_nodes, w_send, _, near_out, _, edges1 = near
+    near_nodes, w_send, near_out, _, edges1 = near
     keep1, away1, zeta, slope, normed, inv, dagg, node_part, edges2, w_recv, sender, receiver = kernel_call(
         functools.partial(forward_kernel, count, slot),
         "forward",
         block_pair(3)
         + [rows, rows, rows, space(n_edges, 1, dtype=F32)]
         + [space(owned, width), space(owned, width, dtype=F32), half_rows, square, ids, ids],
-        [space(2 * width, width), square, space(owned, width), space(2 * owned + n_halo, width)]
+        [space(2 * width, width), square, space(owned, width), space(width + 2 * owned + n_halo, width)]
         + [space(r, width, dtype=F32) for r in (owned, width, 2 * width)]
         + [pltpu.SemaphoreType.DMA((7,))],
         (halo,),
@@ -504,8 +513,9 @@
     def ride(step, keep, arrived, far):
         half = keep.shape[0] // 2
         outs = [space(half, width), space(half + n_far // 2, width), space(n_far, width)]
-        kernel = functools.partial(ride_kernel, step, count, slot)
-        return kernel_call(kernel, "ride", outs, [], (keep, arrived, far), limit=8)
+        return kernel_call(
+            functools.partial(ride_kernel, step), "ride", outs, [], (keep, arrived, far), (moves,), limit=8
+        )
 
     came1 = cube_permute(away1, 0, count)
     halves = [half_rows] * 2
@@ -525,7 +535,6 @@
         (halo,),
         (sender, receiver, near_nodes, edges1, edges2, zeta, dye1, dye2, da1, da2),
     )
-    steps = count.bit_length() - 1
     for step in range(1, steps - 1):
         keep1, away1 = add(keep1, came1)
         if step == 1:

time: 69.6 us -> 69.2 us (level)
  waiting for transfers between devices: 30.2 us -> 29 us
    all_to_all x1, waiting for transfers between devices: 5.93 us -> 4.83 us  [trade(): lax.all_to_all(rows, 'patch', split_axis=0, concat_axis=0, tiled=True)]
where the time goes in v5:
time: 69.2 us; the launch traced here: 68.9 us
  waiting for transfers between devices  29 us (42%)
  Pallas kernels  24.1 us (35%)
  starting transfers between devices  10.7 us (15%)
  matrix products  3.65 us (5%)
  between operations  0.76 us (1%)
    ppermute x8, waiting for transfers between devices, cube_permute(): return lax.ppermute(blocks, 'patch', pairs)  24.2 us
    pallas_call x15, Pallas kernels, kernel_call(): pl.pallas_call(kernel, out_shape=tuple(outs), in_specs=specs, out_specs=(...  24.1 us
    all_to_all x1, starting transfers between devices, trade(): lax.all_to_all(rows, 'patch', split_axis=0, concat_axis=0, tiled=True)  7.38 us
    all_to_all x1, waiting for transfers between devices, trade(): lax.all_to_all(rows, 'patch', split_axis=0, concat_axis=0, tiled=True)  4.83 us
    dot_general x1, matrix products, mm_cols(): lax.dot_general(left, right, (((1,), (1,)), ((), ())), preferred_element_...  3.65 us
    ppermute x8, starting transfers between devices, cube_permute(): return lax.ppermute(blocks, 'patch', pairs)  3.29 us
  transfers between devices with their start and end apart: 9, of which 8 were waited for; matrix products, arithmetic and copies ran while one was open for 5% of the time, Pallas kernels for 17%

profile of v5, /device:TPU:0, one launch (start us, length us, event | category | flops | bytes accessed | tf_op | source)
XLA Modules:
  0.0 68.9 jit_solution(13959909697846484551)
XLA Ops:
  0.6 1.9 %pick.1 = (bf16[64,256]{1,0:T(8,128)(2,1)}, bf16[128,512]{1,0:T(8,128)(2,1)}) custom-call(s32[4,16]{1,0:T(4,128)} %bitcast.12, bf16[256,512]{1,0:T(8,128)(2,1)} %nodes_far.1), custom_call_target="tpu_custom_call" | custom-call | flops 1024 | bytes 1024 | tf_op jit(solution)/shard_map/pick/pallas_call | solution.py:423
  2.5 7.4 %all-to-all-start = ((bf16[16,8,512]{2,1,0:T(8,128)(2,1)}), bf16[16,8,512]{2,1,0:T(8,128)(2,1)S(1)}, u32[]{:S(2)}, u32[]{:S(2)}) async-start(bf16[16,8,512]{2,1,0:T(8,128)(2,1)} %bitcast.9), calls=%async_computation | async-start | bytes 262144 | tf_op jit(solution)/shard_map/all_to_all | solution.py:440
  9.9 2.5 %local.1 = (bf16[256,512]{1,0:T(8,128)(2,1)S(1)}, bf16[512,512]{1,0:T(8,128)(2,1)S(1)}, bf16[512,512]{1,0:T(8,128)(2,1)S(1)}, bf16[1024,512]{1,0:T(8,128)(2,1)S(...) custom-call(bf16[256,512]{1,0:T(8,128)(2,1)} %nodes_far.1, bf16[1536,512]{1,0:T(8,128)(2,1)} %w_edge_in_far.3, ...), custom_call_target="tpu_custom_call" | custom-call | flops 1024 | bytes 1024 | tf_op jit(solution)/shard_map/local/pallas_call | solution.py:423
  12.4 0.0 copy-start
  12.4 0.6 copy-done
  13.0 4.8 %all-to-all-done = bf16[16,8,512]{2,1,0:T(8,128)(2,1)S(1)} async-done(((bf16[16,8,512]{2,1,0:T(8,128)(2,1)}), bf16[16,8,512]{2,1,0:T(8,128)(2,1)S(1)}, u32[]{:S(2)}, u32[]{:S(2)}) %all-to-all-start) | async-done | bytes 131104 | tf_op jit(solution)/shard_map/all_to_all | solution.py:440
  17.8 8.7 %forward.1 = (bf16[768,512]{1,0:T(8,128)(2,1)S(1)}, bf16[768,512]{1,0:T(8,128)(2,1)S(1)}, bf16[2048,512]{1,0:T(8,128)(2,1)S(1)}, bf16[2048,512]{1,0:T(8,128)(2,1...) custom-call(bf16[128,512]{1,0:T(8,128)(2,1)S(1)} %bitcast.7, ...), custom_call_target="tpu_custom_call" | custom-call | flops 1024 | bytes 1024 | tf_op jit(solution)/shard_map/forward/pallas_call | solution.py:423
  26.5 0.1 collective-permute-start
  26.6 1.6 %backward.2 = (bf16[1024,512]{1,0:T(8,128)(2,1)S(1)}, bf16[1024,512]{1,0:T(8,128)(2,1)S(1)}) custom-call(s32[1,2048]{1,0:T(1,128)S(1)} %get-tuple-element.77.recv_ref, bf16[2048,512]{1,0:T(8,128)(2,1)S(1)} %get-tuple-element.79.zeta_ref, bf16[2048,512]{1,0:T(8,128)(2,1)S(1)} %get-tuple-element.81.slope_ref, ...), custom_call_target="tpu_custom_call" | custom-call | flops 1024 | bytes 1024 | tf_op jit(solution)/shard_map/backward/pallas_call | solution.py:423
  28.3 0.6 collective-permute-done.arrived_ref
  28.9 0.1 add.3
  29.0 0.1 collective-permute-start.1
  29.1 1.6 %backward.3 = (bf16[1024,512]{1,0:T(8,128)(2,1)S(1)}, bf16[1024,512]{1,0:T(8,128)(2,1)S(1)}) custom-call(s32[1,2048]{1,0:T(1,128)S(1)} %get-tuple-element.77.recv_ref, bf16[2048,512]{1,0:T(8,128)(2,1)S(1)} %get-tuple-element.79.zeta_ref, bf16[2048,512]{1,0:T(8,128)(2,1)S(1)} %get-tuple-element.81.slope_ref, ...), custom_call_target="tpu_custom_call" | custom-call | flops 1024 | bytes 1024 | tf_op jit(solution)/shard_map/backward/pallas_call | solution.py:423
  30.7 0.0 copy-start.1
  30.7 4.5 %weights.1 = (bf16[1024,512]{1,0:T(8,128)(2,1)S(1)}, bf16[1056,512]{1,0:T(8,128)(2,1)S(1)}, bf16[256,512]{1,0:T(8,128)(2,1)S(1)}, bf16[256,512]{1,0:T(8,128)(2,1)S(1)}, bf16[64,512]{1,0:T(8,128)(2,1)S(1)}) custom-call(bf16[128,512]{1,0:T(8,128)(2,1)S(1)} %bitcast.8, s32[1,2048]{1,0:T(1,128)S(1)} %get-tuple-element.76.send_ref, ...), custom_call_target="tpu_custom_call" | custom-call | flops 1024 | bytes 1024 | tf_op jit(solution)/shard_map/weights/pallas_call | solution.py:423
  35.2 1.6 %collective-permute-done.1.arrived_ref = bf16[384,512]{1,0:T(8,128)(2,1)S(1)} collective-permute-done((bf16[384,512]{1,0:T(8,128)(2,1)S(1)}, bf16[384,512]{1,0:T(8,128)(2,1)S(1)}, u32[]{:S(2)}, u32[]{:S(2)}) %collective-permute-start.1) | collective-permute-done | bytes 393248 | tf_op jit(solution)/shard_map/ppermute | solution.py:67
  36.9 0.1 collective-permute-start.2
  36.9 2.7 %collective-permute-done.2.arrived_ref = bf16[1056,512]{1,0:T(8,128)(2,1)S(1)} collective-permute-done((bf16[1056,512]{1,0:T(8,128)(2,1)S(1)}, bf16[1056,512]{1,0:T(8,128)(2,1)S(1)}, u32[]{:S(2)}, u32[]{:S(2)}) %collective-permute-start.2) | collective-permute-done | bytes 1081376 | tf_op jit(solution)/shard_map/ppermute | solution.py:67
  39.6 0.0 copy-done.1
  39.6 0.0 copy-start.2
  39.6 0.2 ride.3
  39.8 0.5 collective-permute-start.4
  40.4 0.0 collective-permute-start.3
  40.4 7.8 %collective-permute-done.3.arrived_ref = bf16[192,512]{1,0:T(8,128)(2,1)S(1)} collective-permute-done((bf16[192,512]{1,0:T(8,128)(2,1)S(1)}, bf16[192,512]{1,0:T(8,128)(2,1)S(1)}, u32[]{:S(2)}, u32[]{:S(2)}) %collective-permute-start.3) | collective-permute-done | bytes 196640 | tf_op jit(solution)/shard_map/ppermute | solution.py:67
  48.2 2.6 %collective-permute-done.4.arrived_ref = bf16[544,512]{1,0:T(8,128)(2,1)S(1)} collective-permute-done((bf16[544,512]{1,0:T(8,128)(2,1)S(1)}, bf16[544,512]{1,0:T(8,128)(2,1)S(1)}, u32[]{:S(2)}, u32[]{:S(2)}) %collective-permute-start.4) | collective-permute-done | bytes 557088 | tf_op jit(solution)/shard_map/ppermute | solution.py:67
  50.8 0.2 ride.4
  51.0 0.8 %collective-permute-start.5 = (bf16[288,512]{1,0:T(8,128)(2,1)S(1)}, bf16[288,512]{1,0:T(8,128)(2,1)S(1)}, u32[]{:S(2)}, u32[]{:S(2)}) collective-permute-start(bf16[288,512]{1,0:T(8,128)(2,1)S(1)} %get-tuple-element.110), channel_id=1, source_target_pairs={{0,4},{1,3},{2,6},{3,1},{4,0},{5,7},{6,2},{7,5},{8,12},{9,11},{10,... | collective-permute-start | bytes 884744 | tf_op jit(solution)/shard_map/ppermute | solution.py:67
  51.7 1.3 %collective-permute-start.6 = (bf16[96,512]{1,0:T(8,128)(2,1)S(1)}, bf16[96,512]{1,0:T(8,128)(2,1)S(1)}, u32[]{:S(2)}, u32[]{:S(2)}) collective-permute-start(bf16[96,512]{1,0:T(8,128)(2,1)S(1)} %get-tuple-element.113), channel_id=1, source_target_pairs={{0,8},{1,9},{2,10},{3,11},{4,12},{5,13},{6,14},{7,15},{8,0},{9,1},... | collective-permute-start | bytes 294920 | tf_op jit(solution)/shard_map/ppermute | solution.py:67
  53.1 6.8 %collective-permute-done.5.arrived_ref = bf16[288,512]{1,0:T(8,128)(2,1)S(1)} collective-permute-done((bf16[288,512]{1,0:T(8,128)(2,1)S(1)}, bf16[288,512]{1,0:T(8,128)(2,1)S(1)}, u32[]{:S(2)}, u32[]{:S(2)}) %collective-permute-start.5) | collective-permute-done | bytes 294944 | tf_op jit(solution)/shard_map/ppermute | solution.py:67
  59.8 0.2 ride.5
  60.0 0.0 collective-permute-done.6.came_ref
  60.0 0.5 collective-permute-start.7
  60.5 0.7 node_total.1
  61.2 0.0 copy-done.2
  61.2 0.8 %node.1 = (f32[256,512]{1,0:T(8,128)S(1)}, bf16[32,256]{1,0:T(8,128)(2,1)S(1)}) custom-call(bf16[256,512]{1,0:T(8,128)(2,1)S(1)} %get-tuple-element.117.own_ref, bf16[256,512]{1,0:T(8,128)(2,1)S(1)} %get-tuple-element.118.recv_ref, f32[256,512]{1,0:T(8,128)S(1)} %get-tuple-element.119.part_ref, bf16[512,512]{1,0:T(8,128)(2,1)S(1)} %get-tuple-element.72.w_send.w_send_ref, ...), custom_call_target="tpu_custom_call" | custom-call | flops 1024 | bytes 1024 | tf_op jit(solution)/shard_map/node/pallas_call | solution.py:423
  61.9 3.6 %convolution_convert_fusion = bf16[2048,512]{1,0:T(8,128)(2,1)} fusion(bf16[1024,512]{1,0:T(8,128)(2,1)S(1)} %get-tuple-element.127.da2_ref, bf16[1024,512]{1,0:T(8,128)(2,1)S(1)} %get-tuple-element.126.da1_ref, bf16[1536,512]{1,0:T(8,128)(2,1)} %w_edge_in_far.3), kind=kOutput, calls=%fused_computation | convolution fusion | flops 1078984704 | bytes 4718592 | tf_op jit(solution)/shard_map/dot_general | solution.py:27
  65.6 2.1 %collective-permute-done.7.arrived_ref = bf16[160,512]{1,0:T(8,128)(2,1)S(1)} collective-permute-done((bf16[160,512]{1,0:T(8,128)(2,1)S(1)}, bf16[160,512]{1,0:T(8,128)(2,1)S(1)}, u32[]{:S(2)}, u32[]{:S(2)}) %collective-permute-start.7) | collective-permute-done | bytes 163872 | tf_op jit(solution)/shard_map/ppermute | solution.py:67
  67.7 1.2 %last.1 = (f32[32,512]{1,0:T(8,128)}, f32[96,512]{1,0:T(8,128)}, bf16[256,512]{1,0:T(8,128)(2,1)}) custom-call(bf16[128,512]{1,0:T(8,128)(2,1)S(1)} %get-tuple-element.112.keep_ref, bf16[160,512]{1,0:T(8,128)(2,1)S(1)} %collective-permute-done.7.arrived_ref, bf16[32,256]{1,0:T(8,128)(2,1)S(1)} %get-tuple-element.123.late_pick_ref, ...), custom_call_target="tpu_custom_call" | custom-call | flops 1024 | bytes 1024 | tf_op jit(solution)/shard_map/last/pallas_call | solution.py:423
  (2 shorter events, 0.1 us)
Async XLA Ops:
  2.5 15.3 %all-to-all-start = ((bf16[16,8,512]{2,1,0:T(8,128)(2,1)}), bf16[16,8,512]{2,1,0:T(8,128)(2,1)S(1)}, u32[]{:S(2)}, u32[]{:S(2)}) async-start(bf16[16,8,512]{2,1,0:T(8,128)(2,1)} %bitcast.9), calls=%async_computation | async-start | bytes 262144 | tf_op jit(solution)/shard_map/all_to_all | solution.py:440
  12.4 0.6 copy-start
  26.5 2.4 %collective-permute-start = (bf16[768,512]{1,0:T(8,128)(2,1)S(1)}, bf16[768,512]{1,0:T(8,128)(2,1)S(1)}, u32[]{:S(2)}, u32[]{:S(2)}) collective-permute-start(bf16[768,512]{1,0:T(8,128)(2,1)S(1)} %get-tuple-element.80), channel_id=1, source_target_pairs={{0,1},{1,0},{2,3},{3,2},{4,5},{5,4},{6,7},{7,6},{8,9},{9,8},{10,11... | collective-permute-start | bytes 2359304 | tf_op jit(solution)/shard_map/ppermute | solution.py:67
  29.0 7.8 %collective-permute-start.1 = (bf16[384,512]{1,0:T(8,128)(2,1)S(1)}, bf16[384,512]{1,0:T(8,128)(2,1)S(1)}, u32[]{:S(2)}, u32[]{:S(2)}) collective-permute-start(bf16[384,512]{1,0:T(8,128)(2,1)S(1)} %get-tuple-element.96), channel_id=1, source_target_pairs={{0,2},{1,5},{2,0},{3,7},{4,6},{5,1},{6,4},{7,3},{8,10},{9,13},{10,... | collective-permute-start | bytes 1179656 | tf_op jit(solution)/shard_map/ppermute | solution.py:67
  30.7 9.0 %copy-start.1 = (bf16[3,96,96]{2,1,0:T(8,128)(2,1)S(1)}, bf16[3,96,96]{2,1,0:T(8,128)(2,1)}, u32[]{:S(2)}) copy-start(bf16[3,96,96]{2,1,0:T(8,128)(2,1)} %copy-done) | copy-start | bytes 165892
  36.9 2.8 %collective-permute-start.2 = (bf16[1056,512]{1,0:T(8,128)(2,1)S(1)}, bf16[1056,512]{1,0:T(8,128)(2,1)S(1)}, u32[]{:S(2)}, u32[]{:S(2)}) collective-permute-start(bf16[1056,512]{1,0:T(8,128)(2,1)S(1)} %get-tuple-element.99), channel_id=1, source_target_pairs={{0,1},{1,0},{2,3},{3,2},{4,5},{5,4},{6,7},{7,6},{8,9},{9,8},{10,11... | collective-permute-start | bytes 3244040 | tf_op jit(solution)/shard_map/ppermute | solution.py:67
  39.6 21.5 %copy-start.2 = (bf16[64,256]{1,0:T(8,128)(2,1)S(1)}, bf16[64,256]{1,0:T(8,128)(2,1)}, u32[]{:S(2)}) copy-start(bf16[64,256]{1,0:T(8,128)(2,1)} %get-tuple-element.122.pick_ref) | copy-start | bytes 98308
  39.8 10.9 %collective-permute-start.4 = (bf16[544,512]{1,0:T(8,128)(2,1)S(1)}, bf16[544,512]{1,0:T(8,128)(2,1)S(1)}, u32[]{:S(2)}, u32[]{:S(2)}) collective-permute-start(bf16[544,512]{1,0:T(8,128)(2,1)S(1)} %get-tuple-element.106), channel_id=1, source_target_pairs={{0,2},{1,5},{2,0},{3,7},{4,6},{5,1},{6,4},{7,3},{8,10},{9,13},{10,... | collective-permute-start | bytes 1671176 | tf_op jit(solution)/shard_map/ppermute | solution.py:67
  40.4 7.8 %collective-permute-start.3 = (bf16[192,512]{1,0:T(8,128)(2,1)S(1)}, bf16[192,512]{1,0:T(8,128)(2,1)S(1)}, u32[]{:S(2)}, u32[]{:S(2)}) collective-permute-start(bf16[192,512]{1,0:T(8,128)(2,1)S(1)} %get-tuple-element.104), channel_id=1, source_target_pairs={{0,4},{1,3},{2,6},{3,1},{4,0},{5,7},{6,2},{7,5},{8,12},{9,11},{10,... | collective-permute-start | bytes 589832 | tf_op jit(solution)/shard_map/ppermute | solution.py:67
  51.0 8.9 %collective-permute-start.5 = (bf16[288,512]{1,0:T(8,128)(2,1)S(1)}, bf16[288,512]{1,0:T(8,128)(2,1)S(1)}, u32[]{:S(2)}, u32[]{:S(2)}) collective-permute-start(bf16[288,512]{1,0:T(8,128)(2,1)S(1)} %get-tuple-element.110), channel_id=1, source_target_pairs={{0,4},{1,3},{2,6},{3,1},{4,0},{5,7},{6,2},{7,5},{8,12},{9,11},{10,... | collective-permute-start | bytes 884744 | tf_op jit(solution)/shard_map/ppermute | solution.py:67
  51.7 8.3 %collective-permute-start.6 = (bf16[96,512]{1,0:T(8,128)(2,1)S(1)}, bf16[96,512]{1,0:T(8,128)(2,1)S(1)}, u32[]{:S(2)}, u32[]{:S(2)}) collective-permute-start(bf16[96,512]{1,0:T(8,128)(2,1)S(1)} %get-tuple-element.113), channel_id=1, source_target_pairs={{0,8},{1,9},{2,10},{3,11},{4,12},{5,13},{6,14},{7,15},{8,0},{9,1},... | collective-permute-start | bytes 294920 | tf_op jit(solution)/shard_map/ppermute | solution.py:67
  60.0 7.7 %collective-permute-start.7 = (bf16[160,512]{1,0:T(8,128)(2,1)S(1)}, bf16[160,512]{1,0:T(8,128)(2,1)S(1)}, u32[]{:S(2)}, u32[]{:S(2)}) collective-permute-start(bf16[160,512]{1,0:T(8,128)(2,1)S(1)} %get-tuple-element.115), channel_id=1, source_target_pairs={{0,8},{1,9},{2,10},{3,11},{4,12},{5,13},{6,14},{7,15},{8,0},{9,1},... | collective-permute-start | bytes 491528 | tf_op jit(solution)/shard_map/ppermute | solution.py:67

commit v6 on v5

--- a/solution.py
+++ b/solution.py
@@ -109,7 +109,7 @@
     return jnp.where(lax.broadcasted_iota(jnp.int32, shape, 1) == place * slot + row, 1.0, 0.0).astype(BF16)
 
 
-def put_blocks(sources, me, count, keep_ref, send_ref):
+def put_blocks(sources, me, count, keep_ref, *send_refs):
     shares = [source.shape[0] // count for source in sources]
     half = count // 2
     size = keep_ref.shape[0] // half
@@ -126,8 +126,10 @@
         ]
         if spare:
             parts.append(jnp.zeros((spare, keep_ref.shape[1]), F32))
-        start = place % half * size
-        (keep_ref if place < half else send_ref)[start : start + size] = jnp.concatenate(parts, axis=0).astype(BF16)
+        each = half // len(send_refs)
+        ref = keep_ref if place < half else send_refs[(place - half) // each]
+        start = (place if place < half else place % each) * size
+        ref[start : start + size] = jnp.concatenate(parts, axis=0).astype(BF16)
 
 
 def pick_kernel(count, picks_ref, nodes_ref, pick_ref, rows_ref):
@@ -308,7 +310,10 @@
     da1_ref,
     da2_ref,
     keep_ref,
-    away_ref,
+    away1_ref,
+    away2_ref,
+    away3_ref,
+    away4_ref,
     own_ref,
     recv_sums_ref,
     far_ref,
@@ -335,7 +340,7 @@
     own_ref[...] = own
     recv_sums_ref[...] = recv
     far_ref[...] = far
-    away_ref[keep_ref.shape[0] :] = far[n_far // 2 :]
+    away4_ref[away3_ref.shape[0] :] = far[n_far // 2 :]
     shape = (n_far, count * HALO_ROWS)
     column = lax.broadcasted_iota(jnp.int32, shape, 1)
     device = column // HALO_ROWS
@@ -350,7 +355,7 @@
         grads_ei[cols] = mm_rows(edges1_ref[:, cols], da1_ref[...]) + mm_rows(edges2_ref[:, cols], da2_ref[...])
     grads_ei[width : 2 * width] = mm_rows(nodes, own) + mm_rows(halo, far)
     grads_ei[2 * width :] = mm_rows(nodes, recv)
-    put_blocks((grads_eo, grads_ei), me, count, keep_ref, away_ref)
+    put_blocks((grads_eo, grads_ei), me, count, keep_ref, away1_ref, away2_ref, away3_ref, away4_ref)
 
 
 def move_rows(step, count, slot):
@@ -364,11 +369,20 @@
     return jnp.concatenate([mm(take_rows(step + 1, count, slot), after).astype(BF16), after], axis=0)
 
 
-def ride_kernel(step, keep_ref, arrived_ref, far_ref, moves_ref, next_keep_ref, next_away_ref, next_far_ref):
+def ride_kernel(step, pieces, keep_ref, far_ref, *refs):
+    arrived_refs, (moves_ref, next_keep_ref, next_away_ref, next_far_ref) = refs[:pieces], refs[pieces:]
     size, half = keep_ref.shape[0], next_keep_ref.shape[0]
-    moved = mm(moves_ref[step], jnp.concatenate([far_ref[...], arrived_ref[size:]], axis=0)).astype(BF16)
-    next_keep_ref[...] = keep_ref[:half] + arrived_ref[:half]
-    next_away_ref[:half] = keep_ref[half:] + arrived_ref[half:size]
+    each = size // pieces
+    moved = mm(moves_ref[step], jnp.concatenate([far_ref[...], arrived_refs[-1][each:]], axis=0)).astype(BF16)
+    for i, ref in enumerate(arrived_refs):
+        start = i * each
+        stop = start + each
+        near = min(stop, half)
+        if start < half:
+            next_keep_ref[start:near] = keep_ref[start:near] + ref[: near - start]
+        if stop > half:
+            first = max(start, half)
+            next_away_ref[first - half : stop - half] = keep_ref[first:stop] + ref[first - start : each]
     split = moved.shape[0] - next_far_ref.shape[0]
     next_away_ref[half:] = moved[:split]
     next_far_ref[...] = moved[split:]
@@ -513,9 +527,8 @@
     def ride(step, keep, arrived, far):
         half = keep.shape[0] // 2
         outs = [space(half, width), space(half + n_far // 2, width), space(n_far, width)]
-        return kernel_call(
-            functools.partial(ride_kernel, step), "ride", outs, [], (keep, arrived, far), (moves,), limit=8
-        )
+        kernel = functools.partial(ride_kernel, step, len(arrived))
+        return kernel_call(kernel, "ride", outs, [], (keep, far, *arrived), (moves,), limit=8)
 
     came1 = cube_permute(away1, 0, count)
     halves = [half_rows] * 2
@@ -527,24 +540,23 @@
     came1 = cube_permute(away1, 1, count)
     args = (receiver, zeta, slope, normed, inv, dagg, near_out)
     dye2, da2 = kernel_call(functools.partial(backward_kernel, n_edges // 2), "backward", halves, [], (), args)
-    keep2, away2, own_sums, recv_sums, far_sums = kernel_call(
+    keep_shape = block_pair(4)[0]
+    piece_shapes = [space(keep_shape.shape[0] // 4 + riders, width) for riders in (0, 0, 0, n_far // 2)]
+    keep2, *pieces, own_sums, recv_sums, far_sums = kernel_call(
         functools.partial(weights_kernel, count, slot),
         "weights",
-        block_pair(4, n_far // 2) + [space(owned, width), space(owned, width), space(n_far, width)],
+        [keep_shape, *piece_shapes, space(owned, width), space(owned, width), space(n_far, width)],
         [space(r, width, dtype=F32) for r in (2 * owned + -(-n_far // LANES) * LANES, width, 3 * width)],
         (halo,),
         (sender, receiver, near_nodes, edges1, edges2, zeta, dye1, dye2, da1, da2),
     )
+    came2 = [cube_permute(piece, 0, count) for piece in pieces]
     for step in range(1, steps - 1):
         keep1, away1 = add(keep1, came1)
-        if step == 1:
-            away1, away2 = in_order(away1, away2)
-            came2 = cube_permute(away2, 0, count)
-        else:
-            away1, came2 = in_order(away1, came2)
+        away1, came2 = in_order(away1, came2)
         came1 = cube_permute(away1, step + 1, count)
         keep2, away2, far_sums = ride(step - 1, keep2, came2, far_sums)
-        came2 = cube_permute(away2, step, count)
+        came2 = [cube_permute(away2, step, count)]
     keep2, away2, far_sums = ride(steps - 2, keep2, came2, far_sums)
     came1, away2 = in_order(came1, away2)
     _, (da1, da2, own_sums) = in_order(away2, (da1, da2, own_sums))

time: 69.2 us -> 68.8 us (level)
  waiting for transfers between devices: 29 us -> 25.3 us
  starting transfers between devices: 10.7 us -> 13.9 us
    ppermute x8 -> x11, waiting for transfers between devices: 24.2 us -> 20.5 us  [cube_permute(): return lax.ppermute(blocks, 'patch', pairs)]
    ppermute x8 -> x11, starting transfers between devices: 3.29 us -> 6.54 us  [cube_permute(): return lax.ppermute(blocks, 'patch', pairs)]
  transfers between devices with their start and end apart: 9 -> 12, of which waited for: 8 -> 10; matrix products, arithmetic and copies ran while one was open for 5% -> 5% of each run, Pallas kernels for 17% -> 17%
where the time goes in v6:
time: 68.8 us; the launch traced here: 68.4 us
  waiting for transfers between devices  25.3 us (37%)
  Pallas kernels  24.2 us (35%)
  starting transfers between devices  13.9 us (20%)
  matrix products  3.65 us (5%)
  between operations  0.76 us (1%)
    pallas_call x15, Pallas kernels, kernel_call(): pl.pallas_call(kernel, out_shape=tuple(outs), in_specs=specs, out_specs=(...  24.2 us
    ppermute x11, waiting for transfers between devices, cube_permute(): return lax.ppermute(blocks, 'patch', pairs)  20.5 us
    all_to_all x1, starting transfers between devices, trade(): lax.all_to_all(rows, 'patch', split_axis=0, concat_axis=0, tiled=True)  7.38 us
    ppermute x11, starting transfers between devices, cube_permute(): return lax.ppermute(blocks, 'patch', pairs)  6.54 us
    all_to_all x1, waiting for transfers between devices, trade(): lax.all_to_all(rows, 'patch', split_axis=0, concat_axis=0, tiled=True)  4.83 us
    dot_general x1, matrix products, mm_cols(): lax.dot_general(left, right, (((1,), (1,)), ((), ())), preferred_element_...  3.65 us
  transfers between devices with their start and end apart: 12, of which 10 were waited for; matrix products, arithmetic and copies ran while one was open for 5% of the time, Pallas kernels for 17%

profile of v6, /device:TPU:0, one launch (start us, length us, event | category | flops | bytes accessed | tf_op | source)
XLA Modules:
  0.0 68.4 jit_solution(17789432370519313605)
XLA Ops:
  0.6 1.9 %pick.1 = (bf16[64,256]{1,0:T(8,128)(2,1)}, bf16[128,512]{1,0:T(8,128)(2,1)}) custom-call(s32[4,16]{1,0:T(4,128)} %bitcast.12, bf16[256,512]{1,0:T(8,128)(2,1)} %nodes_far.1), custom_call_target="tpu_custom_call" | custom-call | flops 1024 | bytes 1024 | tf_op jit(solution)/shard_map/pick/pallas_call | solution.py:437
  2.5 7.4 %all-to-all-start = ((bf16[16,8,512]{2,1,0:T(8,128)(2,1)}), bf16[16,8,512]{2,1,0:T(8,128)(2,1)S(1)}, u32[]{:S(2)}, u32[]{:S(2)}) async-start(bf16[16,8,512]{2,1,0:T(8,128)(2,1)} %bitcast.9), calls=%async_computation | async-start | bytes 262144 | tf_op jit(solution)/shard_map/all_to_all | solution.py:454
  9.9 2.5 %local.1 = (bf16[256,512]{1,0:T(8,128)(2,1)S(1)}, bf16[512,512]{1,0:T(8,128)(2,1)S(1)}, bf16[512,512]{1,0:T(8,128)(2,1)S(1)}, bf16[1024,512]{1,0:T(8,128)(2,1)S(...) custom-call(bf16[256,512]{1,0:T(8,128)(2,1)} %nodes_far.1, bf16[1536,512]{1,0:T(8,128)(2,1)} %w_edge_in_far.3, ...), custom_call_target="tpu_custom_call" | custom-call | flops 1024 | bytes 1024 | tf_op jit(solution)/shard_map/local/pallas_call | solution.py:437
  12.4 0.0 copy-start
  12.4 0.6 copy-done
  13.0 4.8 %all-to-all-done = bf16[16,8,512]{2,1,0:T(8,128)(2,1)S(1)} async-done(((bf16[16,8,512]{2,1,0:T(8,128)(2,1)}), bf16[16,8,512]{2,1,0:T(8,128)(2,1)S(1)}, u32[]{:S(2)}, u32[]{:S(2)}) %all-to-all-start) | async-done | bytes 131104 | tf_op jit(solution)/shard_map/all_to_all | solution.py:454
  17.8 8.7 %forward.1 = (bf16[768,512]{1,0:T(8,128)(2,1)S(1)}, bf16[768,512]{1,0:T(8,128)(2,1)S(1)}, bf16[2048,512]{1,0:T(8,128)(2,1)S(1)}, bf16[2048,512]{1,0:T(8,128)(2,1...) custom-call(bf16[128,512]{1,0:T(8,128)(2,1)S(1)} %bitcast.7, ...), custom_call_target="tpu_custom_call" | custom-call | flops 1024 | bytes 1024 | tf_op jit(solution)/shard_map/forward/pallas_call | solution.py:437
  26.5 0.1 collective-permute-start
  26.6 1.6 %backward.2 = (bf16[1024,512]{1,0:T(8,128)(2,1)S(1)}, bf16[1024,512]{1,0:T(8,128)(2,1)S(1)}) custom-call(s32[1,2048]{1,0:T(1,128)S(1)} %get-tuple-element.83.recv_ref, bf16[2048,512]{1,0:T(8,128)(2,1)S(1)} %get-tuple-element.85.zeta_ref, bf16[2048,512]{1,0:T(8,128)(2,1)S(1)} %get-tuple-element.87.slope_ref, ...), custom_call_target="tpu_custom_call" | custom-call | flops 1024 | bytes 1024 | tf_op jit(solution)/shard_map/backward/pallas_call | solution.py:437
  28.3 0.6 collective-permute-done.arrived_ref
  28.9 0.1 add.3
  29.0 0.1 collective-permute-start.1
  29.1 1.6 %backward.3 = (bf16[1024,512]{1,0:T(8,128)(2,1)S(1)}, bf16[1024,512]{1,0:T(8,128)(2,1)S(1)}) custom-call(s32[1,2048]{1,0:T(1,128)S(1)} %get-tuple-element.83.recv_ref, bf16[2048,512]{1,0:T(8,128)(2,1)S(1)} %get-tuple-element.85.zeta_ref, bf16[2048,512]{1,0:T(8,128)(2,1)S(1)} %get-tuple-element.87.slope_ref, ...), custom_call_target="tpu_custom_call" | custom-call | flops 1024 | bytes 1024 | tf_op jit(solution)/shard_map/backward/pallas_call | solution.py:437
  30.7 0.0 copy-start.1
  30.7 4.5 %weights.1 = (bf16[1024,512]{1,0:T(8,128)(2,1)S(1)}, bf16[256,512]{1,0:T(8,128)(2,1)S(1)}, bf16[256,512]{1,0:T(8,128)(2,1)S(1)}, bf16[256,512]{1,0:T(8,128)(2,1)...) custom-call(bf16[128,512]{1,0:T(8,128)(2,1)S(1)} %bitcast.8, ...), custom_call_target="tpu_custom_call" | custom-call | flops 1024 | bytes 1024 | tf_op jit(solution)/shard_map/weights/pallas_call | solution.py:437
  35.2 0.2 collective-permute-start.5
  35.4 0.4 collective-permute-start.2
  35.8 0.1 collective-permute-start.3
  36.0 0.4 collective-permute-start.4
  36.3 0.5 collective-permute-done.1.arrived_ref
  36.9 0.4 collective-permute-done.2.refs_0_
  37.3 0.4 collective-permute-done.3.refs_1_
  37.6 0.4 collective-permute-done.4.refs_2_
  38.0 0.0 collective-permute-done.5.refs_3_
  38.0 0.0 copy-done.1
  38.0 0.0 copy-start.2
  38.0 0.2 ride.3
  38.2 2.1 %collective-permute-start.7 = (bf16[544,512]{1,0:T(8,128)(2,1)S(1)}, bf16[544,512]{1,0:T(8,128)(2,1)S(1)}, u32[]{:S(2)}, u32[]{:S(2)}) collective-permute-start(bf16[544,512]{1,0:T(8,128)(2,1)S(1)} %get-tuple-element.119), channel_id=1, source_target_pairs={{0,2},{1,5},{2,0},{3,7},{4,6},{5,1},{6,4},{7,3},{8,10},{9,13},{10,... | collective-permute-start | bytes 1671176 | tf_op jit(solution)/shard_map/ppermute | solution.py:67
  40.3 0.0 collective-permute-start.6
  40.3 7.8 %collective-permute-done.6.arrived_ref = bf16[192,512]{1,0:T(8,128)(2,1)S(1)} collective-permute-done((bf16[192,512]{1,0:T(8,128)(2,1)S(1)}, bf16[192,512]{1,0:T(8,128)(2,1)S(1)}, u32[]{:S(2)}, u32[]{:S(2)}) %collective-permute-start.6) | collective-permute-done | bytes 196640 | tf_op jit(solution)/shard_map/ppermute | solution.py:67
  48.2 1.8 %collective-permute-done.7.refs_0_ = bf16[544,512]{1,0:T(8,128)(2,1)S(1)} collective-permute-done((bf16[544,512]{1,0:T(8,128)(2,1)S(1)}, bf16[544,512]{1,0:T(8,128)(2,1)S(1)}, u32[]{:S(2)}, u32[]{:S(2)}) %collective-permute-start.7) | collective-permute-done | bytes 557088 | tf_op jit(solution)/shard_map/ppermute | solution.py:67
  49.9 0.2 ride.4
  50.1 1.2 %collective-permute-start.8 = (bf16[288,512]{1,0:T(8,128)(2,1)S(1)}, bf16[288,512]{1,0:T(8,128)(2,1)S(1)}, u32[]{:S(2)}, u32[]{:S(2)}) collective-permute-start(bf16[288,512]{1,0:T(8,128)(2,1)S(1)} %get-tuple-element.123), channel_id=1, source_target_pairs={{0,4},{1,3},{2,6},{3,1},{4,0},{5,7},{6,2},{7,5},{8,12},{9,11},{10,... | collective-permute-start | bytes 884744 | tf_op jit(solution)/shard_map/ppermute | solution.py:67
  51.3 0.8 %collective-permute-start.9 = (bf16[96,512]{1,0:T(8,128)(2,1)S(1)}, bf16[96,512]{1,0:T(8,128)(2,1)S(1)}, u32[]{:S(2)}, u32[]{:S(2)}) collective-permute-start(bf16[96,512]{1,0:T(8,128)(2,1)S(1)} %get-tuple-element.125), channel_id=1, source_target_pairs={{0,8},{1,9},{2,10},{3,11},{4,12},{5,13},{6,14},{7,15},{8,0},{9,1},... | collective-permute-start | bytes 294920 | tf_op jit(solution)/shard_map/ppermute | solution.py:67
  52.1 6.9 %collective-permute-done.8.refs_0_ = bf16[288,512]{1,0:T(8,128)(2,1)S(1)} collective-permute-done((bf16[288,512]{1,0:T(8,128)(2,1)S(1)}, bf16[288,512]{1,0:T(8,128)(2,1)S(1)}, u32[]{:S(2)}, u32[]{:S(2)}) %collective-permute-start.8) | collective-permute-done | bytes 294944 | tf_op jit(solution)/shard_map/ppermute | solution.py:67
  59.0 0.2 ride.5
  59.1 0.0 collective-permute-done.9.came_ref
  59.1 1.2 %collective-permute-start.10 = (bf16[160,512]{1,0:T(8,128)(2,1)S(1)}, bf16[160,512]{1,0:T(8,128)(2,1)S(1)}, u32[]{:S(2)}, u32[]{:S(2)}) collective-permute-start(bf16[160,512]{1,0:T(8,128)(2,1)S(1)} %get-tuple-element.127), channel_id=1, source_target_pairs={{0,8},{1,9},{2,10},{3,11},{4,12},{5,13},{6,14},{7,15},{8,0},{9,1},... | collective-permute-start | bytes 491528 | tf_op jit(solution)/shard_map/ppermute | solution.py:67
  60.4 0.7 %node_total.1 = (f32[32,512]{1,0:T(8,128)}, f32[64,512]{1,0:T(8,128)}) custom-call(bf16[96,512]{1,0:T(8,128)(2,1)S(1)} %get-tuple-element.142.kept_ref, bf16[96,512]{1,0:T(8,128)(2,1)S(1)} %collective-permute-done.9.came_ref), custom_call_target="tpu_custom_call" | custom-call | flops 1024 | bytes 1024 | tf_op jit(solution)/shard_map/node_total/pallas_call | solution.py:437
  61.1 0.0 copy-done.2
  61.1 0.8 %node.1 = (f32[256,512]{1,0:T(8,128)S(1)}, bf16[32,256]{1,0:T(8,128)(2,1)S(1)}) custom-call(bf16[256,512]{1,0:T(8,128)(2,1)S(1)} %get-tuple-element.129.own_ref, bf16[256,512]{1,0:T(8,128)(2,1)S(1)} %get-tuple-element.130.recv_ref, f32[256,512]{1,0:T(8,128)S(1)} %get-tuple-element.131.part_ref, bf16[512,512]{1,0:T(8,128)(2,1)S(1)} %get-tuple-element.78.w_send.w_send_ref, ...), custom_call_target="tpu_custom_call" | custom-call | flops 1024 | bytes 1024 | tf_op jit(solution)/shard_map/node/pallas_call | solution.py:437
  61.8 3.6 %convolution_convert_fusion = bf16[2048,512]{1,0:T(8,128)(2,1)} fusion(bf16[1024,512]{1,0:T(8,128)(2,1)S(1)} %get-tuple-element.139.da2_ref, bf16[1024,512]{1,0:T(8,128)(2,1)S(1)} %get-tuple-element.138.da1_ref, bf16[1536,512]{1,0:T(8,128)(2,1)} %w_edge_in_far.3), kind=kOutput, calls=%fused_computation | convolution fusion | flops 1078984704 | bytes 4718592 | tf_op jit(solution)/shard_map/dot_general | solution.py:27
  65.5 1.7 %collective-permute-done.10.arrived_ref = bf16[160,512]{1,0:T(8,128)(2,1)S(1)} collective-permute-done((bf16[160,512]{1,0:T(8,128)(2,1)S(1)}, bf16[160,512]{1,0:T(8,128)(2,1)S(1)}, u32[]{:S(2)}, u32[]{:S(2)}) %collective-permute-start.10) | collective-permute-done | bytes 163872 | tf_op jit(solution)/shard_map/ppermute | solution.py:67
  67.2 1.2 %last.1 = (f32[32,512]{1,0:T(8,128)}, f32[96,512]{1,0:T(8,128)}, bf16[256,512]{1,0:T(8,128)(2,1)}) custom-call(bf16[128,512]{1,0:T(8,128)(2,1)S(1)} %get-tuple-element.124.keep_ref, bf16[160,512]{1,0:T(8,128)(2,1)S(1)} %collective-permute-done.10.arrived_ref, bf16[32,256]{1,0:T(8,128)(2,1)S(1)} %get-tuple-element.135.late_pick_ref, ...), custom_call_target="tpu_custom_call" | custom-call | flops 1024 | bytes 1024 | tf_op jit(solution)/shard_map/last/pallas_call | solution.py:437
  (2 shorter events, 0.1 us)
Async XLA Ops:
  2.5 15.3 %all-to-all-start = ((bf16[16,8,512]{2,1,0:T(8,128)(2,1)}), bf16[16,8,512]{2,1,0:T(8,128)(2,1)S(1)}, u32[]{:S(2)}, u32[]{:S(2)}) async-start(bf16[16,8,512]{2,1,0:T(8,128)(2,1)} %bitcast.9), calls=%async_computation | async-start | bytes 262144 | tf_op jit(solution)/shard_map/all_to_all | solution.py:454
  12.4 0.6 copy-start
  26.5 2.4 %collective-permute-start = (bf16[768,512]{1,0:T(8,128)(2,1)S(1)}, bf16[768,512]{1,0:T(8,128)(2,1)S(1)}, u32[]{:S(2)}, u32[]{:S(2)}) collective-permute-start(bf16[768,512]{1,0:T(8,128)(2,1)S(1)} %get-tuple-element.86), channel_id=1, source_target_pairs={{0,1},{1,0},{2,3},{3,2},{4,5},{5,4},{6,7},{7,6},{8,9},{9,8},{10,11... | collective-permute-start | bytes 2359304 | tf_op jit(solution)/shard_map/ppermute | solution.py:67
  29.0 7.8 %collective-permute-start.1 = (bf16[384,512]{1,0:T(8,128)(2,1)S(1)}, bf16[384,512]{1,0:T(8,128)(2,1)S(1)}, u32[]{:S(2)}, u32[]{:S(2)}) collective-permute-start(bf16[384,512]{1,0:T(8,128)(2,1)S(1)} %get-tuple-element.103), channel_id=1, source_target_pairs={{0,2},{1,5},{2,0},{3,7},{4,6},{5,1},{6,4},{7,3},{8,10},{9,13},{10,... | collective-permute-start | bytes 1179656 | tf_op jit(solution)/shard_map/ppermute | solution.py:67
  30.7 7.3 %copy-start.1 = (bf16[3,96,96]{2,1,0:T(8,128)(2,1)S(1)}, bf16[3,96,96]{2,1,0:T(8,128)(2,1)}, u32[]{:S(2)}) copy-start(bf16[3,96,96]{2,1,0:T(8,128)(2,1)} %copy-done) | copy-start | bytes 165892
  35.2 2.8 %collective-permute-start.5 = (bf16[288,512]{1,0:T(8,128)(2,1)S(1)}, bf16[288,512]{1,0:T(8,128)(2,1)S(1)}, u32[]{:S(2)}, u32[]{:S(2)}) collective-permute-start(bf16[288,512]{1,0:T(8,128)(2,1)S(1)} %get-tuple-element.108), channel_id=1, source_target_pairs={{0,1},{1,0},{2,3},{3,2},{4,5},{5,4},{6,7},{7,6},{8,9},{9,8},{10,11... | collective-permute-start | bytes 884744 | tf_op jit(solution)/shard_map/ppermute | solution.py:67
  35.4 1.8 %collective-permute-start.2 = (bf16[256,512]{1,0:T(8,128)(2,1)S(1)}, bf16[256,512]{1,0:T(8,128)(2,1)S(1)}, u32[]{:S(2)}, u32[]{:S(2)}) collective-permute-start(bf16[256,512]{1,0:T(8,128)(2,1)S(1)} %get-tuple-element.105), channel_id=1, source_target_pairs={{0,1},{1,0},{2,3},{3,2},{4,5},{5,4},{6,7},{7,6},{8,9},{9,8},{10,11... | collective-permute-start | bytes 786440 | tf_op jit(solution)/shard_map/ppermute | solution.py:67
  35.8 1.8 %collective-permute-start.3 = (bf16[256,512]{1,0:T(8,128)(2,1)S(1)}, bf16[256,512]{1,0:T(8,128)(2,1)S(1)}, u32[]{:S(2)}, u32[]{:S(2)}) collective-permute-start(bf16[256,512]{1,0:T(8,128)(2,1)S(1)} %get-tuple-element.106), channel_id=1, source_target_pairs={{0,1},{1,0},{2,3},{3,2},{4,5},{5,4},{6,7},{7,6},{8,9},{9,8},{10,11... | collective-permute-start | bytes 786440 | tf_op jit(solution)/shard_map/ppermute | solution.py:67
  36.0 2.1 %collective-permute-start.4 = (bf16[256,512]{1,0:T(8,128)(2,1)S(1)}, bf16[256,512]{1,0:T(8,128)(2,1)S(1)}, u32[]{:S(2)}, u32[]{:S(2)}) collective-permute-start(bf16[256,512]{1,0:T(8,128)(2,1)S(1)} %get-tuple-element.107), channel_id=1, source_target_pairs={{0,1},{1,0},{2,3},{3,2},{4,5},{5,4},{6,7},{7,6},{8,9},{9,8},{10,11... | collective-permute-start | bytes 786440 | tf_op jit(solution)/shard_map/ppermute | solution.py:67
  38.0 23.0 %copy-start.2 = (bf16[64,256]{1,0:T(8,128)(2,1)S(1)}, bf16[64,256]{1,0:T(8,128)(2,1)}, u32[]{:S(2)}) copy-start(bf16[64,256]{1,0:T(8,128)(2,1)} %get-tuple-element.134.pick_ref) | copy-start | bytes 98308
  38.2 11.7 %collective-permute-start.7 = (bf16[544,512]{1,0:T(8,128)(2,1)S(1)}, bf16[544,512]{1,0:T(8,128)(2,1)S(1)}, u32[]{:S(2)}, u32[]{:S(2)}) collective-permute-start(bf16[544,512]{1,0:T(8,128)(2,1)S(1)} %get-tuple-element.119), channel_id=1, source_target_pairs={{0,2},{1,5},{2,0},{3,7},{4,6},{5,1},{6,4},{7,3},{8,10},{9,13},{10,... | collective-permute-start | bytes 1671176 | tf_op jit(solution)/shard_map/ppermute | solution.py:67
  40.3 7.8 %collective-permute-start.6 = (bf16[192,512]{1,0:T(8,128)(2,1)S(1)}, bf16[192,512]{1,0:T(8,128)(2,1)S(1)}, u32[]{:S(2)}, u32[]{:S(2)}) collective-permute-start(bf16[192,512]{1,0:T(8,128)(2,1)S(1)} %get-tuple-element.117), channel_id=1, source_target_pairs={{0,4},{1,3},{2,6},{3,1},{4,0},{5,7},{6,2},{7,5},{8,12},{9,11},{10,... | collective-permute-start | bytes 589832 | tf_op jit(solution)/shard_map/ppermute | solution.py:67
  50.1 8.9 %collective-permute-start.8 = (bf16[288,512]{1,0:T(8,128)(2,1)S(1)}, bf16[288,512]{1,0:T(8,128)(2,1)S(1)}, u32[]{:S(2)}, u32[]{:S(2)}) collective-permute-start(bf16[288,512]{1,0:T(8,128)(2,1)S(1)} %get-tuple-element.123), channel_id=1, source_target_pairs={{0,4},{1,3},{2,6},{3,1},{4,0},{5,7},{6,2},{7,5},{8,12},{9,11},{10,... | collective-permute-start | bytes 884744 | tf_op jit(solution)/shard_map/ppermute | solution.py:67
  51.3 7.8 %collective-permute-start.9 = (bf16[96,512]{1,0:T(8,128)(2,1)S(1)}, bf16[96,512]{1,0:T(8,128)(2,1)S(1)}, u32[]{:S(2)}, u32[]{:S(2)}) collective-permute-start(bf16[96,512]{1,0:T(8,128)(2,1)S(1)} %get-tuple-element.125), channel_id=1, source_target_pairs={{0,8},{1,9},{2,10},{3,11},{4,12},{5,13},{6,14},{7,15},{8,0},{9,1},... | collective-permute-start | bytes 294920 | tf_op jit(solution)/shard_map/ppermute | solution.py:67
  59.1 8.1 %collective-permute-start.10 = (bf16[160,512]{1,0:T(8,128)(2,1)S(1)}, bf16[160,512]{1,0:T(8,128)(2,1)S(1)}, u32[]{:S(2)}, u32[]{:S(2)}) collective-permute-start(bf16[160,512]{1,0:T(8,128)(2,1)S(1)} %get-tuple-element.127), channel_id=1, source_target_pairs={{0,8},{1,9},{2,10},{3,11},{4,12},{5,13},{6,14},{7,15},{8,0},{9,1},... | collective-permute-start | bytes 491528 | tf_op jit(solution)/shard_map/ppermute | solution.py:67

commit v7 on v6

--- a/solution.py
+++ b/solution.py
@@ -132,24 +132,22 @@
         ref[start : start + size] = jnp.concatenate(parts, axis=0).astype(BF16)
 
 
-def pick_kernel(count, picks_ref, nodes_ref, pick_ref, rows_ref):
-    slot = picks_ref.shape[0]
-    owned = nodes_ref.shape[0]
-    me = lax.axis_index("patch")
-
-    def choose(rows, start):
-        shape = (rows, count)
-        row = lax.broadcasted_iota(jnp.int32, shape, 0)
-        first = start(lax.broadcasted_iota(jnp.int32, shape, 1))
-        ids = jnp.zeros(shape, jnp.int32)
-        for place in range(slot):
-            ids = ids + jnp.where(row == first + place, picks_ref[place : place + 1] + 1, 0)
-        ids = jnp.sum(ids.astype(F32), axis=1, keepdims=True).astype(jnp.int32) - 1
-        node = lax.broadcasted_iota(jnp.int32, (rows, owned), 1)
-        return jnp.where(node == ids, 1.0, 0.0).astype(BF16)
-
-    rows_ref[...] = mm(choose(count * HALO_ROWS, lambda device: device * HALO_ROWS), nodes_ref[...]).astype(BF16)
-    pick_ref[...] = choose(count * slot, lambda device: cube_place(device ^ me, me & 1, count) * slot)
+def choose_rows(picks_ref, rows, owned, start):
+    slot, count = picks_ref.shape
+    shape = (rows, count)
+    row = lax.broadcasted_iota(jnp.int32, shape, 0)
+    first = start(lax.broadcasted_iota(jnp.int32, shape, 1))
+    ids = jnp.zeros(shape, jnp.int32)
+    for place in range(slot):
+        ids = ids + jnp.where(row == first + place, picks_ref[place : place + 1] + 1, 0)
+    ids = jnp.sum(ids.astype(F32), axis=1, keepdims=True).astype(jnp.int32) - 1
+    node = lax.broadcasted_iota(jnp.int32, (rows, owned), 1)
+    return jnp.where(node == ids, 1.0, 0.0).astype(BF16)
+
+
+def pick_kernel(picks_ref, nodes_ref, rows_ref):
+    chosen = choose_rows(picks_ref, rows_ref.shape[0], nodes_ref.shape[0], lambda device: device * HALO_ROWS)
+    rows_ref[...] = mm(chosen, nodes_ref[...]).astype(BF16)
 
 
 def local_kernel(
@@ -389,12 +387,16 @@
 
 
 def node_kernel(
-    step, count, slot, own_ref, recv_ref, part_ref, w_send_ref, w_recv_ref, far_ref, pick_ref, out_ref, late_pick_ref
+    step, count, slot, own_ref, recv_ref, part_ref, w_send_ref, w_recv_ref, far_ref, picks_ref, out_ref, late_pick_ref
 ):
+    me = lax.axis_index("patch")
     take = take_rows(step, count, slot)
-    stays = mm_rows(take, jnp.ones((take.shape[0], pick_ref.shape[1]), BF16)) == 0.0
-    early_pick = jnp.where(stays, pick_ref[...], jnp.zeros_like(pick_ref[...]))
-    late_pick_ref[...] = mm(take, pick_ref[...]).astype(BF16)
+    pick = choose_rows(
+        picks_ref, count * slot, own_ref.shape[0], lambda device: cube_place(device ^ me, me & 1, count) * slot
+    )
+    stays = mm_rows(take, jnp.ones((take.shape[0], pick.shape[1]), BF16)) == 0.0
+    early_pick = jnp.where(stays, pick, jnp.zeros_like(pick))
+    late_pick_ref[...] = mm(take, pick).astype(BF16)
     own = own_ref[...].astype(F32) + mm_rows(early_pick, far_ref[...])
     out_ref[...] = (
         part_ref[...] + mm_cols(own.astype(BF16), w_send_ref[...]) + mm_cols(recv_ref[...], w_recv_ref[...])
@@ -484,14 +486,10 @@
 
     n_far = count * slot
     steps = count.bit_length() - 1
-    pick, halo_out = kernel_call(
-        functools.partial(pick_kernel, count),
-        "pick",
-        [jax.ShapeDtypeStruct((n_far, owned), BF16), jax.ShapeDtypeStruct((n_halo, width), BF16)],
-        [],
-        (send_rows[0].T, nodes),
-        limit=60,
-    )
+    picks = send_rows[0].T
+    halo_out = kernel_call(
+        pick_kernel, "pick", [jax.ShapeDtypeStruct((n_halo, width), BF16)], [], (picks, nodes), limit=60
+    )[0]
     halo = trade(halo_out)
     rows, square, ids = space(n_edges, width), space(width, width), space(1, n_edges, dtype=jnp.int32)
     half_rows = space(n_edges // 2, width)
@@ -567,7 +565,7 @@
         "node",
         [space(owned, width, dtype=F32), space(n_far // 2, owned)],
         [],
-        (own_sums, recv_sums, node_part, w_send, w_recv, far_sums, pick),
+        (own_sums, recv_sums, node_part, w_send, w_recv, far_sums, picks),
     )
 
     def whole(*parts):

time: 68.8 us -> 68.8 us (level)
  no operation moved by 1% of the time
where the time goes in v7:
time: 68.8 us; the launch traced here: 68.4 us
  waiting for transfers between devices  25.3 us (37%)
  Pallas kernels  24.2 us (35%)
  starting transfers between devices  13.9 us (20%)
  matrix products  3.65 us (5%)
  between operations  0.76 us (1%)
    pallas_call x15, Pallas kernels, kernel_call(): pl.pallas_call(kernel, out_shape=tuple(outs), in_specs=specs, out_specs=(...  24.2 us
    ppermute x11, waiting for transfers between devices, cube_permute(): return lax.ppermute(blocks, 'patch', pairs)  20.5 us
    all_to_all x1, starting transfers between devices, trade(): lax.all_to_all(rows, 'patch', split_axis=0, concat_axis=0, tiled=True)  7.38 us
    ppermute x11, starting transfers between devices, cube_permute(): return lax.ppermute(blocks, 'patch', pairs)  6.53 us
    all_to_all x1, waiting for transfers between devices, trade(): lax.all_to_all(rows, 'patch', split_axis=0, concat_axis=0, tiled=True)  4.83 us
    dot_general x1, matrix products, mm_cols(): lax.dot_general(left, right, (((1,), (1,)), ((), ())), preferred_element_...  3.65 us
  transfers between devices with their start and end apart: 12, of which 10 were waited for; matrix products, arithmetic and copies ran while one was open for 5% of the time, Pallas kernels for 17%

profile of v7, /device:TPU:0, one launch (start us, length us, event | category | flops | bytes accessed | tf_op | source)
XLA Modules:
  0.0 68.4 jit_solution(15648641477146053455)
XLA Ops:
  0.6 1.9 %pick.1 = bf16[128,512]{1,0:T(8,128)(2,1)} custom-call(s32[4,16]{1,0:T(4,128)} %bitcast.9, bf16[256,512]{1,0:T(8,128)(2,1)} %nodes_far.1), custom_call_target="tpu_custom_call" | custom-call | flops 1024 | bytes 1024 | tf_op jit(solution)/shard_map/pick/pallas_call | solution.py:439
  2.5 7.4 %all-to-all-start = ((bf16[16,8,512]{2,1,0:T(8,128)(2,1)}), bf16[16,8,512]{2,1,0:T(8,128)(2,1)S(1)}, u32[]{:S(2)}, u32[]{:S(2)}) async-start(bf16[16,8,512]{2,1,0:T(8,128)(2,1)} %bitcast.11), calls=%async_computation | async-start | bytes 262144 | tf_op jit(solution)/shard_map/all_to_all | solution.py:456
  9.9 2.5 %local.1 = (bf16[256,512]{1,0:T(8,128)(2,1)S(1)}, bf16[512,512]{1,0:T(8,128)(2,1)S(1)}, bf16[512,512]{1,0:T(8,128)(2,1)S(1)}, bf16[1024,512]{1,0:T(8,128)(2,1)S(...) custom-call(bf16[256,512]{1,0:T(8,128)(2,1)} %nodes_far.1, bf16[1536,512]{1,0:T(8,128)(2,1)} %w_edge_in_far.3, ...), custom_call_target="tpu_custom_call" | custom-call | flops 1024 | bytes 1024 | tf_op jit(solution)/shard_map/local/pallas_call | solution.py:439
  12.4 0.0 copy-start
  12.4 0.6 copy-done
  13.0 4.8 %all-to-all-done = bf16[16,8,512]{2,1,0:T(8,128)(2,1)S(1)} async-done(((bf16[16,8,512]{2,1,0:T(8,128)(2,1)}), bf16[16,8,512]{2,1,0:T(8,128)(2,1)S(1)}, u32[]{:S(2)}, u32[]{:S(2)}) %all-to-all-start) | async-done | bytes 131104 | tf_op jit(solution)/shard_map/all_to_all | solution.py:456
  17.8 8.7 %forward.1 = (bf16[768,512]{1,0:T(8,128)(2,1)S(1)}, bf16[768,512]{1,0:T(8,128)(2,1)S(1)}, bf16[2048,512]{1,0:T(8,128)(2,1)S(1)}, bf16[2048,512]{1,0:T(8,128)(2,1...) custom-call(bf16[128,512]{1,0:T(8,128)(2,1)S(1)} %bitcast.7, ...), custom_call_target="tpu_custom_call" | custom-call | flops 1024 | bytes 1024 | tf_op jit(solution)/shard_map/forward/pallas_call | solution.py:439
  26.5 0.1 collective-permute-start
  26.6 1.6 %backward.2 = (bf16[1024,512]{1,0:T(8,128)(2,1)S(1)}, bf16[1024,512]{1,0:T(8,128)(2,1)S(1)}) custom-call(s32[1,2048]{1,0:T(1,128)S(1)} %get-tuple-element.80.recv_ref, bf16[2048,512]{1,0:T(8,128)(2,1)S(1)} %get-tuple-element.82.zeta_ref, bf16[2048,512]{1,0:T(8,128)(2,1)S(1)} %get-tuple-element.84.slope_ref, ...), custom_call_target="tpu_custom_call" | custom-call | flops 1024 | bytes 1024 | tf_op jit(solution)/shard_map/backward/pallas_call | solution.py:439
  28.3 0.6 collective-permute-done.arrived_ref
  28.9 0.1 add.3
  29.0 0.1 collective-permute-start.1
  29.1 1.6 %backward.3 = (bf16[1024,512]{1,0:T(8,128)(2,1)S(1)}, bf16[1024,512]{1,0:T(8,128)(2,1)S(1)}) custom-call(s32[1,2048]{1,0:T(1,128)S(1)} %get-tuple-element.80.recv_ref, bf16[2048,512]{1,0:T(8,128)(2,1)S(1)} %get-tuple-element.82.zeta_ref, bf16[2048,512]{1,0:T(8,128)(2,1)S(1)} %get-tuple-element.84.slope_ref, ...), custom_call_target="tpu_custom_call" | custom-call | flops 1024 | bytes 1024 | tf_op jit(solution)/shard_map/backward/pallas_call | solution.py:439
  30.7 0.0 copy-start.1
  30.7 4.5 %weights.1 = (bf16[1024,512]{1,0:T(8,128)(2,1)S(1)}, bf16[256,512]{1,0:T(8,128)(2,1)S(1)}, bf16[256,512]{1,0:T(8,128)(2,1)S(1)}, bf16[256,512]{1,0:T(8,128)(2,1)...) custom-call(bf16[128,512]{1,0:T(8,128)(2,1)S(1)} %bitcast.8, ...), custom_call_target="tpu_custom_call" | custom-call | flops 1024 | bytes 1024 | tf_op jit(solution)/shard_map/weights/pallas_call | solution.py:439
  35.2 0.2 collective-permute-start.5
  35.4 0.4 collective-permute-start.2
  35.8 0.1 collective-permute-start.3
  36.0 0.4 collective-permute-start.4
  36.3 0.5 collective-permute-done.1.arrived_ref
  36.9 0.4 collective-permute-done.2.refs_0_
  37.3 0.4 collective-permute-done.3.refs_1_
  37.6 0.4 collective-permute-done.4.refs_2_
  38.0 0.0 collective-permute-done.5.refs_3_
  38.0 0.0 copy-done.1
  38.0 0.0 copy-start.2
  38.0 0.2 ride.3
  38.2 2.1 %collective-permute-start.7 = (bf16[544,512]{1,0:T(8,128)(2,1)S(1)}, bf16[544,512]{1,0:T(8,128)(2,1)S(1)}, u32[]{:S(2)}, u32[]{:S(2)}) collective-permute-start(bf16[544,512]{1,0:T(8,128)(2,1)S(1)} %get-tuple-element.116), channel_id=1, source_target_pairs={{0,2},{1,5},{2,0},{3,7},{4,6},{5,1},{6,4},{7,3},{8,10},{9,13},{10,... | collective-permute-start | bytes 1671176 | tf_op jit(solution)/shard_map/ppermute | solution.py:67
  40.3 0.0 collective-permute-start.6
  40.3 7.8 %collective-permute-done.6.arrived_ref = bf16[192,512]{1,0:T(8,128)(2,1)S(1)} collective-permute-done((bf16[192,512]{1,0:T(8,128)(2,1)S(1)}, bf16[192,512]{1,0:T(8,128)(2,1)S(1)}, u32[]{:S(2)}, u32[]{:S(2)}) %collective-permute-start.6) | collective-permute-done | bytes 196640 | tf_op jit(solution)/shard_map/ppermute | solution.py:67
  48.2 1.8 %collective-permute-done.7.refs_0_ = bf16[544,512]{1,0:T(8,128)(2,1)S(1)} collective-permute-done((bf16[544,512]{1,0:T(8,128)(2,1)S(1)}, bf16[544,512]{1,0:T(8,128)(2,1)S(1)}, u32[]{:S(2)}, u32[]{:S(2)}) %collective-permute-start.7) | collective-permute-done | bytes 557088 | tf_op jit(solution)/shard_map/ppermute | solution.py:67
  49.9 0.2 ride.4
  50.1 1.2 %collective-permute-start.8 = (bf16[288,512]{1,0:T(8,128)(2,1)S(1)}, bf16[288,512]{1,0:T(8,128)(2,1)S(1)}, u32[]{:S(2)}, u32[]{:S(2)}) collective-permute-start(bf16[288,512]{1,0:T(8,128)(2,1)S(1)} %get-tuple-element.120), channel_id=1, source_target_pairs={{0,4},{1,3},{2,6},{3,1},{4,0},{5,7},{6,2},{7,5},{8,12},{9,11},{10,... | collective-permute-start | bytes 884744 | tf_op jit(solution)/shard_map/ppermute | solution.py:67
  51.3 0.8 %collective-permute-start.9 = (bf16[96,512]{1,0:T(8,128)(2,1)S(1)}, bf16[96,512]{1,0:T(8,128)(2,1)S(1)}, u32[]{:S(2)}, u32[]{:S(2)}) collective-permute-start(bf16[96,512]{1,0:T(8,128)(2,1)S(1)} %get-tuple-element.122), channel_id=1, source_target_pairs={{0,8},{1,9},{2,10},{3,11},{4,12},{5,13},{6,14},{7,15},{8,0},{9,1},... | collective-permute-start | bytes 294920 | tf_op jit(solution)/shard_map/ppermute | solution.py:67
  52.1 6.9 %collective-permute-done.8.refs_0_ = bf16[288,512]{1,0:T(8,128)(2,1)S(1)} collective-permute-done((bf16[288,512]{1,0:T(8,128)(2,1)S(1)}, bf16[288,512]{1,0:T(8,128)(2,1)S(1)}, u32[]{:S(2)}, u32[]{:S(2)}) %collective-permute-start.8) | collective-permute-done | bytes 294944 | tf_op jit(solution)/shard_map/ppermute | solution.py:67
  59.0 0.2 ride.5
  59.1 0.0 collective-permute-done.9.came_ref
  59.1 1.2 %collective-permute-start.10 = (bf16[160,512]{1,0:T(8,128)(2,1)S(1)}, bf16[160,512]{1,0:T(8,128)(2,1)S(1)}, u32[]{:S(2)}, u32[]{:S(2)}) collective-permute-start(bf16[160,512]{1,0:T(8,128)(2,1)S(1)} %get-tuple-element.124), channel_id=1, source_target_pairs={{0,8},{1,9},{2,10},{3,11},{4,12},{5,13},{6,14},{7,15},{8,0},{9,1},... | collective-permute-start | bytes 491528 | tf_op jit(solution)/shard_map/ppermute | solution.py:67
  60.4 0.7 %node_total.1 = (f32[32,512]{1,0:T(8,128)}, f32[64,512]{1,0:T(8,128)}) custom-call(bf16[96,512]{1,0:T(8,128)(2,1)S(1)} %get-tuple-element.138.kept_ref, bf16[96,512]{1,0:T(8,128)(2,1)S(1)} %collective-permute-done.9.came_ref), custom_call_target="tpu_custom_call" | custom-call | flops 1024 | bytes 1024 | tf_op jit(solution)/shard_map/node_total/pallas_call | solution.py:439
  61.0 0.0 copy-done.2
  61.1 0.8 %node.1 = (f32[256,512]{1,0:T(8,128)S(1)}, bf16[32,256]{1,0:T(8,128)(2,1)S(1)}) custom-call(bf16[256,512]{1,0:T(8,128)(2,1)S(1)} %get-tuple-element.126.own_ref, bf16[256,512]{1,0:T(8,128)(2,1)S(1)} %get-tuple-element.127.recv_ref, f32[256,512]{1,0:T(8,128)S(1)} %get-tuple-element.128.part_ref, bf16[512,512]{1,0:T(8,128)(2,1)S(1)} %get-tuple-element.75.w_send.w_send_ref, ...), custom_call_target="tpu_custom_call" | custom-call | flops 1024 | bytes 1024 | tf_op jit(solution)/shard_map/node/pallas_call | solution.py:439
  61.8 3.6 %convolution_convert_fusion = bf16[2048,512]{1,0:T(8,128)(2,1)} fusion(bf16[1024,512]{1,0:T(8,128)(2,1)S(1)} %get-tuple-element.135.da2_ref, bf16[1024,512]{1,0:T(8,128)(2,1)S(1)} %get-tuple-element.134.da1_ref, bf16[1536,512]{1,0:T(8,128)(2,1)} %w_edge_in_far.3), kind=kOutput, calls=%fused_computation | convolution fusion | flops 1078984704 | bytes 4718592 | tf_op jit(solution)/shard_map/dot_general | solution.py:27
  65.5 1.7 %collective-permute-done.10.arrived_ref = bf16[160,512]{1,0:T(8,128)(2,1)S(1)} collective-permute-done((bf16[160,512]{1,0:T(8,128)(2,1)S(1)}, bf16[160,512]{1,0:T(8,128)(2,1)S(1)}, u32[]{:S(2)}, u32[]{:S(2)}) %collective-permute-start.10) | collective-permute-done | bytes 163872 | tf_op jit(solution)/shard_map/ppermute | solution.py:67
  67.2 1.2 %last.1 = (f32[32,512]{1,0:T(8,128)}, f32[96,512]{1,0:T(8,128)}, bf16[256,512]{1,0:T(8,128)(2,1)}) custom-call(bf16[128,512]{1,0:T(8,128)(2,1)S(1)} %get-tuple-element.121.keep_ref, bf16[160,512]{1,0:T(8,128)(2,1)S(1)} %collective-permute-done.10.arrived_ref, bf16[32,256]{1,0:T(8,128)(2,1)S(1)} %get-tuple-element.131.late_pick_ref, ...), custom_call_target="tpu_custom_call" | custom-call | flops 1024 | bytes 1024 | tf_op jit(solution)/shard_map/last/pallas_call | solution.py:439
  (2 shorter events, 0.1 us)
Async XLA Ops:
  2.5 15.3 %all-to-all-start = ((bf16[16,8,512]{2,1,0:T(8,128)(2,1)}), bf16[16,8,512]{2,1,0:T(8,128)(2,1)S(1)}, u32[]{:S(2)}, u32[]{:S(2)}) async-start(bf16[16,8,512]{2,1,0:T(8,128)(2,1)} %bitcast.11), calls=%async_computation | async-start | bytes 262144 | tf_op jit(solution)/shard_map/all_to_all | solution.py:456
  12.4 0.6 copy-start
  26.5 2.4 %collective-permute-start = (bf16[768,512]{1,0:T(8,128)(2,1)S(1)}, bf16[768,512]{1,0:T(8,128)(2,1)S(1)}, u32[]{:S(2)}, u32[]{:S(2)}) collective-permute-start(bf16[768,512]{1,0:T(8,128)(2,1)S(1)} %get-tuple-element.83), channel_id=1, source_target_pairs={{0,1},{1,0},{2,3},{3,2},{4,5},{5,4},{6,7},{7,6},{8,9},{9,8},{10,11... | collective-permute-start | bytes 2359304 | tf_op jit(solution)/shard_map/ppermute | solution.py:67
  29.0 7.8 %collective-permute-start.1 = (bf16[384,512]{1,0:T(8,128)(2,1)S(1)}, bf16[384,512]{1,0:T(8,128)(2,1)S(1)}, u32[]{:S(2)}, u32[]{:S(2)}) collective-permute-start(bf16[384,512]{1,0:T(8,128)(2,1)S(1)} %get-tuple-element.100), channel_id=1, source_target_pairs={{0,2},{1,5},{2,0},{3,7},{4,6},{5,1},{6,4},{7,3},{8,10},{9,13},{10,... | collective-permute-start | bytes 1179656 | tf_op jit(solution)/shard_map/ppermute | solution.py:67
  30.7 7.3 %copy-start.1 = (bf16[3,96,96]{2,1,0:T(8,128)(2,1)S(1)}, bf16[3,96,96]{2,1,0:T(8,128)(2,1)}, u32[]{:S(2)}) copy-start(bf16[3,96,96]{2,1,0:T(8,128)(2,1)} %copy-done) | copy-start | bytes 165892
  35.2 2.8 %collective-permute-start.5 = (bf16[288,512]{1,0:T(8,128)(2,1)S(1)}, bf16[288,512]{1,0:T(8,128)(2,1)S(1)}, u32[]{:S(2)}, u32[]{:S(2)}) collective-permute-start(bf16[288,512]{1,0:T(8,128)(2,1)S(1)} %get-tuple-element.105), channel_id=1, source_target_pairs={{0,1},{1,0},{2,3},{3,2},{4,5},{5,4},{6,7},{7,6},{8,9},{9,8},{10,11... | collective-permute-start | bytes 884744 | tf_op jit(solution)/shard_map/ppermute | solution.py:67
  35.4 1.8 %collective-permute-start.2 = (bf16[256,512]{1,0:T(8,128)(2,1)S(1)}, bf16[256,512]{1,0:T(8,128)(2,1)S(1)}, u32[]{:S(2)}, u32[]{:S(2)}) collective-permute-start(bf16[256,512]{1,0:T(8,128)(2,1)S(1)} %get-tuple-element.102), channel_id=1, source_target_pairs={{0,1},{1,0},{2,3},{3,2},{4,5},{5,4},{6,7},{7,6},{8,9},{9,8},{10,11... | collective-permute-start | bytes 786440 | tf_op jit(solution)/shard_map/ppermute | solution.py:67
  35.8 1.8 %collective-permute-start.3 = (bf16[256,512]{1,0:T(8,128)(2,1)S(1)}, bf16[256,512]{1,0:T(8,128)(2,1)S(1)}, u32[]{:S(2)}, u32[]{:S(2)}) collective-permute-start(bf16[256,512]{1,0:T(8,128)(2,1)S(1)} %get-tuple-element.103), channel_id=1, source_target_pairs={{0,1},{1,0},{2,3},{3,2},{4,5},{5,4},{6,7},{7,6},{8,9},{9,8},{10,11... | collective-permute-start | bytes 786440 | tf_op jit(solution)/shard_map/ppermute | solution.py:67
  36.0 2.1 %collective-permute-start.4 = (bf16[256,512]{1,0:T(8,128)(2,1)S(1)}, bf16[256,512]{1,0:T(8,128)(2,1)S(1)}, u32[]{:S(2)}, u32[]{:S(2)}) collective-permute-start(bf16[256,512]{1,0:T(8,128)(2,1)S(1)} %get-tuple-element.104), channel_id=1, source_target_pairs={{0,1},{1,0},{2,3},{3,2},{4,5},{5,4},{6,7},{7,6},{8,9},{9,8},{10,11... | collective-permute-start | bytes 786440 | tf_op jit(solution)/shard_map/ppermute | solution.py:67
  38.0 23.0 %copy-start.2 = (s32[1,16,4]{1,2,0:T(4,128)S(1)}, s32[1,16,4]{1,2,0:T(4,128)}, u32[]{:S(2)}) copy-start(s32[1,16,4]{1,2,0:T(4,128)} %param.17) | copy-start | bytes 772
  38.2 11.7 %collective-permute-start.7 = (bf16[544,512]{1,0:T(8,128)(2,1)S(1)}, bf16[544,512]{1,0:T(8,128)(2,1)S(1)}, u32[]{:S(2)}, u32[]{:S(2)}) collective-permute-start(bf16[544,512]{1,0:T(8,128)(2,1)S(1)} %get-tuple-element.116), channel_id=1, source_target_pairs={{0,2},{1,5},{2,0},{3,7},{4,6},{5,1},{6,4},{7,3},{8,10},{9,13},{10,... | collective-permute-start | bytes 1671176 | tf_op jit(solution)/shard_map/ppermute | solution.py:67
  40.3 7.8 %collective-permute-start.6 = (bf16[192,512]{1,0:T(8,128)(2,1)S(1)}, bf16[192,512]{1,0:T(8,128)(2,1)S(1)}, u32[]{:S(2)}, u32[]{:S(2)}) collective-permute-start(bf16[192,512]{1,0:T(8,128)(2,1)S(1)} %get-tuple-element.114), channel_id=1, source_target_pairs={{0,4},{1,3},{2,6},{3,1},{4,0},{5,7},{6,2},{7,5},{8,12},{9,11},{10,... | collective-permute-start | bytes 589832 | tf_op jit(solution)/shard_map/ppermute | solution.py:67
  50.1 8.9 %collective-permute-start.8 = (bf16[288,512]{1,0:T(8,128)(2,1)S(1)}, bf16[288,512]{1,0:T(8,128)(2,1)S(1)}, u32[]{:S(2)}, u32[]{:S(2)}) collective-permute-start(bf16[288,512]{1,0:T(8,128)(2,1)S(1)} %get-tuple-element.120), channel_id=1, source_target_pairs={{0,4},{1,3},{2,6},{3,1},{4,0},{5,7},{6,2},{7,5},{8,12},{9,11},{10,... | collective-permute-start | bytes 884744 | tf_op jit(solution)/shard_map/ppermute | solution.py:67
  51.3 7.8 %collective-permute-start.9 = (bf16[96,512]{1,0:T(8,128)(2,1)S(1)}, bf16[96,512]{1,0:T(8,128)(2,1)S(1)}, u32[]{:S(2)}, u32[]{:S(2)}) collective-permute-start(bf16[96,512]{1,0:T(8,128)(2,1)S(1)} %get-tuple-element.122), channel_id=1, source_target_pairs={{0,8},{1,9},{2,10},{3,11},{4,12},{5,13},{6,14},{7,15},{8,0},{9,1},... | collective-permute-start | bytes 294920 | tf_op jit(solution)/shard_map/ppermute | solution.py:67
  59.1 8.1 %collective-permute-start.10 = (bf16[160,512]{1,0:T(8,128)(2,1)S(1)}, bf16[160,512]{1,0:T(8,128)(2,1)S(1)}, u32[]{:S(2)}, u32[]{:S(2)}) collective-permute-start(bf16[160,512]{1,0:T(8,128)(2,1)S(1)} %get-tuple-element.124), channel_id=1, source_target_pairs={{0,8},{1,9},{2,10},{3,11},{4,12},{5,13},{6,14},{7,15},{8,0},{9,1},... | collective-permute-start | bytes 491528 | tf_op jit(solution)/shard_map/ppermute | solution.py:67
